TPU v7x, 128 devices: a whole 4x4x4 slice. The times are simulated.
128 devices in a mesh: elem: 16 (over x, y), lev: 8 (over z, core).
Axes of the slice: x: 4, y: 4, z: 4, core: 2. Of those that a mesh axis runs over, the one named last changes fastest.
Arguments:
- right_side: float32 [128, 16, 16384], P('lev', None, 'elem'), may hold values from -150 to 150, as said below
- metric: float32 [3, 16, 16384], P(None, None, 'elem'), may hold values from -0.3 to 0.5, as said below
- mass_weight: float32 [16, 16384], P(None, 'elem'), may hold values from 0.5 to 2
- helmholtz: float32 [128], P('lev'), may hold values from 0.5 to 2
- vertical: float32 [128, 16384], P('lev', 'elem'), may hold values from 0.5 to 2
- block_inverse: float32 [16, 8, 8, 16384], P('lev', None, None, 'elem'), may hold values from 0 to 1.1, as said below
- edge_neighbour: int32 [16384, 4], P('elem'), may hold values from -1 to 65535, as said below
- edge_flip: int32 [16384, 4], P('elem'), may hold values from 0 to 1, as said below
- corner_neighbour: int32 [16384, 4, 3], P('elem'), may hold values from -1 to 65535, as said below
- element_count: int32 [16], P('elem'), may hold values from 512 to 1024, as said below
Outputs:
- solution: float32 [128, 16, 16384], P('lev', None, 'elem')
- residual: float32 [128, 16, 16384], P('lev', None, 'elem')
- direction: float32 [128, 16, 16384], P('lev', None, 'elem')
Inputs may be any that keep to these rules, and one draw needn't show every extreme that they name: `right_side`: grows along the element slots and the levels; not promised to be smooth. At every node metric[0] > 0, metric[2] > 0 and metric[1] squared is below metric[0] metric[2]. Each block_inverse[k, :, :, g] is symmetric positive definite. edge_neighbour[g, j] = 4 h + i where side i of element slot h (device index along elem times 1024 plus slot) meets side j of slot g, or -1 on the patch border and on empty slots; the relation is mutual. Slots that meet by a side or a corner lie on the same device of elem or on one next to it: on the device before among its last 129 live slots, on the device after among its first 129. `edge_flip`: 1 where the two sides that meet run in opposite node orders, 0 elsewhere and on empty slots. corner_neighbour[g, k] lists the corners 4 h + c of the other element slots that share corner k of slot g, padded with -1; the relation is mutual. The live slots of device d are its first element_count[d]; the counts add up to 12288, and some device is full.
All inputs are finite; a program needn't handle non-finite values.
Results may differ from a plain program's by a relative error of at most 0.008.
Values sent between devices are 32-bit elements; how exact they have to be, the bound alone decides.
No kernel may reach another device: no remote copies, remote signals or barrier semaphores. Data moves between devices by JAX's collectives and lax.ppermute only.
A program may use at most 128 MiB of HBM per device.

v0:
```python
import math

import jax
import jax.numpy as jnp
import numpy as np
from jax import lax
from jax.sharding import PartitionSpec as P

BLOCK = 8
COLUMNS = 128
ITERATIONS = 3


PENALTY = 2.0
PICKS = [1, 2, 7, 11, 13, 14, 4, 8, 0, 3, 15, 12]
EDGE_NODES = [1, 2, 7, 11, 13, 14, 4, 8]
CORNER_NODES = [0, 3, 15, 12]


def passed_along(value, axis, steps):
    count = lax.axis_size(axis)
    initial, last = (max(0, -steps), min(count, count - steps))
    return lax.ppermute(value, axis, [(source, source + steps) for source in range(initial, last)])


def with_halo(shard, sides, width):
    for axis, dim in sides:
        peers, length = (lax.axis_size(axis), shard.shape[dim])
        up = [(i, (i + 1) % peers) for i in range(peers - 1)]
        down = [(j, i) for i, j in up]
        last = lax.slice_in_dim(shard, length - width, length, axis=dim)
        initial = lax.slice_in_dim(shard, 0, width, axis=dim)
        before = lax.ppermute(last, axis, up)
        after = lax.ppermute(initial, axis, down)
        shard = jnp.concatenate([before, shard, after], axis=dim)
    return shard


def gradient_table():
    root = 1.0 / math.sqrt(5.0)
    points = [-1.0, -root, root, 1.0]
    legendre = [0.5 * (5.0 * p * p * p - 3.0 * p) for p in points]
    matrix = [[0.0 for col in range(4)] for row in range(4)]
    for row in range(4):
        for col in range(4):
            if row != col:
                matrix[row][col] = legendre[row] / (legendre[col] * (points[row] - points[col]))
    matrix[0][0] = -3.0
    matrix[3][3] = 3.0
    derivative = np.array(matrix)
    return np.concatenate([np.kron(np.eye(4), derivative), np.kron(derivative, np.eye(4))], axis=0)


def select_table():
    table = np.zeros((12, 16))
    for entry in range(12):
        table[entry, PICKS[entry]] = 1.0
    return table


def edge_place():
    table = np.zeros((16, 8))
    for entry in range(8):
        table[EDGE_NODES[entry], entry] = 1.0
    return table


def corner_place():
    table = np.zeros((16, 4))
    for entry in range(4):
        table[CORNER_NODES[entry], entry] = 1.0
    return table


def stiffness(field, metric):
    table = jnp.asarray(gradient_table(), dtype=field.dtype)
    gradients = jnp.einsum("kn,lne->lke", table, field, precision=lax.Precision.HIGHEST)
    along_x = gradients[:, :16]
    along_y = gradients[:, 16:]
    flux_x = metric[0] * along_x + metric[1] * along_y
    flux_y = metric[1] * along_x + metric[2] * along_y
    return jnp.einsum(
        "kn,lke->lne",
        table,
        jnp.concatenate([flux_x, flux_y], axis=1),
        precision=lax.Precision.HIGHEST,
    )


def boundary_values(field):
    table = jnp.asarray(select_table(), dtype=field.dtype)
    return jnp.einsum("kn,lne->lke", table, field, precision=lax.Precision.HIGHEST)


def edge_sources(edge_neighbour, edge_flip, locate, columns_total):
    present = edge_neighbour >= 0
    target = jnp.where(present, edge_neighbour, 0)
    element = target // 4
    side_there = target % 4
    column = jnp.where(present, locate(element), 0)
    indices = []
    presence = []
    for side_here in range(4):
        for node_here in range(2):
            node_there = jnp.where(edge_flip[:, side_here] == 1, 1 - node_here, node_here)
            indices.append(
                (2 * side_there[:, side_here] + node_there) * columns_total + column[:, side_here]
            )
            presence.append(present[:, side_here])
    return (jnp.stack(indices), jnp.stack(presence).astype(jnp.float32))


def corner_sources(corner_neighbour, locate, columns_total):
    present = corner_neighbour >= 0
    target = jnp.where(present, corner_neighbour, 0)
    element = target // 4
    corner = target % 4
    column = jnp.where(present, locate(element), 0)
    position = (8 + corner) * columns_total + column
    slot_count = position.shape[0]
    flat_position = jnp.transpose(position, (1, 2, 0)).reshape(12, slot_count)
    flat_present = jnp.transpose(present, (1, 2, 0)).reshape(12, slot_count)
    return (flat_position, flat_present.astype(jnp.float32))


def penalty_term(border_values, pooled, position, weight):
    level_count, unused, slot_count = border_values.shape
    flattened = pooled.reshape(level_count, -1)
    picked = jnp.take(flattened, position.reshape(-1), axis=1).reshape(level_count, 20, slot_count)
    edge_jump = weight[:8][None] * (border_values[:, :8] - picked[:, :8])
    corner_gap = weight[8:][None] * (jnp.repeat(border_values[:, 8:], 3, axis=1) - picked[:, 8:])
    corner_jump = jnp.sum(corner_gap.reshape(level_count, 4, 3, slot_count), axis=2)
    edge_table = jnp.asarray(edge_place(), dtype=border_values.dtype)
    corner_table = jnp.asarray(corner_place(), dtype=border_values.dtype)
    placed_edges = jnp.einsum("nk,lke->lne", edge_table, edge_jump, precision=lax.Precision.HIGHEST)
    placed_corners = jnp.einsum(
        "nk,lke->lne", corner_table, corner_jump, precision=lax.Precision.HIGHEST
    )
    return placed_edges + placed_corners


def column_solve(field, inverse, coupling):
    blocks = field.reshape(inverse.shape[0], inverse.shape[1], field.shape[1], field.shape[2])

    def forward(carried, pieces):
        level_block, matrix, linking = pieces
        lifted = jnp.concatenate([level_block[:1] + carried[None], level_block[1:]], axis=0)
        solved = jnp.einsum("ije,jke->ike", matrix, lifted, precision=lax.Precision.HIGHEST)
        return (linking[None, :] * solved[-1], solved)

    initial = jnp.zeros(field.shape[1:], field.dtype)
    unused, solved = lax.scan(forward, initial, (blocks, inverse, coupling))

    def backward(carried, pieces):
        level_block, matrix, linking = pieces
        corrected = level_block + (linking[None, :] * carried)[None] * matrix[:, -1][:, None, :]
        return (corrected[0], corrected)

    unused, result = lax.scan(backward, initial, (solved, inverse, coupling), reverse=True)
    return result.reshape(field.shape)


def residual_norm(residual, smoothed):
    return lax.psum(jnp.sum(residual * smoothed), ("elem", "lev"))


def body(
    right_side,
    metric,
    mass_weight,
    helmholtz,
    vertical,
    block_inverse,
    edge_neighbour,
    edge_flip,
    corner_neighbour,
    element_count,
):
    level_count, node_count, slot_count = right_side.shape
    border = COLUMNS + 1
    pool_width = slot_count + 2 * border
    living = jnp.arange(slot_count, dtype=jnp.int32) < element_count[0]
    source = jnp.where(living[None, None, :], right_side, jnp.zeros_like(right_side))
    below_coupling = passed_along(vertical[-1:], "lev", 1)
    position = lax.axis_index("elem")
    linking = vertical[BLOCK - 1 :: BLOCK][:, None, None, :]
    inverse_columns, link_columns = (
        lax.all_to_all(block_inverse, "lev", split_axis=3, concat_axis=0, tiled=True),
        lax.all_to_all(linking, "lev", split_axis=3, concat_axis=0, tiled=True),
    )
    link_rows = link_columns[:, 0, 0, :]

    def column_part(pieces):
        return column_solve(pieces, inverse_columns, link_rows)

    def precondition(residual):
        columns = column_part(
            lax.all_to_all(residual, "lev", split_axis=2, concat_axis=0, tiled=True)
        )
        return lax.all_to_all(columns, "lev", split_axis=0, concat_axis=2, tiled=True)

    solution = jnp.zeros_like(source)
    residual = source
    smoothed = precondition(residual)
    direction = smoothed
    norm_now = residual_norm(residual, smoothed)
    for iteration in range(ITERATIONS):
        border_values = boundary_values(direction)
        tail_rows = lax.dynamic_slice_in_dim(border_values, element_count[0] - border, border, 2)
        tail_in, count_in = passed_along((tail_rows, element_count.astype(jnp.float32)), "elem", 1)
        head_in = passed_along(border_values[:, :, :border], "elem", -1)
        pooled = jnp.concatenate([tail_in, border_values, head_in], axis=2)
        count_before = count_in[0].astype(jnp.int32)

        def locate(element):
            holder = element // slot_count
            within = element % slot_count
            earlier_column = within - (count_before - border)
            later_column = border + slot_count + within
            return jnp.where(
                holder == position,
                border + within,
                jnp.where(holder < position, earlier_column, later_column),
            )

        edge_index, edge_weight = edge_sources(edge_neighbour, edge_flip, locate, pool_width)
        corner_index, corner_weight = corner_sources(corner_neighbour, locate, pool_width)
        all_index = jnp.concatenate([edge_index, corner_index], axis=0)
        all_weight = jnp.concatenate([edge_weight, corner_weight], axis=0)
        jump_term = penalty_term(border_values, pooled, all_index, all_weight)
        padded = with_halo(direction, (("lev", 0),), 1)
        level_flux = vertical[:, None, :] * (direction - padded[2:])
        first_flux = below_coupling[:, None, :] * (padded[:1] - direction[:1])
        below_flux = jnp.concatenate([first_flux, level_flux[:-1]], axis=0)
        diagonal = helmholtz[:, None, None] * mass_weight[None] * direction
        applied = (
            diagonal + stiffness(direction, metric) + PENALTY * jump_term + level_flux - below_flux
        )
        curvature = lax.psum(jnp.sum(direction * applied), ("elem", "lev"))
        step_size = norm_now / curvature
        solution = solution + step_size * direction
        residual = residual - step_size * applied
        smoothed = precondition(residual)
        norm_next = residual_norm(residual, smoothed)
        direction = smoothed + norm_next / norm_now * direction
        norm_now = norm_next
    return (solution, residual, direction)


def solution(mesh):
    in_specs = (
        P("lev", None, "elem"),
        P(None, None, "elem"),
        P(None, "elem"),
        P("lev"),
        P("lev", "elem"),
        P("lev", None, None, "elem"),
        P("elem", None),
        P("elem", None),
        P("elem", None, None),
        P("elem"),
    )
    out_specs = (P("lev", None, "elem"), P("lev", None, "elem"), P("lev", None, "elem"))
    return jax.shard_map(body, mesh=mesh, in_specs=in_specs, out_specs=out_specs, check_vma=False)
```

profile of v0, /device:TPU:1, one launch (start us, length us, event | category | flops | bytes accessed | tf_op | source)
XLA Modules:
  0.0 1994.6 jit_solution(9099762603844453529)
XLA Ops:
  107.7 126.3 %while.120 = (s32[]{:T(128)}, f32[16,128]{0,1:T(8,128)S(1)}, f32[16,8,16,128]{3,2,1,0:T(8,128)S(1)}, f32[16,128]{1,0:T(8,128)S(1)}, f32[16,8,16,128]{2,3,1,0:T(8...) while((s32[]{:T(128)}, f32[16,128]{0,1:T(8,128)S(1)}, ...), condition=%wide.region_1.2_spmd.clone, body=%wide.region_0.1_spmd.clone.sunk | while | flops 1595396 | bytes 3467399 | solution.py:152
  251.8 15.0 all-to-all-done.3
  297.9 71.2 %gather_fusion = f32[20480,16]{1,0:T(8,128)} fusion(f32[16,15384]{0,1:T(8,128)} %copy.255, s32[20480]{0:T(1024)S(1)} %fusion.126), kind=kCustom, calls=%fused_computation.clone | custom fusion | bytes 2703360 | tf_op jit(solution)/shard_map/jit(_take)/gather | solution.py:129
  369.1 11.9 broadcast_select_fusion.2
  406.9 66.3 %all-reduce = (f32[]{:T(128)}, f32[]{:T(128)}) all-reduce(f32[]{:T(128)} %get-tuple-element.929, f32[]{:T(128)} %get-tuple-element.928), channel_id=1, replica_groups=mesh['elem'=16,'lev'=8] {'elem','lev'}, use_global_device_ids=true, to_apply=%region_5.6 | all-reduce | flops 2 | bytes 16 | tf_op jit(solution)/shard_map/psum | solution.py:164
  495.5 15.1 all-to-all-done.4
  532.3 147.0 %while.121 = (s32[]{:T(128)}, f32[16,128]{0,1:T(8,128)S(1)}, f32[16,8,16,128]{3,2,1,0:T(8,128)}, f32[16,128]{1,0:T(8,128)}, f32[16,8,16,128]{2,3,1,0:T(8,128)}, ...) while((s32[]{:T(128)}, f32[16,128]{0,1:T(8,128)S(1)}, ...), condition=%wide.region_10.12_spmd.clone, body=%wide.region_9.11_spmd.clone.sunk | while | flops 1595396 | bytes 3467907 | solution.py:152
  679.4 37.7 %while.117 = (s32[]{:T(128)}, f32[16,128]{1,0:T(8,128)S(1)}, f32[16,8,16,128]{3,2,1,0:T(8,128)S(1)}, f32[16,8,16,128]{3,2,1,0:T(8,128)}, f32[16,128]{1,0:T(8,128...) while((s32[]{:T(128)}, f32[16,128]{1,0:T(8,128)S(1)}, f32[16,8,16,128]{3,2,1,0:T(8,128)S(1)}, ...), condition=%wide.region_12.14_spmd, body=%wide.region_11.13_spmd.sunk | while | flops 38915 | bytes 326765 | solution.py:159
  717.1 18.3 all_to_all.165
  738.5 63.8 %psum.51 = f32[]{:T(128)} all-reduce(f32[]{:T(128)} %fusion.101), channel_id=1, replica_groups=mesh['elem'=16,'lev'=8] {'elem','lev'}, use_global_device_ids=true, to_apply=%region_14.16 | all-reduce | flops 1 | bytes 8 | tf_op jit(solution)/shard_map/psum | solution.py:164
  831.4 71.2 %gather_fusion.1 = f32[20480,16]{1,0:T(8,128)} fusion(f32[16,15384]{0,1:T(8,128)} %copy.271, s32[20480]{0:T(1024)S(1)} %fusion.126), kind=kCustom, calls=%fused_computation.1.clone | custom fusion | bytes 2703360 | tf_op jit(solution)/shard_map/jit(_take)/gather | solution.py:129
  941.6 68.2 %psum.52 = f32[]{:T(128)} all-reduce(f32[]{:T(128)} %get-tuple-element.1068), channel_id=1, replica_groups=mesh['elem'=16,'lev'=8] {'elem','lev'}, use_global_device_ids=true, to_apply=%region_17.19 | all-reduce | flops 1 | bytes 8 | tf_op jit(solution)/shard_map/psum | solution.py:239
  1034.1 15.1 all-to-all-done.6
  1075.2 184.8 %while.122 = (s32[]{:T(128)}, f32[16,128]{0,1:T(8,128)S(1)}, f32[16,8,16,128]{3,2,1,0:T(8,128)}, f32[16,128]{1,0:T(8,128)}, f32[16,8,16,128]{2,3,1,0:T(8,128)}, ...) while((s32[]{:T(128)}, f32[16,128]{0,1:T(8,128)S(1)}, ...), condition=%wide.region_19.21_spmd.clone, body=%wide.region_18.20_spmd.clone.sunk | while | flops 1595396 | bytes 3467907 | solution.py:152
  1261.1 47.2 %while.118 = (s32[]{:T(128)}, f32[16,128]{1,0:T(8,128)S(1)}, f32[16,8,16,128]{3,2,1,0:T(8,128)}, f32[16,8,16,128]{3,2,1,0:T(8,128)}, f32[16,128]{1,0:T(8,128)}, ...) while((s32[]{:T(128)}, f32[16,128]{1,0:T(8,128)S(1)}, f32[16,8,16,128]{3,2,1,0:T(8,128)}, ...), condition=%wide.region_21.23_spmd, body=%wide.region_20.22_spmd.sunk | while | flops 38915 | bytes 326765 | solution.py:159
  1308.3 19.4 all_to_all.166
  1330.7 64.7 %psum.53 = f32[]{:T(128)} all-reduce(f32[]{:T(128)} %fusion.100), channel_id=1, replica_groups=mesh['elem'=16,'lev'=8] {'elem','lev'}, use_global_device_ids=true, to_apply=%region_23.25 | all-reduce | flops 1 | bytes 8 | tf_op jit(solution)/shard_map/psum | solution.py:164
  1424.3 71.2 %gather_fusion.2 = f32[20480,16]{1,0:T(8,128)} fusion(f32[16,15384]{0,1:T(8,128)} %copy.284, s32[20480]{0:T(1024)S(1)} %fusion.126), kind=kCustom, calls=%fused_computation.2.clone | custom fusion | bytes 2703360 | tf_op jit(solution)/shard_map/jit(_take)/gather | solution.py:129
  1536.0 68.2 %psum.54 = f32[]{:T(128)} all-reduce(f32[]{:T(128)} %get-tuple-element.1070), channel_id=1, replica_groups=mesh['elem'=16,'lev'=8] {'elem','lev'}, use_global_device_ids=true, to_apply=%region_26.28 | all-reduce | flops 1 | bytes 8 | tf_op jit(solution)/shard_map/psum | solution.py:239
  1628.4 15.1 all-to-all-done.8
  1669.6 184.6 %while.123 = (s32[]{:T(128)}, f32[16,128]{0,1:T(8,128)S(1)}, f32[16,8,16,128]{3,2,1,0:T(8,128)}, f32[16,128]{1,0:T(8,128)}, f32[16,8,16,128]{2,3,1,0:T(8,128)}, ...) while((s32[]{:T(128)}, f32[16,128]{0,1:T(8,128)S(1)}, ...), condition=%wide.region_28.30_spmd.clone, body=%wide.region_27.29_spmd.clone.sunk | while | flops 1595396 | bytes 3467907 | solution.py:152
  1855.3 47.2 %while.119 = (s32[]{:T(128)}, f32[16,128]{1,0:T(8,128)S(1)}, f32[16,8,16,128]{3,2,1,0:T(8,128)}, f32[16,8,16,128]{3,2,1,0:T(8,128)}, f32[16,128]{1,0:T(8,128)}, ...) while((s32[]{:T(128)}, f32[16,128]{1,0:T(8,128)S(1)}, f32[16,8,16,128]{3,2,1,0:T(8,128)}, ...), condition=%wide.region_30.32_spmd, body=%wide.region_29.31_spmd.sunk | while | flops 38915 | bytes 326765 | solution.py:159
  1902.5 19.4 all_to_all.167
  1925.0 64.7 %psum.55 = f32[]{:T(128)} all-reduce(f32[]{:T(128)} %fusion.99), channel_id=1, replica_groups=mesh['elem'=16,'lev'=8] {'elem','lev'}, use_global_device_ids=true, to_apply=%region_32.34 | all-reduce | flops 1 | bytes 8 | tf_op jit(solution)/shard_map/psum | solution.py:164
  (1509 shorter events, 1251.0 us)
Async XLA Ops:
  5.2 32.2 %all-to-all-start = ((f32[8,1,256]{2,1,0:T(1,128)}), f32[8,1,256]{2,1,0:T(1,128)S(1)}, u32[]{:S(2)}, u32[]{:S(2)}) async-start(f32[8,1,256]{2,1,0:T(1,128)} %reshape.604), calls=%async_computation | async-start | bytes 16384 | tf_op jit(solution)/shard_map/all_to_all | solution.py:189
  12.7 49.8 %collective-permute-start.2 = (f32[1]{0:T(128)}, f32[1]{0:T(128)}, u32[]{:S(2)}, u32[]{:S(2)}) collective-permute-start(f32[1]{0:T(128)} %convert_element_type.36), channel_id=1, source_target_pairs={{0,8},{8,16},{16,24},{24,32},{32,40},{40,48},{48,56},{56,64},{64,7... | collective-permute-start | bytes 20 | tf_op jit(solution)/shard_map/ppermute | solution.py:23
  17.4 266.2 %collective-permute-start.4 = (f32[1,1024]{1,0:T(1,128)S(1)}, f32[1,1024]{1,0:T(1,128)S(1)}, u32[]{:S(2)}, u32[]{:S(2)}) collective-permute-start(f32[1,1024]{1,0:T(1,128)S(1)} %slice.422), channel_id=1, source_target_pairs={{0,1},{1,2},{2,3},{3,4},{4,5},{5,6},{6,7},{8,9},{9,10},{10,11},{11... | collective-permute-start | bytes 12296 | tf_op jit(solution)/shard_map/ppermute | solution.py:23
  37.5 18.5 all-to-all-start.2
  55.9 220.4 %copy-start.11 = (f32[16,1024]{1,0:T(8,128)}, f32[16,1024]{1,0:T(8,128)S(1)}, u32[]{:S(2)}) copy-start(f32[16,1024]{1,0:T(8,128)S(1)} %get-tuple-element.1050) | copy-start | bytes 196612
  56.0 220.4 %copy-start.14 = (f32[16,1024]{1,0:T(8,128)}, f32[16,1024]{1,0:T(8,128)S(1)}, u32[]{:S(2)}) copy-start(f32[16,1024]{1,0:T(8,128)S(1)} %get-tuple-element.1051) | copy-start | bytes 196612
  56.0 220.4 %copy-start.17 = (f32[16,1024]{1,0:T(8,128)}, f32[16,1024]{1,0:T(8,128)S(1)}, u32[]{:S(2)}) copy-start(f32[16,1024]{1,0:T(8,128)S(1)} %get-tuple-element.1052) | copy-start | bytes 196612
  56.0 32.2 %all-to-all-start.1 = ((f32[8,1,32768]{2,1,0:T(1,128)}), f32[8,1,32768]{2,1,0:T(1,128)S(1)}, u32[]{:S(2)}, u32[]{:S(2)}) async-start(f32[8,1,32768]{2,1,0:T(1,128)} %reshape.606), calls=%async_computation.1 | async-start | bytes 2097152 | tf_op jit(solution)/shard_map/all_to_all | solution.py:198
  246.9 19.9 all-to-all-start.3
  268.0 18.4 collective-permute-start
  271.3 12.1 collective-permute-start.3
  278.2 9.9 collective-permute-start.1
  280.9 3.8 collective-permute-start.5
  490.5 20.1 %all-to-all-start.4 = ((f32[8,1,32768]{2,1,0:T(1,128)}), f32[8,1,32768]{2,1,0:T(1,128)}, u32[]{:S(2)}, u32[]{:S(2)}) async-start(f32[8,1,32768]{2,1,0:T(1,128)} %reshape.610), calls=%async_computation.4 | async-start | bytes 2097152 | tf_op jit(solution)/shard_map/all_to_all | solution.py:198
  808.2 12.4 collective-permute-start.6
  809.9 10.8 collective-permute-start.7
  811.2 5.8 collective-permute-start.9
  818.3 117.5 %collective-permute-start.8 = (f32[1,16,1024]{2,1,0:T(8,128)}, f32[1,16,1024]{2,1,0:T(8,128)}, u32[]{:S(2)}, u32[]{:S(2)}) collective-permute-start(f32[1,16,1024]{2,1,0:T(8,128)} %get-tuple-element.1047), channel_id=1, source_target_pairs={{1,0},{2,1},{3,2},{4,3},{5,4},{6,5},{7,6},{9,8},{10,9},{11,10},{12... | collective-permute-start | bytes 196616 | tf_op jit(solution)/shard_map/ppermute | solution.py:34
  1029.0 20.2 %all-to-all-start.6 = ((f32[8,1,32768]{2,1,0:T(1,128)}), f32[8,1,32768]{2,1,0:T(1,128)}, u32[]{:S(2)}, u32[]{:S(2)}) async-start(f32[8,1,32768]{2,1,0:T(1,128)} %reshape.612), calls=%async_computation.6 | async-start | bytes 2097152 | tf_op jit(solution)/shard_map/all_to_all | solution.py:198
  1401.3 12.2 collective-permute-start.10
  1402.8 10.8 collective-permute-start.11
  1404.1 6.0 collective-permute-start.13
  1411.4 117.4 %collective-permute-start.12 = (f32[1,16,1024]{2,1,0:T(8,128)}, f32[1,16,1024]{2,1,0:T(8,128)}, u32[]{:S(2)}, u32[]{:S(2)}) collective-permute-start(f32[1,16,1024]{2,1,0:T(8,128)} %get-tuple-element.1045), channel_id=1, source_target_pairs={{1,0},{2,1},{3,2},{4,3},{5,4},{6,5},{7,6},{9,8},{10,9},{11,10},{12... | collective-permute-start | bytes 196616 | tf_op jit(solution)/shard_map/ppermute | solution.py:34
  1623.3 20.2 %all-to-all-start.8 = ((f32[8,1,32768]{2,1,0:T(1,128)}), f32[8,1,32768]{2,1,0:T(1,128)}, u32[]{:S(2)}, u32[]{:S(2)}) async-start(f32[8,1,32768]{2,1,0:T(1,128)} %reshape.614), calls=%async_computation.8 | async-start | bytes 2097152 | tf_op jit(solution)/shard_map/all_to_all | solution.py:198
  (45 other events, 2453.3 us)
where the time goes:
time: 2020 us; the launch traced here: 1990 us
  local copies, waits for them, and re-layouts  1020 us (50%)
  blocking collectives  453 us (22%)
  other arithmetic  202 us (10%)
  matrix products  169 us (8%)
  starting transfers between devices  71.4 us (4%)
  waiting for transfers between devices  63.2 us (3%)
    while x128, local copies, waits for them, and re-layouts  359 us
    psum x4, blocking collectives, residual_norm(): return lax.psum(jnp.sum(residual * smoothed), ('elem', 'lev'))  259 us
    gather x3, local copies, waits for them, and re-layouts, penalty_term(): jnp.take(flattened, position.reshape(-1), axis=1)  214 us
    psum x2, blocking collectives, body(): curvature = lax.psum(jnp.sum(direction * applied), ('elem', 'lev'))  136 us
    unnamed x122, local copies, waits for them, and re-layouts  130 us
    dot_general x64, matrix products, forward(): jnp.einsum('ije,jke->ike', matrix, lifted, precision=lax.Precision.HIGHEST)  128 us
    dynamic_update_slice x64, other arithmetic, column_solve(): unused, solved = lax.scan(forward, initial, (blocks, inverse, coupling))  71.3 us
    all_to_all x3, blocking collectives, precondition(): lax.all_to_all(columns, 'lev', split_axis=0, concat_axis=2, tiled=True)  57.1 us
  transfers between devices with their start and end apart: 21, of which 6 were waited for; matrix products, arithmetic and copies ran while one was open for 23% of the time, Pallas kernels for 0%

commit v1 on v0

v1 whole, which is shorter than its diff:
```python
import math

import jax
import jax.numpy as jnp
import numpy as np
from jax import lax
from jax.experimental import pallas as pl
from jax.experimental.pallas import tpu as pltpu
from jax.sharding import PartitionSpec as P

COLUMNS = 128
ITERATIONS = 3
BORDER = COLUMNS + 1
LANES = 128
LEVELS = 16
NODES = 16
GROUPS = 8
PENALTY = 2.0
ABSENT = 15 * LANES
VMEM_BYTES = 40 * 1024 * 1024
F32 = jnp.float32
BF16 = jnp.bfloat16


def gradient_table():
    root = 1.0 / math.sqrt(5.0)
    points = [-1.0, -root, root, 1.0]
    legendre = [0.5 * (5.0 * p * p * p - 3.0 * p) for p in points]
    matrix = [[0.0 for col in range(4)] for row in range(4)]
    for row in range(4):
        for col in range(4):
            if row != col:
                matrix[row][col] = legendre[row] / (legendre[col] * (points[row] - points[col]))
    matrix[0][0] = -3.0
    matrix[3][3] = 3.0
    derivative = np.array(matrix)
    return np.kron(np.eye(4), derivative), np.kron(derivative, np.eye(4))


def stacked_tables():
    along_x, along_y = gradient_table()
    table = np.concatenate([np.kron(np.eye(8), along_x), np.kron(np.eye(8), along_y)], axis=0)
    table = jnp.asarray(table, F32)
    high = table.astype(BF16)
    low = (table - high.astype(F32)).astype(BF16)
    return jnp.stack([high, low]), jnp.stack([high.T, low.T])


def lane_take(values, index):
    return jnp.take_along_axis(values, index, axis=1, mode="promise_in_bounds")


def row_take(values, index):
    return jnp.take_along_axis(values, index, axis=0, mode="promise_in_bounds")


def iotas():
    rows = lax.broadcasted_iota(jnp.int32, (8, LANES), 0)
    lanes = lax.broadcasted_iota(jnp.int32, (8, LANES), 1)
    return rows, lanes


def by_row(rows, values):
    index = jnp.zeros_like(rows)
    for row, value in enumerate(values):
        if value:
            index = jnp.where(rows == row, value, index)
    return index


def edge_table(low, high, rows):
    from_low = row_take(low, by_row(rows, [1, 2, 7, 0, 0, 0, 4, 0]))
    from_high = row_take(high, by_row(rows, [0, 0, 0, 3, 5, 6, 0, 0]))
    use_low = (rows < 3) | (rows == 6)
    return jnp.where(use_low, from_low, from_high)


def corner_table(low, high, low_next, high_next, rows):
    index_low = by_row(rows, [0, 3, 0, 0, 0, 3, 0, 0])
    index_high = by_row(rows, [0, 0, 7, 4, 0, 0, 7, 4])
    first = jnp.where(rows < 2, row_take(low, index_low), row_take(high, index_high))
    second = jnp.where(rows < 6, row_take(low_next, index_low), row_take(high_next, index_high))
    return jnp.where(rows < 4, first, second)


def store_tables(load, rows, put):
    for pair in range(LEVELS // 2):
        even = load(2 * pair)
        odd = load(2 * pair + 1)
        put(2 * pair, edge_table(even[:8], even[8:], rows))
        put(2 * pair + 1, edge_table(odd[:8], odd[8:], rows))
        put(LEVELS + pair, corner_table(even[:8], even[8:], odd[:8], odd[8:], rows))


def gather_pick(table, first_tile, ints, counts, lists, per_list, tile, edges, corners, pick):
    rows, lanes = iotas()
    for item in range(16):
        source = jnp.broadcast_to(ints[item : item + 1, :], (8, LANES))
        lane = jnp.bitwise_and(source, LANES - 1)
        holder = lax.shift_right_logical(source, 7)
        slot = item * 8 + tile
        members = range(LEVELS) if item < 4 else range(LEVELS, LEVELS + 8)

        def step(turn, sums, lane=lane, holder=holder, slot=slot, members=members):
            which = lists[slot * per_list + turn]
            hit = holder == which
            column = pl.multiple_of((which - first_tile) * LANES, LANES)
            return tuple(
                jnp.where(hit, lane_take(table[member, :, pl.ds(column, LANES)], lane), value)
                for member, value in zip(members, sums)
            )

        start = tuple(jnp.zeros((8, LANES), F32) for member in members)
        sums = lax.fori_loop(0, counts[slot], step, start)
        for position, value in enumerate(sums):
            if item < 4:
                edges[item, position] = value
            else:
                corners[item - 4, position] = value
    low_index = ints[16:24, :]
    high_index = ints[24:32, :]
    for level in range(LEVELS):
        pair, half = level // 2, level % 2
        low = jnp.where(
            (rows == 1) | (rows == 2),
            row_take(edges[0, level], low_index),
            jnp.where(
                rows == 7, row_take(edges[1, level], low_index), row_take(edges[3, level], low_index)
            ),
        )
        low = jnp.where((rows == 5) | (rows == 6), 0.0, low)
        high = jnp.where(
            rows == 3,
            row_take(edges[1, level], high_index),
            jnp.where(rows == 0, row_take(edges[3, level], high_index), row_take(edges[2, level], high_index)),
        )
        high = jnp.where((rows == 1) | (rows == 2), 0.0, high)
        sums = []
        for corner in range(4):
            total = None
            for other in range(3):
                item = 3 * corner + other
                index = jnp.broadcast_to(ints[36 + item : 37 + item, :], (8, LANES)) + 4 * half
                value = row_take(corners[item, pair], index)
                total = value if total is None else total + value
            sums.append(total)
        low = jnp.where(rows == 0, sums[0], jnp.where(rows == 3, sums[1], low))
        high = jnp.where(rows == 7, sums[2], jnp.where(rows == 4, sums[3], high))
        pick[level, 0:8, :] = low
        pick[level, 8:16, :] = high


def group_rows(inverse, vertical):
    link0, link1 = vertical[7:8, :], vertical[15:16, :]
    up0 = link0 * inverse[0, 7, 0:1, :]
    up1 = link1 * inverse[1, 7, 0:1, :]
    down0 = link0 * inverse[0, 0, 7:8, :]
    down1 = link1 * inverse[1, 0, 7:8, :]
    response = inverse[0, 0, 0:1, :] + down0 * inverse[1, 0, 0:1, :] * up0
    return up1 * up0, response, down0 * down1


def group_response(load, inverse, vertical):
    link0, link1 = vertical[7:8, :], vertical[15:16, :]
    down0 = link0 * inverse[0, 0, 7:8, :]
    last0 = first0 = last1 = first1 = None
    for j in range(8):
        value0, value1 = load(j), load(8 + j)
        terms = (
            inverse[0, 7, j : j + 1, :] * value0,
            inverse[0, 0, j : j + 1, :] * value0,
            inverse[1, 7, j : j + 1, :] * value1,
            inverse[1, 0, j : j + 1, :] * value1,
        )
        if j == 0:
            last0, first0, last1, first1 = terms
        else:
            last0, first0, last1, first1 = (
                last0 + terms[0],
                first0 + terms[1],
                last1 + terms[2],
                first1 + terms[3],
            )
    carried = link0 * last0
    upward = link1 * (last1 + inverse[1, 7, 0:1, :] * carried)
    downward = first0 + down0 * (first1 + inverse[1, 0, 0:1, :] * carried)
    return upward, downward


def total_of(values):
    return jnp.sum(jnp.sum(values, axis=1, keepdims=True), axis=0, keepdims=True)


def begin_kernel(count, right_side, inverse, vertical, residual, message):
    tile = pl.program_id(0)
    lanes = lax.broadcasted_iota(jnp.int32, (NODES, LANES), 1)
    living = lanes + tile * LANES < count[0]

    for level in range(LEVELS):
        residual[level] = jnp.where(living, right_side[level], 0.0)
    upward, downward = group_response(lambda level: residual[level], inverse, vertical)
    message[0, 0:16, :] = upward
    message[0, 16:32, :] = downward
    coupling = group_rows(inverse, vertical)
    for row in range(3):
        message[0, 32 + row : 33 + row, :] = coupling[row]
    message[0, 35:40, :] = jnp.zeros((5, LANES), F32)


def scan_kernel(received, coupling, carried, dots):
    value = jnp.zeros((16, LANES), F32)
    for group in range(GROUPS):
        carried[group, 0:16, :] = value
        value = coupling[group, 0:1, :] * value + received[group, 0:16, :]
    value = jnp.zeros((16, LANES), F32)
    for group in reversed(range(GROUPS)):
        carried[group, 16:32, :] = value
        value = (
            received[group, 16:32, :]
            + coupling[group, 1:2, :] * carried[group, 0:16, :]
            + coupling[group, 2:3, :] * value
        )
    total = received[0, 32:33, :]
    for group in range(1, GROUPS):
        total = total + received[group, 32:33, :]
    dots[...] = jnp.broadcast_to(total, (16, LANES))


def solve_kernel(first, *refs):
    if first:
        count, residual_in, came, inverse, vertical = refs[:5]
        smoothed, product, tail, head, tables, parts = refs[5:]
        residual = residual_in
        state = came
    else:
        count, residual_in, image, came, state_in, dots, norm, inverse, vertical = refs[:9]
        residual, state, step, smoothed, product, tail, head, tables, parts = refs[9:]
        step_size = norm[0:1, :] / total_of(dots[...])
        for level in range(LEVELS):
            residual[level] = residual_in[level] - step_size * image[level]
        state[0] = state_in[0] - step_size * came[0]
        step[...] = jnp.broadcast_to(step_size, (8, LANES))
    tile = pl.program_id(0)
    rows, lanes = iotas()
    link0, link1 = vertical[7:8, :], vertical[15:16, :]
    below = state[0, 0:16, :]
    above = state[0, 16:32, :]

    def block_product(block, lifted):
        solved = []
        for i in range(8):
            total = inverse[block, i, 0:1, :] * lifted[0]
            for j in range(1, 8):
                total = total + inverse[block, i, j : j + 1, :] * lifted[j]
            solved.append(total)
        return solved

    values = [residual[level] for level in range(8)]
    lower = block_product(0, [values[0] + below] + values[1:])
    values = [residual[8 + level] for level in range(8)]
    upper = block_product(1, [values[0] + link0 * lower[7]] + values[1:])
    lift = link1 * above
    upper = [upper[i] + lift * inverse[1, i, 7:8, :] for i in range(8)]
    lift = link0 * upper[0]
    lower = [lower[i] + lift * inverse[0, i, 7:8, :] for i in range(8)]
    total = None
    for level, value in enumerate(lower + upper):
        smoothed[level] = value
        term = value * residual[level]
        total = term if total is None else total + term

    @pl.when(tile == 0)
    def clear():
        parts[...] = jnp.zeros((16, LANES), F32)
        tail[...] = jnp.zeros((25, 8, LANES), F32)
        head[...] = jnp.zeros((25, 8, LANES), F32)

    parts[...] += total

    @pl.when(tile == GROUPS - 1)
    def finish():
        product[...] = jnp.broadcast_to(jnp.sum(parts[...], axis=0, keepdims=True), (LANES, LANES))

    start = count[0] - LANES
    start_tile = lax.shift_right_logical(start, 7)
    offset = jnp.bitwise_and(start, LANES - 1)
    extra = start - 1
    extra_tile = lax.shift_right_logical(extra, 7)
    extra_lane = jnp.bitwise_and(extra, LANES - 1)
    in_tail = (tile == start_tile) | (tile == start_tile + 1)
    in_extra = tile == extra_tile

    def put(position, value):
        tables[position] = value

    @pl.when(in_tail | in_extra | (tile < 2))
    def build():
        store_tables(lambda level: smoothed[level], rows, put)

    @pl.when(in_tail)
    def fill_tail():
        index = jnp.bitwise_and(lanes + offset, LANES - 1)
        before_wrap = (lanes < LANES - offset).astype(jnp.int32)
        wanted = before_wrap == (tile == start_tile).astype(jnp.int32)
        for position in range(24):
            tail[position] = jnp.where(wanted, lane_take(tables[position], index), tail[position])

    @pl.when(in_extra)
    def fill_extra():
        index = jnp.zeros_like(lanes) + extra_lane
        packed = jnp.zeros((8, LANES), F32)
        for position in range(24):
            packed = jnp.where(lanes == position, lane_take(tables[position], index), packed)
        tail[24] = packed

    @pl.when(tile == 0)
    def fill_head():
        for position in range(24):
            head[position] = tables[position]

    @pl.when(tile == 1)
    def fill_head_extra():
        packed = jnp.zeros((8, LANES), F32)
        for position in range(24):
            packed = jnp.where(
                lanes == position, lane_take(tables[position], jnp.zeros_like(lanes)), packed
            )
        head[24] = packed


def split(values):
    high = values.astype(BF16)
    return high, (values - high.astype(F32)).astype(BF16)


def product3(table, values):
    high, low = split(values)
    result = jnp.dot(table[0], high, preferred_element_type=F32)
    result = result + jnp.dot(table[0], low, preferred_element_type=F32)
    return result + jnp.dot(table[1], high, preferred_element_type=F32)


def operate_kernel(
    helmholtz,
    counts,
    lists,
    field,
    ints,
    copies,
    metric,
    mass,
    vertical,
    below_row,
    state,
    forward,
    backward,
    applied,
    table,
    edges,
    corners,
    pick,
):
    tile = pl.program_id(0)
    rows, lanes = iotas()
    here = pl.ds(pl.multiple_of(tile * LANES, LANES), LANES)

    @pl.when(tile == 0)
    def build():
        def one(part, unused):
            there = pl.ds(pl.multiple_of(part * LANES, LANES), LANES)

            def put(position, value):
                table[position, :, there] = value

            store_tables(lambda level: field[level, :, there], rows, put)
            return unused

        lax.fori_loop(0, GROUPS, one, 0)

    gather_pick(table, 0, ints, counts, lists, 8, tile, edges, corners, pick)
    mixed, along_y, along_x = metric[1], metric[2], metric[0]
    for half in range(2):
        values = jnp.concatenate([field[8 * half + level, :, here] for level in range(8)], axis=0)
        gradients = product3(forward, values)
        flux_x = []
        flux_y = []
        for level in range(8):
            part_x = gradients[16 * level : 16 * level + 16]
            part_y = gradients[128 + 16 * level : 144 + 16 * level]
            flux_x.append(along_x * part_x + mixed * part_y)
            flux_y.append(mixed * part_x + along_y * part_y)
        stiff = product3(backward, jnp.concatenate(flux_x + flux_y, axis=0))
        for level in range(8):
            applied[8 * half + level] = stiff[16 * level : 16 * level + 16]
    twice = PENALTY * copies[...]
    flux = state[0, 0:16, :] + below_row[0:1, :] * field[0, :, here]
    for level in range(LEVELS):
        value = field[level, :, here]
        higher = field[level + 1, :, here] if level < LEVELS - 1 else state[0, 16:32, :]
        next_flux = vertical[level : level + 1, :] * (value - higher)
        applied[level] = (
            applied[level]
            + (helmholtz[level] * mass[...] + twice) * value
            + (next_flux - flux)
            - PENALTY * pick[level]
        )
        flux = next_flux


def image_kernel(first, *refs):
    if first:
        counts, lists, totals, applied, smoothed, ints, before, after, norms, inverse, vertical = refs[:11]
        refs = refs[11:]
    else:
        counts, lists, totals, applied, smoothed, ints, before, after, norms, inverse, vertical = refs[:11]
        norm_in, direction_in, image_in = refs[11:14]
        refs = refs[14:]
    direction, image, message, norm, table, edges, corners, pick, parts = refs
    tile = pl.program_id(0)
    rows, lanes = iotas()
    new = total_of(norms[...])
    norm[...] = jnp.broadcast_to(new, (8, LANES))

    @pl.when(tile == 0)
    def build():
        parts[...] = jnp.zeros((16, LANES), F32)
        for position in range(24):
            index = jnp.full((8, LANES), position, jnp.int32)
            table[position, :, 0:LANES] = before[position]
            table[position, :, LANES : 2 * LANES] = after[position]
            table[position, :, 2 * LANES : 3 * LANES] = jnp.where(
                lanes == 0, lane_take(before[24], index), lane_take(after[24], index)
            )

    pick[...] = jnp.zeros((LEVELS, NODES, LANES), F32)

    @pl.when(totals[tile] > 0)
    def reach():
        gather_pick(table, 8, ints, counts, lists, 3, tile, edges, corners, pick)

    if not first:
        ratio = new / norm_in[0:1, :]
    total = None
    for level in range(LEVELS):
        value = smoothed[level]
        result = applied[level] - PENALTY * pick[level]
        if not first:
            value = value + ratio * direction_in[level]
            result = result + ratio * image_in[level]
        direction[level] = value
        image[level] = result
        term = value * result
        total = term if total is None else total + term
    parts[...] += total
    upward, downward = group_response(lambda level: image[level], inverse, vertical)
    message[tile, 0:16, :] = upward
    message[tile, 16:32, :] = downward

    @pl.when(tile == GROUPS - 1)
    def finish():
        dot = jnp.sum(parts[...], axis=0, keepdims=True)
        for target in range(GROUPS):
            message[target, 32:33, :] = dot
            message[target, 33:40, :] = jnp.zeros((7, LANES), F32)


def field_spec():
    return pl.BlockSpec((LEVELS, NODES, LANES), lambda t: (0, 0, t))


def row_spec(rows):
    return pl.BlockSpec((rows, LANES), lambda t: (0, t))


def whole(*shape):
    return pl.BlockSpec(shape, lambda t: (0,) * len(shape))


def tile_spec(rows):
    return pl.BlockSpec((1, rows, LANES), lambda t: (t, 0, 0))


def inverse_spec():
    return pl.BlockSpec((2, 8, 8, LANES), lambda t: (0, 0, 0, t))


def scalars():
    return pl.BlockSpec(memory_space=pltpu.SMEM)


def struct(*shape):
    return jax.ShapeDtypeStruct(shape, F32)


def call(kernel, name, in_specs, out_specs, out_shape, scratch, cost, args):
    return pl.pallas_call(
        kernel,
        grid=(GROUPS,),
        in_specs=in_specs,
        out_specs=out_specs,
        out_shape=out_shape,
        scratch_shapes=scratch,
        name=name,
        compiler_params=pltpu.CompilerParams(
            dimension_semantics=("arbitrary",), vmem_limit_bytes=VMEM_BYTES
        ),
        cost_estimate=pl.CostEstimate(flops=cost, bytes_accessed=6 << 20, transcendentals=0),
    )(*args)


FIELD = (LEVELS, NODES, 1024)
PICK_SCRATCH = [
    ((4, LEVELS, 8, LANES), F32),
    ((12, 8, 8, LANES), F32),
    ((LEVELS, NODES, LANES), F32),
]


def vmem(shapes):
    return [pltpu.VMEM(shape, dtype) for shape, dtype in shapes]


def neighbour_lists(source, first_tile, tile_count):
    holder = (source // LANES).reshape(16, 8, LANES)
    tiles = first_tile + jnp.arange(tile_count, dtype=jnp.int32)
    used = jnp.any(holder[:, :, None, :] == tiles[None, None, :, None], axis=3)
    place = jnp.cumsum(used.astype(jnp.int32), axis=2) - 1
    slots = jnp.arange(tile_count, dtype=jnp.int32)
    chosen = used[:, :, :, None] & (place[:, :, :, None] == slots)
    lists = jnp.sum(jnp.where(chosen, tiles[None, None, :, None], 0), axis=2)
    counts = jnp.sum(used.astype(jnp.int32), axis=2)
    return counts, lists.astype(jnp.int32)


def neighbour_tables(edge_neighbour, edge_flip, corner_neighbour, count_before, position):
    slot_count = edge_neighbour.shape[0]

    def locate(element):
        holder = element // slot_count
        within = element % slot_count
        earlier = within - (count_before - BORDER)
        earlier = jnp.where(earlier == 0, 10 * LANES, 8 * LANES + earlier - 1)
        later = jnp.where(within < LANES, 9 * LANES + within, 10 * LANES + 1)
        return jnp.where(holder == position, within, jnp.where(holder < position, earlier, later))

    edges = jnp.transpose(edge_neighbour)
    flips = jnp.transpose(edge_flip)
    corners = jnp.transpose(corner_neighbour, (1, 2, 0)).reshape(12, slot_count)
    everything = jnp.concatenate([edges, corners], axis=0)
    present = everything >= 0
    target = jnp.where(present, everything, 0)
    source = jnp.where(present, locate(target // 4), ABSENT)
    side = target % 4
    straight = 2 * side[:4] + jnp.where(flips == 1, 1, 0)
    swapped = 2 * side[:4] + jnp.where(flips == 1, 0, 1)
    none = jnp.zeros_like(straight[0])
    low = [none, straight[0], swapped[0], none, straight[3], none, none, straight[1]]
    high = [swapped[3], none, none, swapped[1], none, straight[2], swapped[2], none]
    ints = jnp.concatenate([source, jnp.stack(low), jnp.stack(high), side], axis=0).astype(jnp.int32)
    on = present.astype(F32)
    shared = jnp.sum(on[4:].reshape(4, 3, slot_count), axis=1)
    nothing = jnp.zeros_like(shared[0])
    copies = jnp.stack(
        [
            shared[0], on[0], on[0], shared[1], on[3], nothing, nothing, on[1],
            on[3], nothing, nothing, on[1], shared[3], on[2], on[2], shared[2],
        ]
    )
    return source, ints, copies


def body(
    right_side,
    metric,
    mass_weight,
    helmholtz,
    vertical,
    block_inverse,
    edge_neighbour,
    edge_flip,
    corner_neighbour,
    element_count,
):
    peers = lax.axis_size("elem")
    groups = lax.axis_size("lev")
    position = lax.axis_index("elem")
    upward_elem = [(i, i + 1) for i in range(peers - 1)]
    downward_elem = [(i + 1, i) for i in range(peers - 1)]
    upward_lev = [(i, i + 1) for i in range(groups - 1)]

    residual, message = call(
        begin_kernel,
        "begin",
        [scalars(), field_spec(), inverse_spec(), row_spec(16)],
        [field_spec(), tile_spec(40)],
        [struct(*FIELD), struct(8, 40, LANES)],
        [],
        1 << 22,
        (element_count, right_side, block_inverse, vertical),
    )
    received = lax.all_to_all(message, "lev", split_axis=0, concat_axis=0, tiled=True)
    coupling = received[:, 32:40, :]

    def scan_groups(received):
        return pl.pallas_call(
            scan_kernel,
            out_shape=[struct(8, 32, LANES), struct(16, LANES)],
            name="scan",
            cost_estimate=pl.CostEstimate(flops=1 << 16, bytes_accessed=1 << 18, transcendentals=0),
        )(received, coupling)

    carried, unused = scan_groups(received)
    came = lax.all_to_all(carried, "lev", split_axis=0, concat_axis=0, tiled=True)

    count_before = lax.ppermute(element_count, "elem", upward_elem)[0]
    edge_rows = jnp.stack([vertical[15], block_inverse[1, 7, 7]])
    rows_below = lax.ppermute(edge_rows, "lev", upward_lev)
    below_row = (rows_below[0] * (rows_below[0] * rows_below[1] - 1.0))[None]
    source, ints, copies = neighbour_tables(
        edge_neighbour, edge_flip, corner_neighbour, count_before, position
    )
    own_counts, own_lists = neighbour_lists(source, 0, 8)
    far_counts, far_lists = neighbour_lists(source, 8, 3)
    far_totals = jnp.sum(far_counts, axis=0)
    own_counts, own_lists = own_counts.reshape(-1), own_lists.reshape(-1)
    far_counts, far_lists = far_counts.reshape(-1), far_lists.reshape(-1)
    forward, backward = stacked_tables()

    solve_scratch = vmem([((24, 8, LANES), F32), ((16, LANES), F32)])
    solve_outs = ([field_spec(), whole(LANES, LANES), whole(25, 8, LANES), whole(25, 8, LANES)],
                  [struct(*FIELD), struct(LANES, LANES), struct(25, 8, LANES), struct(25, 8, LANES)])
    smoothed, product, tail, head = call(
        lambda *refs: solve_kernel(True, *refs),
        "solve_first",
        [scalars(), field_spec(), tile_spec(32), inverse_spec(), row_spec(16)],
        *solve_outs,
        solve_scratch,
        1 << 22,
        (element_count, residual, came, block_inverse, vertical),
    )
    state = came
    solution = direction = image = norm = None
    for iteration in range(ITERATIONS):
        norms = lax.all_to_all(product, ("elem", "lev"), split_axis=0, concat_axis=0, tiled=True)
        before = lax.ppermute(tail, "elem", upward_elem)
        after = lax.ppermute(head, "elem", downward_elem)
        applied = call(
            operate_kernel,
            "operate",
            [
                scalars(), scalars(), scalars(), whole(*FIELD), row_spec(48), row_spec(16),
                pl.BlockSpec((3, NODES, LANES), lambda t: (0, 0, t)), row_spec(16), row_spec(16),
                row_spec(1), tile_spec(32), whole(2, 256, 128), whole(2, 128, 256),
            ],
            field_spec(),
            struct(*FIELD),
            vmem([((24, 8, 1024), F32)] + PICK_SCRATCH),
            1 << 30,
            (
                helmholtz, own_counts, own_lists, smoothed, ints, copies, metric, mass_weight,
                vertical, below_row, state, forward, backward,
            ),
        )
        first = iteration == 0
        args = [
            far_counts, far_lists, far_totals, applied, smoothed, ints, before, after, norms,
            block_inverse, vertical,
        ]
        specs = [
            scalars(), scalars(), scalars(), field_spec(), field_spec(), row_spec(48),
            whole(25, 8, LANES), whole(25, 8, LANES), whole(LANES, LANES), inverse_spec(), row_spec(16),
        ]
        if not first:
            args += [norm, direction, image]
            specs += [whole(8, LANES), field_spec(), field_spec()]
        direction, image, message, norm = call(
            lambda *refs, first=first: image_kernel(first, *refs),
            "image_first" if first else "image",
            specs,
            [field_spec(), field_spec(), whole(8, 40, LANES), whole(8, LANES)],
            [struct(*FIELD), struct(*FIELD), struct(8, 40, LANES), struct(8, LANES)],
            vmem([((24, 8, 3 * LANES), F32)] + PICK_SCRATCH + [((16, LANES), F32)]),
            1 << 22,
            args,
        )
        received = lax.all_to_all(message, "lev", split_axis=0, concat_axis=0, tiled=True)
        carried, dots = scan_groups(received)
        came = lax.all_to_all(carried, "lev", split_axis=0, concat_axis=0, tiled=True)
        dots = lax.all_to_all(dots, "elem", split_axis=0, concat_axis=0, tiled=True)
        residual, state, step, smoothed, product, tail, head = call(
            lambda *refs: solve_kernel(False, *refs),
            "solve",
            [
                scalars(), field_spec(), field_spec(), tile_spec(32), tile_spec(32), whole(16, LANES),
                whole(8, LANES), inverse_spec(), row_spec(16),
            ],
            [field_spec(), tile_spec(32), whole(8, LANES)] + solve_outs[0],
            [struct(*FIELD), struct(8, 32, LANES), struct(8, LANES)] + solve_outs[1],
            solve_scratch,
            1 << 22,
            (element_count, residual, image, came, state, dots, norm, block_inverse, vertical),
        )
        moved = step[0, 0] * direction
        solution = moved if first else solution + moved
    norms = lax.all_to_all(product, ("elem", "lev"), split_axis=0, concat_axis=0, tiled=True)
    direction = smoothed + jnp.sum(norms) / norm[0, 0] * direction
    return (solution, residual, direction)


def solution(mesh):
    in_specs = (
        P("lev", None, "elem"),
        P(None, None, "elem"),
        P(None, "elem"),
        P("lev"),
        P("lev", "elem"),
        P("lev", None, None, "elem"),
        P("elem", None),
        P("elem", None),
        P("elem", None, None),
        P("elem"),
    )
    out_specs = (P("lev", None, "elem"), P("lev", None, "elem"), P("lev", None, "elem"))
    return jax.shard_map(body, mesh=mesh, in_specs=in_specs, out_specs=out_specs, check_vma=False)
```

time: 2020 us -> 369 us (0.18); the launches traced: 1990 us -> 369 us
  local copies, waits for them, and re-layouts: 1020 us -> 48 us
  blocking collectives: 453 us -> 147 us
  other arithmetic: 202 us -> 12.8 us
  matrix products: 169 us -> 0 us
  Pallas kernels: 0 us -> 87.8 us
  waiting for transfers between devices: 63.2 us -> 11.4 us
    psum x6 -> x0, blocking collectives: 396 us -> none  [the longest x4 259 us: residual_norm(): return lax.psum(jnp.sum(residual * smoothed), ('elem', 'lev'))]
    while x129 -> x0, local copies, waits for them, and re-layouts: 364 us -> none
    gather x3 -> x0, local copies, waits for them, and re-layouts: 214 us -> none  [penalty_term(): jnp.take(flattened, position.reshape(-1), axis=1)]
    dot_general x79 -> x0, matrix products: 169 us -> none  [the longest x64 128 us: forward(): jnp.einsum('ije,jke->ike', matrix, lifted, precision=lax.Precision.HIGHEST)]
    all_to_all x3 -> x9, blocking collectives: 57.1 us -> 147 us  [the longest x3 81.8 us: body(): dots = lax.all_to_all(dots, 'elem', split_axis=0, concat_axis=0, tiled=True)]
    unnamed x122 -> x99, local copies, waits for them, and re-layouts: 130 us -> 42.2 us
    pallas_call x0 -> x15, Pallas kernels: none -> 87.8 us  [the longest x11 81.3 us: call(): pl.pallas_call(kernel, grid=(GROUPS,), in_specs=in_specs, out_specs=out_s...]
    dynamic_update_slice x64 -> x0, other arithmetic: 71.3 us -> none  [column_solve(): unused, solved = lax.scan(forward, initial, (blocks, inverse, coupling))]
  transfers between devices with their start and end apart: 21 -> 14, of which waited for: 6 -> 2; matrix products, arithmetic and copies ran while one was open for 23% -> 3% of each run, Pallas kernels for 0% -> 15%
where the time goes in v1:
time: 369 us
  blocking collectives  147 us (40%)
  Pallas kernels  87.8 us (24%)
  starting transfers between devices  59.2 us (16%)
  local copies, waits for them, and re-layouts  48 us (13%)
  other arithmetic  12.8 us (3%)
  waiting for transfers between devices  11.4 us (3%)
  between operations  3.8 us (1%)
    all_to_all x3, blocking collectives, body(): dots = lax.all_to_all(dots, 'elem', split_axis=0, concat_axis=0, tiled=True)  81.8 us
    pallas_call x11, Pallas kernels, call(): pl.pallas_call(kernel, grid=(GROUPS,), in_specs=in_specs, out_specs=out_s...  81.3 us
    unnamed x99, local copies, waits for them, and re-layouts  42.2 us
    all_to_all x3, blocking collectives, body(): lax.all_to_all(carried, 'lev', split_axis=0, concat_axis=0, tiled=True)  32.8 us
    all_to_all x3, blocking collectives, body(): lax.all_to_all(message, 'lev', split_axis=0, concat_axis=0, tiled=True)  32 us
    all_to_all x4, starting transfers between devices, body(): lax.all_to_all(product, ('elem', 'lev'), split_axis=0, concat_axis=0, til...  29.3 us
    all_to_all x4, waiting for transfers between devices, body(): lax.all_to_all(product, ('elem', 'lev'), split_axis=0, concat_axis=0, til...  7.38 us
  transfers between devices with their start and end apart: 14, of which 2 were waited for; matrix products, arithmetic and copies ran while one was open for 3% of the time, Pallas kernels for 15%

profile of v1, /device:TPU:1, one launch (start us, length us, event | category | flops | bytes accessed | tf_op | source)
XLA Modules:
  0.0 369.4 jit_solution(11406156253702563423)
XLA Ops:
  0.6 4.6 %collective-permute-start = (s32[1]{0:T(128)}, s32[1]{0:T(128)}, u32[]{:S(2)}, u32[]{:S(2)}) collective-permute-start(s32[1]{0:T(128)} %param.20), channel_id=1, source_target_pairs={{0,8},{8,16},{16,24},{24,32},{32,40},{40,48},{48,56},{56,64},{64,7... | collective-permute-start | bytes 20 | tf_op jit(solution)/shard_map/ppermute | solution.py:615
  17.8 5.1 %all-to-all-start = ((f32[8,40,128]{2,1,0:T(8,128)}), f32[8,40,128]{2,1,0:T(8,128)S(1)}, u32[]{:S(2)}, u32[]{:S(2)}) async-start(f32[8,40,128]{2,1,0:T(8,128)} %get-tuple-element.47), calls=%async_computation | async-start | bytes 327680 | tf_op jit(solution)/shard_map/all_to_all | solution.py:601
  34.5 4.9 %all-to-all-start.1 = ((f32[8,32,128]{2,1,0:T(8,128)}), f32[8,32,128]{2,1,0:T(8,128)S(1)}, u32[]{:S(2)}, u32[]{:S(2)}) async-start(f32[8,32,128]{2,1,0:T(8,128)} %get-tuple-element.48), calls=%async_computation.1 | async-start | bytes 262144 | tf_op jit(solution)/shard_map/all_to_all | solution.py:613
  51.3 9.1 %all-to-all-start.2 = ((f32[128,1,128]{2,1,0:T(1,128)}), f32[128,1,128]{2,1,0:T(1,128)S(1)}, u32[]{:S(2)}, u32[]{:S(2)}) async-start(f32[128,1,128]{2,1,0:T(1,128)} %bitcast.7), calls=%async_computation.2 | async-start | bytes 131072 | tf_op jit(solution)/shard_map/all_to_all | solution.py:644
  64.6 16.2 %operate.3.refs_3_ = f32[16,16,1024]{2,1,0:T(8,128)S(1)} custom-call(f32[16]{0:T(128)S(1)} %copy-done.38, s32[128]{0:T(128)S(1)} %reshape.163.counts, s32[1024]{0:T(1024)S(1)} %reshape.164.lists, f32[16,16,1024]{2,1,0:T(8,128)S(1)} %get-tuple-element.49.field.refs_4_, s32[48,1024]{1,0:T(8,128)S(1)} %concatenate.23.ints.refs_5_, ...), custom_call_target="tpu_custom_call" | custom-call | flops 1073741824 | bytes 6291456 | tf_op jit(solution)/shard_map/operate/pallas_call | solution.py:496
  84.3 4.8 %image_first.1 = (f32[16,16,1024]{2,1,0:T(8,128)S(1)}, f32[16,16,1024]{2,1,0:T(8,128)S(1)}, f32[8,40,128]{2,1,0:T(8,128)S(1)}, f32[8,128]{1,0:T(8,128)S(1)}) custom-call(s32[128]{0:T(128)S(1)} %reshape.161.refs_0_, s32[384]{0:T(512)S(1)} %reshape.162.refs_1_, s32[8]{0:T(128)S(1)} %get-tuple-element.89.refs_2_, f32[16,16,1024]{2,1,0:T(8,128)S(1)} %copy-done.12, ...), custom_call_target="tpu_custom_call" | custom-call | flops 4194304 | bytes 6291456 | tf_op jit(solution)/shard_map/image_first/pallas_call | solution.py:496
  90.0 10.7 %all_to_all.115.received = f32[8,40,128]{2,1,0:T(8,128)} all-to-all(f32[8,40,128]{2,1,0:T(8,128)S(1)} %get-tuple-element.54), channel_id=1, replica_groups=mesh['elem'=16,'lev'=8] {'lev'}, dimensions={0} | all-to-all | bytes 327680 | tf_op jit(solution)/shard_map/all_to_all | solution.py:686
  102.3 27.3 %all_to_all.116 = f32[16,1,128]{2,1,0:T(1,128)S(1)} all-to-all(f32[16,1,128]{2,1,0:T(1,128)} %bitcast.54), channel_id=1, replica_groups=mesh['elem'=16,'lev'=8] {'elem'}, dimensions={0} | all-to-all | bytes 16384 | tf_op jit(solution)/shard_map/all_to_all | solution.py:689
  129.6 10.9 %all_to_all.117.refs_3_ = f32[8,32,128]{2,1,0:T(8,128)S(1)} all-to-all(f32[8,32,128]{2,1,0:T(8,128)} %get-tuple-element.55), channel_id=1, replica_groups=mesh['elem'=16,'lev'=8] {'lev'}, dimensions={0} | all-to-all | bytes 262144 | tf_op jit(solution)/shard_map/all_to_all | solution.py:688
  149.7 8.0 %all-to-all-start.6 = ((f32[128,1,128]{2,1,0:T(1,128)}), f32[128,1,128]{2,1,0:T(1,128)S(1)}, u32[]{:S(2)}, u32[]{:S(2)}) async-start(f32[128,1,128]{2,1,0:T(1,128)} %bitcast.14), calls=%async_computation.6 | async-start | bytes 131072 | tf_op jit(solution)/shard_map/all_to_all | solution.py:644
  162.4 16.2 %operate.4.refs_3_ = f32[16,16,1024]{2,1,0:T(8,128)S(1)} custom-call(f32[16]{0:T(128)S(1)} %copy-done.38, s32[128]{0:T(128)S(1)} %reshape.163.counts, s32[1024]{0:T(1024)S(1)} %reshape.164.lists, f32[16,16,1024]{2,1,0:T(8,128)S(1)} %copy-done.26, s32[48,1024]{1,0:T(8,128)S(1)} %concatenate.23.ints.refs_5_, f32[16,1024]{1,0:T(8,128)S(1)} %stack.24.copies, ...), custom_call_target="tpu_custom_call" | custom-call | flops 1073741824 | bytes 6291456 | tf_op jit(solution)/shard_map/operate/pallas_call | solution.py:496
  183.3 5.2 %image.2 = (f32[16,16,1024]{2,1,0:T(8,128)S(1)}, f32[16,16,1024]{2,1,0:T(8,128)S(1)}, f32[8,40,128]{2,1,0:T(8,128)S(1)}, f32[8,128]{1,0:T(8,128)S(1)}) custom-call(s32[128]{0:T(128)S(1)} %reshape.161.refs_0_, s32[384]{0:T(512)S(1)} %reshape.162.refs_1_, s32[8]{0:T(128)S(1)} %get-tuple-element.89.refs_2_, f32[16,16,1024]{2,1,0:T(8,128)S(1)} %copy-done.31, ...), custom_call_target="tpu_custom_call" | custom-call | flops 4194304 | bytes 6291456 | tf_op jit(solution)/shard_map/image/pallas_call | solution.py:496
  189.5 10.7 %all_to_all.118.received = f32[8,40,128]{2,1,0:T(8,128)} all-to-all(f32[8,40,128]{2,1,0:T(8,128)S(1)} %get-tuple-element.67), channel_id=1, replica_groups=mesh['elem'=16,'lev'=8] {'lev'}, dimensions={0} | all-to-all | bytes 327680 | tf_op jit(solution)/shard_map/all_to_all | solution.py:686
  201.8 27.3 %all_to_all.119 = f32[16,1,128]{2,1,0:T(1,128)S(1)} all-to-all(f32[16,1,128]{2,1,0:T(1,128)} %bitcast.55), channel_id=1, replica_groups=mesh['elem'=16,'lev'=8] {'elem'}, dimensions={0} | all-to-all | bytes 16384 | tf_op jit(solution)/shard_map/all_to_all | solution.py:689
  229.1 10.9 %all_to_all.120.refs_3_ = f32[8,32,128]{2,1,0:T(8,128)S(1)} all-to-all(f32[8,32,128]{2,1,0:T(8,128)} %get-tuple-element.68), channel_id=1, replica_groups=mesh['elem'=16,'lev'=8] {'lev'}, dimensions={0} | all-to-all | bytes 262144 | tf_op jit(solution)/shard_map/all_to_all | solution.py:688
  250.4 8.0 %all-to-all-start.10 = ((f32[128,1,128]{2,1,0:T(1,128)}), f32[128,1,128]{2,1,0:T(1,128)S(1)}, u32[]{:S(2)}, u32[]{:S(2)}) async-start(f32[128,1,128]{2,1,0:T(1,128)} %bitcast.21), calls=%async_computation.10 | async-start | bytes 131072 | tf_op jit(solution)/shard_map/all_to_all | solution.py:644
  263.1 16.2 %operate.5.refs_3_ = f32[16,16,1024]{2,1,0:T(8,128)S(1)} custom-call(f32[16]{0:T(128)S(1)} %copy-done.38, s32[128]{0:T(128)S(1)} %reshape.163.counts, s32[1024]{0:T(1024)S(1)} %reshape.164.lists, f32[16,16,1024]{2,1,0:T(8,128)S(1)} %copy-done.22, s32[48,1024]{1,0:T(8,128)S(1)} %concatenate.23.ints.refs_5_, f32[16,1024]{1,0:T(8,128)S(1)} %stack.24.copies, ...), custom_call_target="tpu_custom_call" | custom-call | flops 1073741824 | bytes 6291456 | tf_op jit(solution)/shard_map/operate/pallas_call | solution.py:496
  282.8 5.2 %image.3 = (f32[16,16,1024]{2,1,0:T(8,128)S(1)}, f32[16,16,1024]{2,1,0:T(8,128)S(1)}, f32[8,40,128]{2,1,0:T(8,128)S(1)}, f32[8,128]{1,0:T(8,128)S(1)}) custom-call(s32[128]{0:T(128)S(1)} %reshape.161.refs_0_, s32[384]{0:T(512)S(1)} %reshape.162.refs_1_, s32[8]{0:T(128)S(1)} %get-tuple-element.89.refs_2_, f32[16,16,1024]{2,1,0:T(8,128)S(1)} %copy-done.29, ...), custom_call_target="tpu_custom_call" | custom-call | flops 4194304 | bytes 6291456 | tf_op jit(solution)/shard_map/image/pallas_call | solution.py:496
  290.0 10.7 %all_to_all.121.received = f32[8,40,128]{2,1,0:T(8,128)} all-to-all(f32[8,40,128]{2,1,0:T(8,128)S(1)} %get-tuple-element.80), channel_id=1, replica_groups=mesh['elem'=16,'lev'=8] {'lev'}, dimensions={0} | all-to-all | bytes 327680 | tf_op jit(solution)/shard_map/all_to_all | solution.py:686
  302.3 27.2 %all_to_all.122 = f32[16,1,128]{2,1,0:T(1,128)S(1)} all-to-all(f32[16,1,128]{2,1,0:T(1,128)} %bitcast.53), channel_id=1, replica_groups=mesh['elem'=16,'lev'=8] {'elem'}, dimensions={0} | all-to-all | bytes 16384 | tf_op jit(solution)/shard_map/all_to_all | solution.py:689
  329.5 11.0 %all_to_all.123.refs_3_ = f32[8,32,128]{2,1,0:T(8,128)S(1)} all-to-all(f32[8,32,128]{2,1,0:T(8,128)} %get-tuple-element.81), channel_id=1, replica_groups=mesh['elem'=16,'lev'=8] {'lev'}, dimensions={0} | all-to-all | bytes 262144 | tf_op jit(solution)/shard_map/all_to_all | solution.py:688
  343.0 4.6 %solve.5 = (f32[16,16,1024]{2,1,0:T(8,128)}, f32[8,32,128]{2,1,0:T(8,128)}, f32[8,128]{1,0:T(8,128)S(1)}, f32[16,16,1024]{2,1,0:T(8,128)S(1)}, f32[128,128]{1,0:...) custom-call(s32[1]{0:T(128)S(6)} %copy.52.count.refs_0_, f32[16,16,1024]{2,1,0:T(8,128)S(1)} %copy-done.15, ...), custom_call_target="tpu_custom_call" | custom-call | flops 4194304 | bytes 6291456 | tf_op jit(solution)/shard_map/solve/pallas_call | solution.py:496
  354.9 7.4 %all-to-all-done.14 = f32[128,1,128]{2,1,0:T(1,128)S(1)} async-done(((f32[128,1,128]{2,1,0:T(1,128)}), f32[128,1,128]{2,1,0:T(1,128)S(1)}, u32[]{:S(2)}, u32[]{:S(2)}) %all-to-all-start.14) | async-done | bytes 65568 | tf_op jit(solution)/shard_map/all_to_all | solution.py:705
  364.3 5.2 %multiply_add_fusion = (f32[16,16,1024]{2,1,0:T(8,128)}, f32[16,16,1024]{2,1,0:T(8,128)}) fusion(f32[16,16,1024]{2,1,0:T(8,128)} %copy-done.24, f32[16,16,1024]{2,1,0:T(8,128)} %copy-done.20, f32[]{:T(128)S(6)} %div.73, f32[]{:T(128)} %bitcast.26, f32[16,16,1024]{2,1,0:T(8,128)S(1)} %copy-done.8, f32[]{:T(128)} %bitcast.19, f32[16,16,1024]{2,1,0:T(8,128)S(1)} %copy-done.6, ...), kind=kLoop, calls=%fused_computation | loop fusion | flops 1835008 | bytes 6291472 | tf_op jit(solution)/shard_map/add | solution.py:706
  (180 shorter events, 98.4 us)
Async XLA Ops:
  0.6 23.3 %collective-permute-start = (s32[1]{0:T(128)}, s32[1]{0:T(128)}, u32[]{:S(2)}, u32[]{:S(2)}) collective-permute-start(s32[1]{0:T(128)} %param.20), channel_id=1, source_target_pairs={{0,8},{8,16},{16,24},{24,32},{32,40},{40,48},{48,56},{56,64},{64,7... | collective-permute-start | bytes 20 | tf_op jit(solution)/shard_map/ppermute | solution.py:615
  6.8 44.5 %collective-permute-start.1 = (f32[2,1024]{1,0:T(2,128)S(1)}, f32[2,1024]{1,0:T(2,128)S(1)}, u32[]{:S(2)}, u32[]{:S(2)}) collective-permute-start(f32[2,1024]{1,0:T(2,128)S(1)} %pad_maximum_fusion), channel_id=1, source_target_pairs={{0,1},{1,2},{2,3},{3,4},{4,5},{5,6},{6,7},{8,9},{9,10},{10,11},{11... | collective-permute-start | bytes 24584 | tf_op jit(solution)/shard_map/ppermute | solution.py:617
  17.8 5.1 %copy-start.47 = (s32[1024,4,3]{0,1,2:T(4,128)S(1)}, s32[1024,4,3]{0,1,2:T(4,128)}, u32[]{:S(2)}) copy-start(s32[1024,4,3]{0,1,2:T(4,128)} %param.19) | copy-start | bytes 147460
  17.8 14.4 %all-to-all-start = ((f32[8,40,128]{2,1,0:T(8,128)}), f32[8,40,128]{2,1,0:T(8,128)S(1)}, u32[]{:S(2)}, u32[]{:S(2)}) async-start(f32[8,40,128]{2,1,0:T(8,128)} %get-tuple-element.47), calls=%async_computation | async-start | bytes 327680 | tf_op jit(solution)/shard_map/all_to_all | solution.py:601
  34.5 10.2 %copy-start.1 = (f32[2,8,8,1024]{3,2,1,0:T(8,128)S(1)}, f32[2,8,8,1024]{3,2,1,0:T(8,128)}, u32[]{:S(2)}) copy-start(f32[2,8,8,1024]{3,2,1,0:T(8,128)} %refs_7_.5) | copy-start | bytes 1572868
  34.5 10.2 %all-to-all-start.1 = ((f32[8,32,128]{2,1,0:T(8,128)}), f32[8,32,128]{2,1,0:T(8,128)S(1)}, u32[]{:S(2)}, u32[]{:S(2)}) async-start(f32[8,32,128]{2,1,0:T(8,128)} %get-tuple-element.48), calls=%async_computation.1 | async-start | bytes 262144 | tf_op jit(solution)/shard_map/all_to_all | solution.py:613
  40.6 4.1 %copy-start.3 = (f32[16,1024]{1,0:T(8,128)S(1)}, f32[16,1024]{1,0:T(8,128)}, u32[]{:S(2)}) copy-start(f32[16,1024]{1,0:T(8,128)} %refs_8_.5) | copy-start | bytes 196612
  47.3 33.5 %copy-start.9 = (f32[16,16,1024]{2,1,0:T(8,128)}, f32[16,16,1024]{2,1,0:T(8,128)S(1)}, u32[]{:S(2)}) copy-start(f32[16,16,1024]{2,1,0:T(8,128)S(1)} %get-tuple-element.49.field.refs_4_) | copy-start | bytes 3145732
  47.3 34.5 %collective-permute-start.2 = (f32[25,8,128]{2,1,0:T(8,128)}, f32[25,8,128]{2,1,0:T(8,128)S(1)}, u32[]{:S(2)}, u32[]{:S(2)}) collective-permute-start(f32[25,8,128]{2,1,0:T(8,128)} %get-tuple-element.50), channel_id=1, source_target_pairs={{0,8},{8,16},{16,24},{24,32},{32,40},{40,48},{48,56},{56,64},{64,7... | collective-permute-start | bytes 307208 | tf_op jit(solution)/shard_map/ppermute | solution.py:645
  50.0 31.9 %collective-permute-start.3 = (f32[25,8,128]{2,1,0:T(8,128)S(1)}, f32[25,8,128]{2,1,0:T(8,128)S(1)}, u32[]{:S(2)}, u32[]{:S(2)}) collective-permute-start(f32[25,8,128]{2,1,0:T(8,128)S(1)} %get-tuple-element.51), channel_id=1, source_target_pairs={{8,0},{16,8},{24,16},{32,24},{40,32},{48,40},{56,48},{64,56},{72,6... | collective-permute-start | bytes 307208 | tf_op jit(solution)/shard_map/ppermute | solution.py:646
  51.3 30.5 %all-to-all-start.2 = ((f32[128,1,128]{2,1,0:T(1,128)}), f32[128,1,128]{2,1,0:T(1,128)S(1)}, u32[]{:S(2)}, u32[]{:S(2)}) async-start(f32[128,1,128]{2,1,0:T(1,128)} %bitcast.7), calls=%async_computation.2 | async-start | bytes 131072 | tf_op jit(solution)/shard_map/all_to_all | solution.py:644
  81.8 1.2 copy-start.10
  146.2 33.5 %collective-permute-start.4 = (f32[25,8,128]{2,1,0:T(8,128)}, f32[25,8,128]{2,1,0:T(8,128)S(1)}, u32[]{:S(2)}, u32[]{:S(2)}) collective-permute-start(f32[25,8,128]{2,1,0:T(8,128)} %get-tuple-element.63), channel_id=1, source_target_pairs={{0,8},{8,16},{16,24},{24,32},{32,40},{40,48},{48,56},{56,64},{64,7... | collective-permute-start | bytes 307208 | tf_op jit(solution)/shard_map/ppermute | solution.py:645
  148.4 31.3 %collective-permute-start.5 = (f32[25,8,128]{2,1,0:T(8,128)S(1)}, f32[25,8,128]{2,1,0:T(8,128)S(1)}, u32[]{:S(2)}, u32[]{:S(2)}) collective-permute-start(f32[25,8,128]{2,1,0:T(8,128)S(1)} %get-tuple-element.64), channel_id=1, source_target_pairs={{8,0},{16,8},{24,16},{32,24},{40,32},{48,40},{56,48},{64,56},{72,6... | collective-permute-start | bytes 307208 | tf_op jit(solution)/shard_map/ppermute | solution.py:646
  149.7 30.0 %all-to-all-start.6 = ((f32[128,1,128]{2,1,0:T(1,128)}), f32[128,1,128]{2,1,0:T(1,128)S(1)}, u32[]{:S(2)}, u32[]{:S(2)}) async-start(f32[128,1,128]{2,1,0:T(1,128)} %bitcast.14), calls=%async_computation.6 | async-start | bytes 131072 | tf_op jit(solution)/shard_map/all_to_all | solution.py:644
  157.6 1.2 copy-start.26
  246.9 33.5 %collective-permute-start.6 = (f32[25,8,128]{2,1,0:T(8,128)}, f32[25,8,128]{2,1,0:T(8,128)S(1)}, u32[]{:S(2)}, u32[]{:S(2)}) collective-permute-start(f32[25,8,128]{2,1,0:T(8,128)} %get-tuple-element.76), channel_id=1, source_target_pairs={{0,8},{8,16},{16,24},{24,32},{32,40},{40,48},{48,56},{56,64},{64,7... | collective-permute-start | bytes 307208 | tf_op jit(solution)/shard_map/ppermute | solution.py:645
  249.1 31.3 %collective-permute-start.7 = (f32[25,8,128]{2,1,0:T(8,128)S(1)}, f32[25,8,128]{2,1,0:T(8,128)S(1)}, u32[]{:S(2)}, u32[]{:S(2)}) collective-permute-start(f32[25,8,128]{2,1,0:T(8,128)S(1)} %get-tuple-element.77), channel_id=1, source_target_pairs={{8,0},{16,8},{24,16},{32,24},{40,32},{48,40},{56,48},{64,56},{72,6... | collective-permute-start | bytes 307208 | tf_op jit(solution)/shard_map/ppermute | solution.py:646
  250.4 30.0 %all-to-all-start.10 = ((f32[128,1,128]{2,1,0:T(1,128)}), f32[128,1,128]{2,1,0:T(1,128)S(1)}, u32[]{:S(2)}, u32[]{:S(2)}) async-start(f32[128,1,128]{2,1,0:T(1,128)} %bitcast.21), calls=%async_computation.10 | async-start | bytes 131072 | tf_op jit(solution)/shard_map/all_to_all | solution.py:644
  258.3 1.2 copy-start.22
  263.1 17.2 %copy-start.8 = (f32[16,16,1024]{2,1,0:T(8,128)S(1)}, f32[16,16,1024]{2,1,0:T(8,128)}, u32[]{:S(2)}) copy-start(f32[16,16,1024]{2,1,0:T(8,128)} %copy-done.7) | copy-start | bytes 3145732
  280.3 1.2 copy-start.23
  343.0 21.3 %copy-start.6 = (f32[16,16,1024]{2,1,0:T(8,128)S(1)}, f32[16,16,1024]{2,1,0:T(8,128)}, u32[]{:S(2)}) copy-start(f32[16,16,1024]{2,1,0:T(8,128)} %copy-done.4) | copy-start | bytes 3145732
  348.5 13.8 %all-to-all-start.14 = ((f32[128,1,128]{2,1,0:T(1,128)}), f32[128,1,128]{2,1,0:T(1,128)S(1)}, u32[]{:S(2)}, u32[]{:S(2)}) async-start(f32[128,1,128]{2,1,0:T(1,128)} %bitcast.28), calls=%async_computation.14 | async-start | bytes 131072 | tf_op jit(solution)/shard_map/all_to_all | solution.py:705
  (39 other events, 38.2 us)

commit v2 on v1

--- a/solution.py
+++ b/solution.py
@@ -17,7 +17,8 @@
 GROUPS = 8
 PENALTY = 2.0
 ABSENT = 15 * LANES
-VMEM_BYTES = 40 * 1024 * 1024
+VMEM_BYTES = 12 * 1024 * 1024
+SMALL_VMEM_BYTES = 4 * 1024 * 1024
 F32 = jnp.float32
 BF16 = jnp.bfloat16
 
@@ -94,60 +95,78 @@
 
 def gather_pick(table, first_tile, ints, counts, lists, per_list, tile, edges, corners, pick):
     rows, lanes = iotas()
-    for item in range(16):
-        source = jnp.broadcast_to(ints[item : item + 1, :], (8, LANES))
-        lane = jnp.bitwise_and(source, LANES - 1)
-        holder = lax.shift_right_logical(source, 7)
-        slot = item * 8 + tile
-        members = range(LEVELS) if item < 4 else range(LEVELS, LEVELS + 8)
-
-        def step(turn, sums, lane=lane, holder=holder, slot=slot, members=members):
-            which = lists[slot * per_list + turn]
-            hit = holder == which
-            column = pl.multiple_of((which - first_tile) * LANES, LANES)
-            return tuple(
-                jnp.where(hit, lane_take(table[member, :, pl.ds(column, LANES)], lane), value)
-                for member, value in zip(members, sums)
-            )
-
-        start = tuple(jnp.zeros((8, LANES), F32) for member in members)
-        sums = lax.fori_loop(0, counts[slot], step, start)
-        for position, value in enumerate(sums):
-            if item < 4:
-                edges[item, position] = value
-            else:
-                corners[item - 4, position] = value
+    edges[...] = jnp.zeros(edges.shape, F32)
+    corners[...] = jnp.zeros(corners.shape, F32)
+
+    def step(turn, unused):
+        which = lists[tile * per_list + turn]
+        column = pl.multiple_of((which - first_tile) * LANES, LANES)
+        values = [table[member, :, pl.ds(column, LANES)] for member in range(LEVELS + 8)]
+        for side in range(4):
+            source = jnp.broadcast_to(ints[side : side + 1, :], (8, LANES))
+            lane = jnp.bitwise_and(source, LANES - 1)
+            hit = lax.shift_right_logical(source, 7) == which
+            for place in range(LEVELS):
+                edges[side, place] = jnp.where(
+                    hit, lane_take(values[place], lane), edges[side, place]
+                )
+        for corner in range(4):
+            sums = [corners[corner, place] for place in range(8)]
+            for other in range(3):
+                item = 4 + 3 * corner + other
+                source = jnp.broadcast_to(ints[item : item + 1, :], (8, LANES))
+                node = jnp.broadcast_to(ints[32 + item : 33 + item, :], (8, LANES))
+                lane = jnp.bitwise_and(source, LANES - 1)
+                hit = (lax.shift_right_logical(source, 7) == which) & (
+                    jnp.bitwise_and(rows, 3) == node
+                )
+                for place in range(8):
+                    sums[place] = sums[place] + jnp.where(
+                        hit, lane_take(values[LEVELS + place], lane), 0.0
+                    )
+            for place in range(8):
+                corners[corner, place] = sums[place]
+        return unused
+
+    lax.fori_loop(0, counts[tile], step, 0)
     low_index = ints[16:24, :]
     high_index = ints[24:32, :]
-    for level in range(LEVELS):
-        pair, half = level // 2, level % 2
-        low = jnp.where(
-            (rows == 1) | (rows == 2),
-            row_take(edges[0, level], low_index),
-            jnp.where(
-                rows == 7, row_take(edges[1, level], low_index), row_take(edges[3, level], low_index)
-            ),
-        )
-        low = jnp.where((rows == 5) | (rows == 6), 0.0, low)
-        high = jnp.where(
-            rows == 3,
-            row_take(edges[1, level], high_index),
-            jnp.where(rows == 0, row_take(edges[3, level], high_index), row_take(edges[2, level], high_index)),
-        )
-        high = jnp.where((rows == 1) | (rows == 2), 0.0, high)
+    next_row = jnp.bitwise_and(rows, 4) + jnp.bitwise_and(rows + 1, 3)
+    next_pair = jnp.bitwise_and(rows, 4) + jnp.bitwise_and(rows + 2, 3)
+    other_half = jnp.bitwise_xor(rows, 4)
+    for pair in range(LEVELS // 2):
         sums = []
         for corner in range(4):
-            total = None
-            for other in range(3):
-                item = 3 * corner + other
-                index = jnp.broadcast_to(ints[36 + item : 37 + item, :], (8, LANES)) + 4 * half
-                value = row_take(corners[item, pair], index)
-                total = value if total is None else total + value
-            sums.append(total)
-        low = jnp.where(rows == 0, sums[0], jnp.where(rows == 3, sums[1], low))
-        high = jnp.where(rows == 7, sums[2], jnp.where(rows == 4, sums[3], high))
-        pick[level, 0:8, :] = low
-        pick[level, 8:16, :] = high
+            total = corners[corner, pair]
+            total = total + row_take(total, next_row)
+            total = total + row_take(total, next_pair)
+            sums.append((total, row_take(total, other_half)))
+        for half in range(2):
+            level = 2 * pair + half
+            low = jnp.where(
+                (rows == 1) | (rows == 2),
+                row_take(edges[0, level], low_index),
+                jnp.where(
+                    rows == 7,
+                    row_take(edges[1, level], low_index),
+                    row_take(edges[3, level], low_index),
+                ),
+            )
+            low = jnp.where((rows == 5) | (rows == 6), 0.0, low)
+            high = jnp.where(
+                rows == 3,
+                row_take(edges[1, level], high_index),
+                jnp.where(
+                    rows == 0,
+                    row_take(edges[3, level], high_index),
+                    row_take(edges[2, level], high_index),
+                ),
+            )
+            high = jnp.where((rows == 1) | (rows == 2), 0.0, high)
+            low = jnp.where(rows == 0, sums[0][half], jnp.where(rows == 3, sums[1][half], low))
+            high = jnp.where(rows == 7, sums[2][1 - half], jnp.where(rows == 4, sums[3][1 - half], high))
+            pick[level, 0:8, :] = low
+            pick[level, 8:16, :] = high
 
 
 def group_rows(inverse, vertical):
@@ -204,47 +223,103 @@
     coupling = group_rows(inverse, vertical)
     for row in range(3):
         message[0, 32 + row : 33 + row, :] = coupling[row]
-    message[0, 35:40, :] = jnp.zeros((5, LANES), F32)
-
-
-def scan_kernel(received, coupling, carried, dots):
+    link = vertical[15:16, :]
+    message[0, 35:36, :] = link * (link * inverse[1, 7, 7:8, :] - 1.0)
+    message[0, 36:40, :] = jnp.zeros((4, LANES), F32)
+
+
+def scan_groups(received, coupling, carried):
     value = jnp.zeros((16, LANES), F32)
     for group in range(GROUPS):
         carried[group, 0:16, :] = value
-        value = coupling[group, 0:1, :] * value + received[group, 0:16, :]
+        value = coupling[group, 32:33, :] * value + received[group, 0:16, :]
     value = jnp.zeros((16, LANES), F32)
     for group in reversed(range(GROUPS)):
         carried[group, 16:32, :] = value
         value = (
             received[group, 16:32, :]
-            + coupling[group, 1:2, :] * carried[group, 0:16, :]
-            + coupling[group, 2:3, :] * value
+            + coupling[group, 33:34, :] * carried[group, 0:16, :]
+            + coupling[group, 34:35, :] * value
         )
-    total = received[0, 32:33, :]
+
+
+def scan_first_kernel(received, carried):
+    scan_groups(received, received, carried)
+    for group in range(GROUPS):
+        below = received[group - 1, 35:36, :] if group else jnp.zeros((1, LANES), F32)
+        carried[group, 32:40, :] = jnp.broadcast_to(below, (8, LANES))
+
+
+def scan_kernel(received, coupling, carried, dots):
+    scan_groups(received, coupling, carried)
+    total = received[0, 32:40, :]
     for group in range(1, GROUPS):
-        total = total + received[group, 32:33, :]
-    dots[...] = jnp.broadcast_to(total, (16, LANES))
-
-
-def solve_kernel(first, *refs):
-    if first:
-        count, residual_in, came, inverse, vertical = refs[:5]
-        smoothed, product, tail, head, tables, parts = refs[5:]
-        residual = residual_in
-        state = came
+        total = total + received[group, 32:40, :]
+    dots[...] = total
+
+
+def solve_kernel(stage, last, *refs):
+    refs = list(refs)
+
+    def take(count):
+        taken = refs[:count]
+        del refs[:count]
+        return taken
+
+    count, inverse, vertical, residual_in, came = take(5)
+    if stage:
+        smoothed_in, applied, state_in, dots = take(4)
+    if stage == 2:
+        solution_in, direction_in, image_in, flow_in, scalars_in = take(5)
+    if stage:
+        solution, residual, direction, scalars_out = take(4)
+        if not last:
+            image, flow, state = take(3)
     else:
-        count, residual_in, image, came, state_in, dots, norm, inverse, vertical = refs[:9]
-        residual, state, step, smoothed, product, tail, head, tables, parts = refs[9:]
-        step_size = norm[0:1, :] / total_of(dots[...])
-        for level in range(LEVELS):
-            residual[level] = residual_in[level] - step_size * image[level]
-        state[0] = state_in[0] - step_size * came[0]
-        step[...] = jnp.broadcast_to(step_size, (8, LANES))
+        residual, state = residual_in, came
+    smoothed, product = take(2)
+    if not last:
+        tail, head, tables = take(3)
+    (parts,) = take(1)
     tile = pl.program_id(0)
     rows, lanes = iotas()
+
+    if stage:
+        norm = jnp.sum(dots[0:1, :], axis=1, keepdims=True)
+        curvature = jnp.sum(dots[1:2, :], axis=1, keepdims=True)
+        if stage == 2:
+            cross = jnp.sum(dots[2:3, :], axis=1, keepdims=True)
+            ratio = norm / scalars_in[0:1, 0:1]
+            curvature = curvature + ratio * cross + ratio * ratio * scalars_in[1:2, 0:1]
+        step_size = norm / curvature
+        scalars_out[0:1, :] = jnp.broadcast_to(norm, (1, LANES))
+        scalars_out[1:2, :] = jnp.broadcast_to(curvature, (1, LANES))
+        scalars_out[2:8, :] = jnp.zeros((6, LANES), F32)
+        for level in range(LEVELS):
+            value = smoothed_in[level]
+            result = applied[level]
+            if stage == 2:
+                value = value + ratio * direction_in[level]
+                result = result + ratio * image_in[level]
+                solution[level] = solution_in[level] + step_size * value
+            else:
+                solution[level] = step_size * value
+            direction[level] = value
+            if not last:
+                image[level] = result
+            residual[level] = residual_in[level] - step_size * result
+        change = came[0, 0:32, :]
+        if stage == 2:
+            change = change + ratio * flow_in[0]
+        incoming = state_in[0, 0:32, :] - step_size * change
+        if not last:
+            flow[0] = change
+            state[0] = incoming
+    else:
+        incoming = came[0, 0:32, :]
     link0, link1 = vertical[7:8, :], vertical[15:16, :]
-    below = state[0, 0:16, :]
-    above = state[0, 16:32, :]
+    below = incoming[0:16]
+    above = incoming[16:32]
 
     def block_product(block, lifted):
         solved = []
@@ -272,14 +347,20 @@
     @pl.when(tile == 0)
     def clear():
         parts[...] = jnp.zeros((16, LANES), F32)
+
+    parts[...] += total
+
+    @pl.when(tile == GROUPS - 1)
+    def finish():
+        product[...] = jnp.broadcast_to(jnp.sum(parts[...], axis=0, keepdims=True), product.shape)
+
+    if last:
+        return
+
+    @pl.when(tile == 0)
+    def clear_tail():
         tail[...] = jnp.zeros((25, 8, LANES), F32)
         head[...] = jnp.zeros((25, 8, LANES), F32)
-
-    parts[...] += total
-
-    @pl.when(tile == GROUPS - 1)
-    def finish():
-        product[...] = jnp.broadcast_to(jnp.sum(parts[...], axis=0, keepdims=True), (LANES, LANES))
 
     start = count[0] - LANES
     start_tile = lax.shift_right_logical(start, 7)
@@ -326,6 +407,12 @@
                 lanes == position, lane_take(tables[position], jnp.zeros_like(lanes)), packed
             )
         head[24] = packed
+
+
+def finish_kernel(norms, scalars_in, smoothed, direction_in, direction):
+    ratio = total_of(norms[...]) / scalars_in[0:1, 0:1]
+    for level in range(LEVELS):
+        direction[level] = smoothed[level] + ratio * direction_in[level]
 
 
 def split(values):
@@ -393,7 +480,7 @@
         for level in range(8):
             applied[8 * half + level] = stiff[16 * level : 16 * level + 16]
     twice = PENALTY * copies[...]
-    flux = state[0, 0:16, :] + below_row[0:1, :] * field[0, :, here]
+    flux = state[0, 0:16, :] + below_row[0, 32:33, :] * field[0, :, here]
     for level in range(LEVELS):
         value = field[level, :, here]
         higher = field[level + 1, :, here] if level < LEVELS - 1 else state[0, 16:32, :]
@@ -408,22 +495,19 @@
 
 
 def image_kernel(first, *refs):
-    if first:
-        counts, lists, totals, applied, smoothed, ints, before, after, norms, inverse, vertical = refs[:11]
-        refs = refs[11:]
-    else:
-        counts, lists, totals, applied, smoothed, ints, before, after, norms, inverse, vertical = refs[:11]
-        norm_in, direction_in, image_in = refs[11:14]
-        refs = refs[14:]
-    direction, image, message, norm, table, edges, corners, pick, parts = refs
+    counts, lists, applied, smoothed, ints, before, after, product, inverse, vertical = refs[:10]
+    refs = refs[10:]
+    if not first:
+        direction, previous = refs[:2]
+        refs = refs[2:]
+    image, message, table, edges, corners, pick, parts, crosses = refs
     tile = pl.program_id(0)
     rows, lanes = iotas()
-    new = total_of(norms[...])
-    norm[...] = jnp.broadcast_to(new, (8, LANES))
 
     @pl.when(tile == 0)
     def build():
         parts[...] = jnp.zeros((16, LANES), F32)
+        crosses[...] = jnp.zeros((16, LANES), F32)
         for position in range(24):
             index = jnp.full((8, LANES), position, jnp.int32)
             table[position, :, 0:LANES] = before[position]
@@ -434,34 +518,36 @@
 
     pick[...] = jnp.zeros((LEVELS, NODES, LANES), F32)
 
-    @pl.when(totals[tile] > 0)
+    @pl.when(counts[tile] > 0)
     def reach():
         gather_pick(table, 8, ints, counts, lists, 3, tile, edges, corners, pick)
 
-    if not first:
-        ratio = new / norm_in[0:1, :]
-    total = None
+    total = cross = None
     for level in range(LEVELS):
         value = smoothed[level]
         result = applied[level] - PENALTY * pick[level]
-        if not first:
-            value = value + ratio * direction_in[level]
-            result = result + ratio * image_in[level]
-        direction[level] = value
         image[level] = result
         term = value * result
         total = term if total is None else total + term
+        if not first:
+            term = value * previous[level] + direction[level] * result
+            cross = term if cross is None else cross + term
     parts[...] += total
+    if not first:
+        crosses[...] += cross
     upward, downward = group_response(lambda level: image[level], inverse, vertical)
     message[tile, 0:16, :] = upward
     message[tile, 16:32, :] = downward
 
     @pl.when(tile == GROUPS - 1)
     def finish():
-        dot = jnp.sum(parts[...], axis=0, keepdims=True)
+        curvature = jnp.sum(parts[...], axis=0, keepdims=True)
+        mixed = jnp.sum(crosses[...], axis=0, keepdims=True)
         for target in range(GROUPS):
-            message[target, 32:33, :] = dot
-            message[target, 33:40, :] = jnp.zeros((7, LANES), F32)
+            message[target, 32:33, :] = product[0:1, :]
+            message[target, 33:34, :] = curvature
+            message[target, 34:35, :] = mixed
+            message[target, 35:40, :] = jnp.zeros((5, LANES), F32)
 
 
 def field_spec():
@@ -511,7 +597,7 @@
 FIELD = (LEVELS, NODES, 1024)
 PICK_SCRATCH = [
     ((4, LEVELS, 8, LANES), F32),
-    ((12, 8, 8, LANES), F32),
+    ((4, 8, 8, LANES), F32),
     ((LEVELS, NODES, LANES), F32),
 ]
 
@@ -523,13 +609,30 @@
 def neighbour_lists(source, first_tile, tile_count):
     holder = (source // LANES).reshape(16, 8, LANES)
     tiles = first_tile + jnp.arange(tile_count, dtype=jnp.int32)
-    used = jnp.any(holder[:, :, None, :] == tiles[None, None, :, None], axis=3)
-    place = jnp.cumsum(used.astype(jnp.int32), axis=2) - 1
+    used = jnp.any(holder[:, :, None, :] == tiles[None, None, :, None], axis=(0, 3))
     slots = jnp.arange(tile_count, dtype=jnp.int32)
-    chosen = used[:, :, :, None] & (place[:, :, :, None] == slots)
-    lists = jnp.sum(jnp.where(chosen, tiles[None, None, :, None], 0), axis=2)
-    counts = jnp.sum(used.astype(jnp.int32), axis=2)
-    return counts, lists.astype(jnp.int32)
+    earlier = used[:, None, :] & (slots[None, None, :] < slots[None, :, None])
+    place = jnp.sum(earlier.astype(jnp.int32), axis=2)
+    chosen = used[:, :, None] & (place[:, :, None] == slots)
+    lists = jnp.sum(jnp.where(chosen, tiles[None, :, None], 0), axis=1)
+    return jnp.sum(used.astype(jnp.int32), axis=1), lists.astype(jnp.int32).reshape(-1)
+
+
+def sum_over_elem(value, peers):
+    side = math.isqrt(peers)
+    for inner in (True, False):
+        total = value
+        for shift in range(1, side):
+            pairs = []
+            for i in range(peers):
+                outer, within = i // side, i % side
+                if inner:
+                    pairs.append((i, outer * side + (within + shift) % side))
+                else:
+                    pairs.append((i, (outer + shift) % side * side + within))
+            total = total + lax.ppermute(value, "elem", pairs)
+        value = total
+    return value
 
 
 def neighbour_tables(edge_neighbour, edge_flip, corner_neighbour, count_before, position):
@@ -582,11 +685,9 @@
     element_count,
 ):
     peers = lax.axis_size("elem")
-    groups = lax.axis_size("lev")
     position = lax.axis_index("elem")
     upward_elem = [(i, i + 1) for i in range(peers - 1)]
     downward_elem = [(i + 1, i) for i in range(peers - 1)]
-    upward_lev = [(i, i + 1) for i in range(groups - 1)]
 
     residual, message = call(
         begin_kernel,
@@ -598,50 +699,44 @@
         1 << 22,
         (element_count, right_side, block_inverse, vertical),
     )
-    received = lax.all_to_all(message, "lev", split_axis=0, concat_axis=0, tiled=True)
-    coupling = received[:, 32:40, :]
-
-    def scan_groups(received):
-        return pl.pallas_call(
-            scan_kernel,
-            out_shape=[struct(8, 32, LANES), struct(16, LANES)],
-            name="scan",
-            cost_estimate=pl.CostEstimate(flops=1 << 16, bytes_accessed=1 << 18, transcendentals=0),
-        )(received, coupling)
-
-    carried, unused = scan_groups(received)
+    coupling = lax.all_to_all(message, "lev", split_axis=0, concat_axis=0, tiled=True)
+    scan_cost = pl.CostEstimate(flops=1 << 16, bytes_accessed=1 << 18, transcendentals=0)
+    small = pltpu.CompilerParams(vmem_limit_bytes=SMALL_VMEM_BYTES)
+    carried = pl.pallas_call(
+        scan_first_kernel,
+        out_shape=struct(8, 40, LANES),
+        name="scan_first",
+        cost_estimate=scan_cost,
+        compiler_params=small,
+    )(coupling)
     came = lax.all_to_all(carried, "lev", split_axis=0, concat_axis=0, tiled=True)
+    below_row = came
 
     count_before = lax.ppermute(element_count, "elem", upward_elem)[0]
-    edge_rows = jnp.stack([vertical[15], block_inverse[1, 7, 7]])
-    rows_below = lax.ppermute(edge_rows, "lev", upward_lev)
-    below_row = (rows_below[0] * (rows_below[0] * rows_below[1] - 1.0))[None]
     source, ints, copies = neighbour_tables(
         edge_neighbour, edge_flip, corner_neighbour, count_before, position
     )
     own_counts, own_lists = neighbour_lists(source, 0, 8)
     far_counts, far_lists = neighbour_lists(source, 8, 3)
-    far_totals = jnp.sum(far_counts, axis=0)
-    own_counts, own_lists = own_counts.reshape(-1), own_lists.reshape(-1)
-    far_counts, far_lists = far_counts.reshape(-1), far_lists.reshape(-1)
     forward, backward = stacked_tables()
 
-    solve_scratch = vmem([((24, 8, LANES), F32), ((16, LANES), F32)])
-    solve_outs = ([field_spec(), whole(LANES, LANES), whole(25, 8, LANES), whole(25, 8, LANES)],
-                  [struct(*FIELD), struct(LANES, LANES), struct(25, 8, LANES), struct(25, 8, LANES)])
+    shared_specs = [scalars(), inverse_spec(), row_spec(16), field_spec(), tile_spec(40)]
+    halo = struct(25, 8, LANES)
     smoothed, product, tail, head = call(
-        lambda *refs: solve_kernel(True, *refs),
+        lambda *refs: solve_kernel(0, False, *refs),
         "solve_first",
-        [scalars(), field_spec(), tile_spec(32), inverse_spec(), row_spec(16)],
-        *solve_outs,
-        solve_scratch,
+        shared_specs,
+        [field_spec(), whole(8, LANES), whole(25, 8, LANES), whole(25, 8, LANES)],
+        [struct(*FIELD), struct(8, LANES), halo, halo],
+        vmem([((24, 8, LANES), F32), ((16, LANES), F32)]),
         1 << 22,
-        (element_count, residual, came, block_inverse, vertical),
+        (element_count, block_inverse, vertical, residual, came),
     )
     state = came
-    solution = direction = image = norm = None
+    solution = direction = image = flow = scalar_rows = None
     for iteration in range(ITERATIONS):
-        norms = lax.all_to_all(product, ("elem", "lev"), split_axis=0, concat_axis=0, tiled=True)
+        first = iteration == 0
+        last = iteration == ITERATIONS - 1
         before = lax.ppermute(tail, "elem", upward_elem)
         after = lax.ppermute(head, "elem", downward_elem)
         applied = call(
@@ -650,7 +745,7 @@
             [
                 scalars(), scalars(), scalars(), whole(*FIELD), row_spec(48), row_spec(16),
                 pl.BlockSpec((3, NODES, LANES), lambda t: (0, 0, t)), row_spec(16), row_spec(16),
-                row_spec(1), tile_spec(32), whole(2, 256, 128), whole(2, 128, 256),
+                tile_spec(40), tile_spec(state.shape[1]), whole(2, 256, 128), whole(2, 128, 256),
             ],
             field_spec(),
             struct(*FIELD),
@@ -661,49 +756,86 @@
                 vertical, below_row, state, forward, backward,
             ),
         )
-        first = iteration == 0
         args = [
-            far_counts, far_lists, far_totals, applied, smoothed, ints, before, after, norms,
-            block_inverse, vertical,
+            far_counts, far_lists, applied, smoothed, ints, before, after, product, block_inverse,
+            vertical,
         ]
         specs = [
-            scalars(), scalars(), scalars(), field_spec(), field_spec(), row_spec(48),
-            whole(25, 8, LANES), whole(25, 8, LANES), whole(LANES, LANES), inverse_spec(), row_spec(16),
+            scalars(), scalars(), field_spec(), field_spec(), row_spec(48), whole(25, 8, LANES),
+            whole(25, 8, LANES), whole(8, LANES), inverse_spec(), row_spec(16),
         ]
         if not first:
-            args += [norm, direction, image]
-            specs += [whole(8, LANES), field_spec(), field_spec()]
-        direction, image, message, norm = call(
+            args += [direction, image]
+            specs += [field_spec(), field_spec()]
+        applied, message = call(
             lambda *refs, first=first: image_kernel(first, *refs),
             "image_first" if first else "image",
             specs,
-            [field_spec(), field_spec(), whole(8, 40, LANES), whole(8, LANES)],
-            [struct(*FIELD), struct(*FIELD), struct(8, 40, LANES), struct(8, LANES)],
-            vmem([((24, 8, 3 * LANES), F32)] + PICK_SCRATCH + [((16, LANES), F32)]),
+            [field_spec(), whole(8, 40, LANES)],
+            [struct(*FIELD), struct(8, 40, LANES)],
+            vmem(
+                [((24, 8, 3 * LANES), F32)] + PICK_SCRATCH + [((16, LANES), F32), ((16, LANES), F32)]
+            ),
             1 << 22,
             args,
         )
         received = lax.all_to_all(message, "lev", split_axis=0, concat_axis=0, tiled=True)
-        carried, dots = scan_groups(received)
+        carried, dots = pl.pallas_call(
+            scan_kernel,
+            out_shape=[struct(8, 32, LANES), struct(8, LANES)],
+            name="scan",
+            cost_estimate=scan_cost,
+            compiler_params=small,
+        )(received, coupling)
+        dots = sum_over_elem(dots, peers)
+        carried, dots = lax.optimization_barrier((carried, dots))
         came = lax.all_to_all(carried, "lev", split_axis=0, concat_axis=0, tiled=True)
-        dots = lax.all_to_all(dots, "elem", split_axis=0, concat_axis=0, tiled=True)
-        residual, state, step, smoothed, product, tail, head = call(
-            lambda *refs: solve_kernel(False, *refs),
-            "solve",
-            [
-                scalars(), field_spec(), field_spec(), tile_spec(32), tile_spec(32), whole(16, LANES),
-                whole(8, LANES), inverse_spec(), row_spec(16),
-            ],
-            [field_spec(), tile_spec(32), whole(8, LANES)] + solve_outs[0],
-            [struct(*FIELD), struct(8, 32, LANES), struct(8, LANES)] + solve_outs[1],
-            solve_scratch,
+
+        args = [element_count, block_inverse, vertical, residual, came, smoothed, applied, state, dots]
+        specs = shared_specs[:4] + [
+            tile_spec(32), field_spec(), field_spec(), tile_spec(state.shape[1]), whole(8, LANES),
+        ]
+        if not first:
+            args += [solution, direction, image, flow, scalar_rows]
+            specs += [field_spec(), field_spec(), field_spec(), tile_spec(32), whole(8, LANES)]
+        out_specs = [field_spec(), field_spec(), field_spec(), whole(8, LANES)]
+        shapes = [struct(*FIELD), struct(*FIELD), struct(*FIELD), struct(8, LANES)]
+        if last:
+            out_specs += [field_spec(), whole(LANES, LANES)]
+            shapes += [struct(*FIELD), struct(LANES, LANES)]
+            scratch = vmem([((16, LANES), F32)])
+        else:
+            out_specs += [field_spec(), tile_spec(32), tile_spec(32), field_spec(), whole(8, LANES)]
+            out_specs += [whole(25, 8, LANES), whole(25, 8, LANES)]
+            shapes += [struct(*FIELD), struct(8, 32, LANES), struct(8, 32, LANES), struct(*FIELD)]
+            shapes += [struct(8, LANES), halo, halo]
+            scratch = vmem([((24, 8, LANES), F32), ((16, LANES), F32)])
+        results = call(
+            lambda *refs, first=first, last=last: solve_kernel(1 if first else 2, last, *refs),
+            "solve_last" if last else "solve",
+            specs,
+            out_specs,
+            shapes,
+            scratch,
             1 << 22,
-            (element_count, residual, image, came, state, dots, norm, block_inverse, vertical),
+            args,
         )
-        moved = step[0, 0] * direction
-        solution = moved if first else solution + moved
+        if last:
+            solution, residual, direction, scalar_rows, smoothed, product = results
+        else:
+            solution, residual, direction, scalar_rows, image, flow, state = results[:7]
+            smoothed, product, tail, head = results[7:]
     norms = lax.all_to_all(product, ("elem", "lev"), split_axis=0, concat_axis=0, tiled=True)
-    direction = smoothed + jnp.sum(norms) / norm[0, 0] * direction
+    direction = call(
+        finish_kernel,
+        "finish",
+        [whole(LANES, LANES), whole(8, LANES), field_spec(), field_spec()],
+        field_spec(),
+        struct(*FIELD),
+        [],
+        1 << 20,
+        (norms, scalar_rows, smoothed, direction),
+    )
     return (solution, residual, direction)
 
 

time: 369 us -> 248 us (0.67)
  blocking collectives: 147 us -> 75.7 us
  local copies, waits for them, and re-layouts: 48 us -> 10.4 us
  Pallas kernels: 87.8 us -> 62.6 us
  waiting for transfers between devices: 11.4 us -> 28.7 us
  other arithmetic: 12.8 us -> 2.17 us
  starting transfers between devices: 59.2 us -> 65.8 us
    all_to_all x3 -> x1, blocking collectives: 81.8 us -> 13.5 us  [body(): lax.all_to_all(product, ('elem', 'lev'), split_axis=0, concat_axis=0, til...]
    ppermute x1 -> x18, starting transfers between devices: 4.39 us -> 41.2 us  [sum_over_elem(): total = total + lax.ppermute(value, 'elem', pairs)]
    unnamed x99 -> x37, local copies, waits for them, and re-layouts: 42.2 us -> 8.04 us
    all_to_all x4 -> x0, starting transfers between devices: 29.3 us -> none  [body(): lax.all_to_all(product, ('elem', 'lev'), split_axis=0, concat_axis=0, til...]
    ppermute x1 -> x18, waiting for transfers between devices: 0.01 us -> 21.3 us  [sum_over_elem(): total = total + lax.ppermute(value, 'elem', pairs)]
    pallas_call x11 -> x12, Pallas kernels: 81.3 us -> 61.8 us  [call(): pl.pallas_call(kernel, grid=(GROUPS,), in_specs=in_specs, out_specs=out_s...]
    all_to_all x4 -> x0, waiting for transfers between devices: 7.38 us -> none  [body(): lax.all_to_all(product, ('elem', 'lev'), split_axis=0, concat_axis=0, til...]
    pallas_call x4, Pallas kernels: 6.43 us -> 0.8 us  [the longest x1 0.7 us: body(): pl.pallas_call(scan_first_kernel, out_shape=struct(8, 40, LANES), name='s...]
  transfers between devices with their start and end apart: 14 -> 27, of which waited for: 2 -> 15; matrix products, arithmetic and copies ran while one was open for 3% -> 2% of each run, Pallas kernels for 15% -> 13%
where the time goes in v2:
time: 248 us
  blocking collectives  75.7 us (31%)
  starting transfers between devices  65.8 us (27%)
  Pallas kernels  62.6 us (25%)
  waiting for transfers between devices  28.7 us (12%)
  local copies, waits for them, and re-layouts  10.4 us (4%)
    pallas_call x12, Pallas kernels, call(): pl.pallas_call(kernel, grid=(GROUPS,), in_specs=in_specs, out_specs=out_s...  61.8 us
    ppermute x18, starting transfers between devices, sum_over_elem(): total = total + lax.ppermute(value, 'elem', pairs)  41.2 us
    all_to_all x3, blocking collectives, body(): lax.all_to_all(carried, 'lev', split_axis=0, concat_axis=0, tiled=True)  35.1 us
    all_to_all x3, blocking collectives, body(): lax.all_to_all(message, 'lev', split_axis=0, concat_axis=0, tiled=True)  27.1 us
    ppermute x18, waiting for transfers between devices, sum_over_elem(): total = total + lax.ppermute(value, 'elem', pairs)  21.3 us
    all_to_all x1, blocking collectives, body(): lax.all_to_all(product, ('elem', 'lev'), split_axis=0, concat_axis=0, til...  13.5 us
    unnamed x37, local copies, waits for them, and re-layouts  8.04 us
    all_to_all x1, starting transfers between devices, body(): lax.all_to_all(message, 'lev', split_axis=0, concat_axis=0, tiled=True)  6.4 us
  transfers between devices with their start and end apart: 27, of which 15 were waited for; matrix products, arithmetic and copies ran while one was open for 2% of the time, Pallas kernels for 13%

profile of v2, /device:TPU:1, one launch (start us, length us, event | category | flops | bytes accessed | tf_op | source)
XLA Modules:
  0.0 247.6 jit_solution(14665018461606358247)
XLA Ops:
  0.6 4.5 %collective-permute-start = (s32[1]{0:T(128)}, s32[1]{0:T(128)}, u32[]{:S(2)}, u32[]{:S(2)}) collective-permute-start(s32[1]{0:T(128)} %param.20), channel_id=1, source_target_pairs={{0,8},{8,16},{16,24},{24,32},{32,40},{40,48},{48,56},{56,64},{64,7... | collective-permute-start | bytes 20 | tf_op jit(solution)/shard_map/ppermute | solution.py:715
  11.8 6.4 %all-to-all-start = ((f32[8,40,128]{2,1,0:T(8,128)}), f32[8,40,128]{2,1,0:T(8,128)S(1)}, u32[]{:S(2)}, u32[]{:S(2)}) async-start(f32[8,40,128]{2,1,0:T(8,128)} %get-tuple-element.56), calls=%async_computation | async-start | bytes 327680 | tf_op jit(solution)/shard_map/all_to_all | solution.py:702
  24.4 4.3 %all-to-all-start.1 = ((f32[8,40,128]{2,1,0:T(8,128)}), f32[8,40,128]{2,1,0:T(8,128)S(1)}, u32[]{:S(2)}, u32[]{:S(2)}) async-start(f32[8,40,128]{2,1,0:T(8,128)} %scan_first.1), calls=%async_computation.1 | async-start | bytes 327680 | tf_op jit(solution)/shard_map/all_to_all | solution.py:712
  29.0 5.4 %all-to-all-done.1.refs_4_.below_row.state.refs_7_ = f32[8,40,128]{2,1,0:T(8,128)S(1)} async-done(((f32[8,40,128]{2,1,0:T(8,128)}), f32[8,40,128]{2,1,0:T(8,128)S(1)}, u32[]{:S(2)}, u32[]{:S(2)}) %all-to-all-start.1) | async-done | bytes 163872 | tf_op jit(solution)/shard_map/all_to_all | solution.py:712
  47.4 9.8 %operate.3.refs_2_ = f32[16,16,1024]{2,1,0:T(8,128)S(1)} custom-call(f32[16]{0:T(128)S(1)} %copy-done.9, s32[8]{0:T(128)S(1)} %convert_reduce_fusion.2.counts, s32[64]{0:T(128)S(1)} %reshape.164.lists, f32[16,16,1024]{2,1,0:T(8,128)S(1)} %get-tuple-element.57.field.refs_3_.refs_5_, s32[48,1024]{1,0:T(8,128)S(1)} %concatenate.23.ints.refs_4_, ...), custom_call_target="tpu_custom_call" | custom-call | flops 1073741824 | bytes 6291456 | tf_op jit(solution)/shard_map/operate/pallas_call | solution.py:582
  60.1 9.2 %all_to_all.51.received = f32[8,40,128]{2,1,0:T(8,128)S(1)} all-to-all(f32[8,40,128]{2,1,0:T(8,128)S(1)} %get-tuple-element.61), channel_id=1, replica_groups=mesh['elem'=16,'lev'=8] {'lev'}, dimensions={0} | all-to-all | bytes 327680 | tf_op jit(solution)/shard_map/all_to_all | solution.py:782
  69.3 5.9 %collective-permute-start.5 = (f32[8,128]{1,0:T(8,128)S(1)}, f32[8,128]{1,0:T(8,128)S(1)}, u32[]{:S(2)}, u32[]{:S(2)}) collective-permute-start(f32[8,128]{1,0:T(8,128)S(1)} %get-tuple-element.63), channel_id=1, source_target_pairs={{0,24},{8,0},{16,8},{24,16},{32,56},{40,32},{48,40},{56,48},{64,88... | collective-permute-start | bytes 12296 | tf_op jit(solution)/shard_map/ppermute | solution.py:633
  75.2 5.1 %collective-permute-start.4 = (f32[8,128]{1,0:T(8,128)S(1)}, f32[8,128]{1,0:T(8,128)S(1)}, u32[]{:S(2)}, u32[]{:S(2)}) collective-permute-start(f32[8,128]{1,0:T(8,128)S(1)} %get-tuple-element.63), channel_id=1, source_target_pairs={{0,16},{8,24},{16,0},{24,8},{32,48},{40,56},{48,32},{56,40},{64,80... | collective-permute-start | bytes 12296 | tf_op jit(solution)/shard_map/ppermute | solution.py:633
  90.4 11.7 %all_to_all.52.refs_4_ = f32[8,32,128]{2,1,0:T(8,128)S(1)} all-to-all(f32[8,32,128]{2,1,0:T(8,128)S(1)} %get-tuple-element.64), channel_id=1, replica_groups=mesh['elem'=16,'lev'=8] {'lev'}, dimensions={0} | all-to-all | bytes 262144 | tf_op jit(solution)/shard_map/all_to_all | solution.py:792
  102.2 3.8 %solve.2 = (f32[16,16,1024]{2,1,0:T(8,128)S(1)}, f32[16,16,1024]{2,1,0:T(8,128)S(1)}, f32[16,16,1024]{2,1,0:T(8,128)S(1)}, f32[8,128]{1,0:T(8,128)S(1)}, f32[16,...) custom-call(s32[1]{0:T(128)S(6)} %copy.27.count.refs_0_, ...), custom_call_target="tpu_custom_call" | custom-call | flops 4194304 | bytes 6291456 | tf_op jit(solution)/shard_map/solve/pallas_call | solution.py:582
  108.6 9.8 %operate.4.refs_2_ = f32[16,16,1024]{2,1,0:T(8,128)S(1)} custom-call(f32[16]{0:T(128)S(1)} %copy-done.9, s32[8]{0:T(128)S(1)} %convert_reduce_fusion.2.counts, s32[64]{0:T(128)S(1)} %reshape.164.lists, f32[16,16,1024]{2,1,0:T(8,128)S(1)} %get-tuple-element.68.field.refs_3_.refs_5_, s32[48,1024]{1,0:T(8,128)S(1)} %concatenate.23.ints.refs_4_, ...), custom_call_target="tpu_custom_call" | custom-call | flops 1073741824 | bytes 6291456 | tf_op jit(solution)/shard_map/operate/pallas_call | solution.py:582
  121.8 8.9 %all_to_all.53.received = f32[8,40,128]{2,1,0:T(8,128)S(1)} all-to-all(f32[8,40,128]{2,1,0:T(8,128)S(1)} %get-tuple-element.75), channel_id=1, replica_groups=mesh['elem'=16,'lev'=8] {'lev'}, dimensions={0} | all-to-all | bytes 327680 | tf_op jit(solution)/shard_map/all_to_all | solution.py:782
  130.8 5.8 %collective-permute-start.13 = (f32[8,128]{1,0:T(8,128)S(1)}, f32[8,128]{1,0:T(8,128)S(1)}, u32[]{:S(2)}, u32[]{:S(2)}) collective-permute-start(f32[8,128]{1,0:T(8,128)S(1)} %get-tuple-element.77), channel_id=1, source_target_pairs={{0,24},{8,0},{16,8},{24,16},{32,56},{40,32},{48,40},{56,48},{64,88... | collective-permute-start | bytes 12296 | tf_op jit(solution)/shard_map/ppermute | solution.py:633
  136.6 5.5 %collective-permute-start.12 = (f32[8,128]{1,0:T(8,128)S(1)}, f32[8,128]{1,0:T(8,128)S(1)}, u32[]{:S(2)}, u32[]{:S(2)}) collective-permute-start(f32[8,128]{1,0:T(8,128)S(1)} %get-tuple-element.77), channel_id=1, source_target_pairs={{0,16},{8,24},{16,0},{24,8},{32,48},{40,56},{48,32},{56,40},{64,80... | collective-permute-start | bytes 12296 | tf_op jit(solution)/shard_map/ppermute | solution.py:633
  152.4 11.7 %all_to_all.54.refs_4_ = f32[8,32,128]{2,1,0:T(8,128)S(1)} all-to-all(f32[8,32,128]{2,1,0:T(8,128)S(1)} %get-tuple-element.78), channel_id=1, replica_groups=mesh['elem'=16,'lev'=8] {'lev'}, dimensions={0} | all-to-all | bytes 262144 | tf_op jit(solution)/shard_map/all_to_all | solution.py:792
  164.1 4.8 %solve.3 = (f32[16,16,1024]{2,1,0:T(8,128)S(1)}, f32[16,16,1024]{2,1,0:T(8,128)S(1)}, f32[16,16,1024]{2,1,0:T(8,128)S(1)}, f32[8,128]{1,0:T(8,128)S(1)}, f32[16,...) custom-call(s32[1]{0:T(128)S(6)} %copy.27.count.refs_0_, ...), custom_call_target="tpu_custom_call" | custom-call | flops 4194304 | bytes 6291456 | tf_op jit(solution)/shard_map/solve/pallas_call | solution.py:582
  171.7 9.8 %operate.5.refs_2_ = f32[16,16,1024]{2,1,0:T(8,128)S(1)} custom-call(f32[16]{0:T(128)S(1)} %copy-done.9, s32[8]{0:T(128)S(1)} %convert_reduce_fusion.2.counts, s32[64]{0:T(128)S(1)} %reshape.164.lists, f32[16,16,1024]{2,1,0:T(8,128)S(1)} %get-tuple-element.85.field.refs_3_.refs_5_, s32[48,1024]{1,0:T(8,128)S(1)} %concatenate.23.ints.refs_4_, ...), custom_call_target="tpu_custom_call" | custom-call | flops 1073741824 | bytes 6291456 | tf_op jit(solution)/shard_map/operate/pallas_call | solution.py:582
  185.0 9.1 %all_to_all.55.received = f32[8,40,128]{2,1,0:T(8,128)S(1)} all-to-all(f32[8,40,128]{2,1,0:T(8,128)S(1)} %get-tuple-element.92), channel_id=1, replica_groups=mesh['elem'=16,'lev'=8] {'lev'}, dimensions={0} | all-to-all | bytes 327680 | tf_op jit(solution)/shard_map/all_to_all | solution.py:782
  194.1 5.8 %collective-permute-start.21 = (f32[8,128]{1,0:T(8,128)S(1)}, f32[8,128]{1,0:T(8,128)S(1)}, u32[]{:S(2)}, u32[]{:S(2)}) collective-permute-start(f32[8,128]{1,0:T(8,128)S(1)} %get-tuple-element.94), channel_id=1, source_target_pairs={{0,24},{8,0},{16,8},{24,16},{32,56},{40,32},{48,40},{56,48},{64,88... | collective-permute-start | bytes 12296 | tf_op jit(solution)/shard_map/ppermute | solution.py:633
  199.9 5.5 %collective-permute-start.20 = (f32[8,128]{1,0:T(8,128)S(1)}, f32[8,128]{1,0:T(8,128)S(1)}, u32[]{:S(2)}, u32[]{:S(2)}) collective-permute-start(f32[8,128]{1,0:T(8,128)S(1)} %get-tuple-element.94), channel_id=1, source_target_pairs={{0,16},{8,24},{16,0},{24,8},{32,48},{40,56},{48,32},{56,40},{64,80... | collective-permute-start | bytes 12296 | tf_op jit(solution)/shard_map/ppermute | solution.py:633
  213.9 11.7 %all_to_all.56.refs_4_ = f32[8,32,128]{2,1,0:T(8,128)S(1)} all-to-all(f32[8,32,128]{2,1,0:T(8,128)S(1)} %get-tuple-element.95), channel_id=1, replica_groups=mesh['elem'=16,'lev'=8] {'lev'}, dimensions={0} | all-to-all | bytes 262144 | tf_op jit(solution)/shard_map/all_to_all | solution.py:792
  225.6 5.0 %solve_last.1 = (f32[16,16,1024]{2,1,0:T(8,128)}, f32[16,16,1024]{2,1,0:T(8,128)}, f32[16,16,1024]{2,1,0:T(8,128)S(1)}, f32[8,128]{1,0:T(8,128)S(1)}, f32[16,16,...) custom-call(s32[1]{0:T(128)S(6)} %copy.27.count.refs_0_, f32[2,8,8,1024]{3,2,1,0:T(8,128)S(1)} %copy-done.1, ...), custom_call_target="tpu_custom_call" | custom-call | flops 4194304 | bytes 6291456 | tf_op jit(solution)/shard_map/solve_last/pallas_call | solution.py:582
  230.5 13.5 %all_to_all.57 = f32[128,1,128]{2,1,0:T(1,128)S(1)} all-to-all(f32[128,1,128]{2,1,0:T(1,128)S(1)} %bitcast.15), channel_id=1, replica_groups=mesh['elem'=16,'lev'=8] {'elem','lev'}, dimensions={0} | all-to-all | bytes 131072 | tf_op jit(solution)/shard_map/all_to_all | solution.py:828
  244.1 3.6 %finish.1 = f32[16,16,1024]{2,1,0:T(8,128)} custom-call(f32[128,128]{1,0:T(8,128)S(1)} %bitcast.14, f32[8,128]{1,0:T(8,128)S(1)} %get-tuple-element.104.scalars_in, f32[16,16,1024]{2,1,0:T(8,128)S(1)} %get-tuple-element.105.smoothed, f32[16,16,1024]{2,1,0:T(8,128)S(1)} %get-tuple-element.106.direction_in), custom_call_target="tpu_custom_call" | custom-call | flops 1048576 | bytes 6291456 | tf_op jit(solution)/shard_map/finish/pallas_call | solution.py:582
  (129 shorter events, 68.8 us)
Async XLA Ops:
  0.6 18.7 %collective-permute-start = (s32[1]{0:T(128)}, s32[1]{0:T(128)}, u32[]{:S(2)}, u32[]{:S(2)}) collective-permute-start(s32[1]{0:T(128)} %param.20), channel_id=1, source_target_pairs={{0,8},{8,16},{16,24},{24,32},{32,40},{40,48},{48,56},{56,64},{64,7... | collective-permute-start | bytes 20 | tf_op jit(solution)/shard_map/ppermute | solution.py:715
  11.8 12.0 %all-to-all-start = ((f32[8,40,128]{2,1,0:T(8,128)}), f32[8,40,128]{2,1,0:T(8,128)S(1)}, u32[]{:S(2)}, u32[]{:S(2)}) async-start(f32[8,40,128]{2,1,0:T(8,128)} %get-tuple-element.56), calls=%async_computation | async-start | bytes 327680 | tf_op jit(solution)/shard_map/all_to_all | solution.py:702
  24.4 9.9 %all-to-all-start.1 = ((f32[8,40,128]{2,1,0:T(8,128)}), f32[8,40,128]{2,1,0:T(8,128)S(1)}, u32[]{:S(2)}, u32[]{:S(2)}) async-start(f32[8,40,128]{2,1,0:T(8,128)} %scan_first.1), calls=%async_computation.1 | async-start | bytes 327680 | tf_op jit(solution)/shard_map/all_to_all | solution.py:712
  37.0 20.2 %collective-permute-start.1 = (f32[25,8,128]{2,1,0:T(8,128)}, f32[25,8,128]{2,1,0:T(8,128)S(1)}, u32[]{:S(2)}, u32[]{:S(2)}) collective-permute-start(f32[25,8,128]{2,1,0:T(8,128)} %get-tuple-element.58), channel_id=1, source_target_pairs={{0,8},{8,16},{16,24},{24,32},{32,40},{40,48},{48,56},{56,64},{64,7... | collective-permute-start | bytes 307208 | tf_op jit(solution)/shard_map/ppermute | solution.py:740
  39.7 17.5 %collective-permute-start.2 = (f32[25,8,128]{2,1,0:T(8,128)}, f32[25,8,128]{2,1,0:T(8,128)S(1)}, u32[]{:S(2)}, u32[]{:S(2)}) collective-permute-start(f32[25,8,128]{2,1,0:T(8,128)} %get-tuple-element.59), channel_id=1, source_target_pairs={{8,0},{16,8},{24,16},{32,24},{40,32},{48,40},{56,48},{64,56},{72,6... | collective-permute-start | bytes 307208 | tf_op jit(solution)/shard_map/ppermute | solution.py:741
  69.3 11.0 %collective-permute-start.5 = (f32[8,128]{1,0:T(8,128)S(1)}, f32[8,128]{1,0:T(8,128)S(1)}, u32[]{:S(2)}, u32[]{:S(2)}) collective-permute-start(f32[8,128]{1,0:T(8,128)S(1)} %get-tuple-element.63), channel_id=1, source_target_pairs={{0,24},{8,0},{16,8},{24,16},{32,56},{40,32},{48,40},{56,48},{64,88... | collective-permute-start | bytes 12296 | tf_op jit(solution)/shard_map/ppermute | solution.py:633
  75.2 6.1 %collective-permute-start.4 = (f32[8,128]{1,0:T(8,128)S(1)}, f32[8,128]{1,0:T(8,128)S(1)}, u32[]{:S(2)}, u32[]{:S(2)}) collective-permute-start(f32[8,128]{1,0:T(8,128)S(1)} %get-tuple-element.63), channel_id=1, source_target_pairs={{0,16},{8,24},{16,0},{24,8},{32,48},{40,56},{48,32},{56,40},{64,80... | collective-permute-start | bytes 12296 | tf_op jit(solution)/shard_map/ppermute | solution.py:633
  80.3 3.7 %collective-permute-start.3 = (f32[8,128]{1,0:T(8,128)S(1)}, f32[8,128]{1,0:T(8,128)S(1)}, u32[]{:S(2)}, u32[]{:S(2)}) collective-permute-start(f32[8,128]{1,0:T(8,128)S(1)} %get-tuple-element.63), channel_id=1, source_target_pairs={{0,8},{8,16},{16,24},{24,0},{32,40},{40,48},{48,56},{56,32},{64,72... | collective-permute-start | bytes 12296 | tf_op jit(solution)/shard_map/ppermute | solution.py:633
  86.5 4.0 %collective-permute-start.7 = (f32[8,128]{1,0:T(8,128)S(1)}, f32[8,128]{1,0:T(8,128)S(1)}, u32[]{:S(2)}, u32[]{:S(2)}) collective-permute-start(f32[8,128]{1,0:T(8,128)S(1)} %add_add_fusion.5), channel_id=1, source_target_pairs={{0,64},{8,72},{16,80},{24,88},{32,96},{40,104},{48,112},{56,120},{... | collective-permute-start | bytes 12296 | tf_op jit(solution)/shard_map/ppermute | solution.py:633
  86.6 3.9 %collective-permute-start.6 = (f32[8,128]{1,0:T(8,128)S(1)}, f32[8,128]{1,0:T(8,128)S(1)}, u32[]{:S(2)}, u32[]{:S(2)}) collective-permute-start(f32[8,128]{1,0:T(8,128)S(1)} %add_add_fusion.5), channel_id=1, source_target_pairs={{0,32},{8,40},{16,48},{24,56},{32,64},{40,72},{48,80},{56,88},{64,... | collective-permute-start | bytes 12296 | tf_op jit(solution)/shard_map/ppermute | solution.py:633
  106.0 12.5 %collective-permute-start.9 = (f32[25,8,128]{2,1,0:T(8,128)S(1)}, f32[25,8,128]{2,1,0:T(8,128)S(1)}, u32[]{:S(2)}, u32[]{:S(2)}) collective-permute-start(f32[25,8,128]{2,1,0:T(8,128)S(1)} %get-tuple-element.70), channel_id=1, source_target_pairs={{0,8},{8,16},{16,24},{24,32},{32,40},{40,48},{48,56},{56,64},{64,7... | collective-permute-start | bytes 307208 | tf_op jit(solution)/shard_map/ppermute | solution.py:740
  107.3 11.2 %collective-permute-start.10 = (f32[25,8,128]{2,1,0:T(8,128)S(1)}, f32[25,8,128]{2,1,0:T(8,128)S(1)}, u32[]{:S(2)}, u32[]{:S(2)}) collective-permute-start(f32[25,8,128]{2,1,0:T(8,128)S(1)} %get-tuple-element.71), channel_id=1, source_target_pairs={{8,0},{16,8},{24,16},{32,24},{40,32},{48,40},{56,48},{64,56},{72,6... | collective-permute-start | bytes 307208 | tf_op jit(solution)/shard_map/ppermute | solution.py:741
  130.8 11.3 %collective-permute-start.13 = (f32[8,128]{1,0:T(8,128)S(1)}, f32[8,128]{1,0:T(8,128)S(1)}, u32[]{:S(2)}, u32[]{:S(2)}) collective-permute-start(f32[8,128]{1,0:T(8,128)S(1)} %get-tuple-element.77), channel_id=1, source_target_pairs={{0,24},{8,0},{16,8},{24,16},{32,56},{40,32},{48,40},{56,48},{64,88... | collective-permute-start | bytes 12296 | tf_op jit(solution)/shard_map/ppermute | solution.py:633
  136.6 6.5 %collective-permute-start.12 = (f32[8,128]{1,0:T(8,128)S(1)}, f32[8,128]{1,0:T(8,128)S(1)}, u32[]{:S(2)}, u32[]{:S(2)}) collective-permute-start(f32[8,128]{1,0:T(8,128)S(1)} %get-tuple-element.77), channel_id=1, source_target_pairs={{0,16},{8,24},{16,0},{24,8},{32,48},{40,56},{48,32},{56,40},{64,80... | collective-permute-start | bytes 12296 | tf_op jit(solution)/shard_map/ppermute | solution.py:633
  142.0 3.7 %collective-permute-start.11 = (f32[8,128]{1,0:T(8,128)S(1)}, f32[8,128]{1,0:T(8,128)S(1)}, u32[]{:S(2)}, u32[]{:S(2)}) collective-permute-start(f32[8,128]{1,0:T(8,128)S(1)} %get-tuple-element.77), channel_id=1, source_target_pairs={{0,8},{8,16},{16,24},{24,0},{32,40},{40,48},{48,56},{56,32},{64,72... | collective-permute-start | bytes 12296 | tf_op jit(solution)/shard_map/ppermute | solution.py:633
  146.3 4.0 %collective-permute-start.15 = (f32[8,128]{1,0:T(8,128)S(1)}, f32[8,128]{1,0:T(8,128)S(1)}, u32[]{:S(2)}, u32[]{:S(2)}) collective-permute-start(f32[8,128]{1,0:T(8,128)S(1)} %add_add_fusion.3), channel_id=1, source_target_pairs={{0,64},{8,72},{16,80},{24,88},{32,96},{40,104},{48,112},{56,120},{... | collective-permute-start | bytes 12296 | tf_op jit(solution)/shard_map/ppermute | solution.py:633
  148.7 3.7 %collective-permute-start.14 = (f32[8,128]{1,0:T(8,128)S(1)}, f32[8,128]{1,0:T(8,128)S(1)}, u32[]{:S(2)}, u32[]{:S(2)}) collective-permute-start(f32[8,128]{1,0:T(8,128)S(1)} %add_add_fusion.3), channel_id=1, source_target_pairs={{0,32},{8,40},{16,48},{24,56},{32,64},{40,72},{48,80},{56,88},{64,... | collective-permute-start | bytes 12296 | tf_op jit(solution)/shard_map/ppermute | solution.py:633
  168.9 12.6 %collective-permute-start.17 = (f32[25,8,128]{2,1,0:T(8,128)S(1)}, f32[25,8,128]{2,1,0:T(8,128)S(1)}, u32[]{:S(2)}, u32[]{:S(2)}) collective-permute-start(f32[25,8,128]{2,1,0:T(8,128)S(1)} %get-tuple-element.87), channel_id=1, source_target_pairs={{0,8},{8,16},{16,24},{24,32},{32,40},{40,48},{48,56},{56,64},{64,7... | collective-permute-start | bytes 307208 | tf_op jit(solution)/shard_map/ppermute | solution.py:740
  170.3 11.3 %collective-permute-start.18 = (f32[25,8,128]{2,1,0:T(8,128)S(1)}, f32[25,8,128]{2,1,0:T(8,128)S(1)}, u32[]{:S(2)}, u32[]{:S(2)}) collective-permute-start(f32[25,8,128]{2,1,0:T(8,128)S(1)} %get-tuple-element.88), channel_id=1, source_target_pairs={{8,0},{16,8},{24,16},{32,24},{40,32},{48,40},{56,48},{64,56},{72,6... | collective-permute-start | bytes 307208 | tf_op jit(solution)/shard_map/ppermute | solution.py:741
  194.1 11.3 %collective-permute-start.21 = (f32[8,128]{1,0:T(8,128)S(1)}, f32[8,128]{1,0:T(8,128)S(1)}, u32[]{:S(2)}, u32[]{:S(2)}) collective-permute-start(f32[8,128]{1,0:T(8,128)S(1)} %get-tuple-element.94), channel_id=1, source_target_pairs={{0,24},{8,0},{16,8},{24,16},{32,56},{40,32},{48,40},{56,48},{64,88... | collective-permute-start | bytes 12296 | tf_op jit(solution)/shard_map/ppermute | solution.py:633
  199.9 6.5 %collective-permute-start.20 = (f32[8,128]{1,0:T(8,128)S(1)}, f32[8,128]{1,0:T(8,128)S(1)}, u32[]{:S(2)}, u32[]{:S(2)}) collective-permute-start(f32[8,128]{1,0:T(8,128)S(1)} %get-tuple-element.94), channel_id=1, source_target_pairs={{0,16},{8,24},{16,0},{24,8},{32,48},{40,56},{48,32},{56,40},{64,80... | collective-permute-start | bytes 12296 | tf_op jit(solution)/shard_map/ppermute | solution.py:633
  205.4 3.7 %collective-permute-start.19 = (f32[8,128]{1,0:T(8,128)S(1)}, f32[8,128]{1,0:T(8,128)S(1)}, u32[]{:S(2)}, u32[]{:S(2)}) collective-permute-start(f32[8,128]{1,0:T(8,128)S(1)} %get-tuple-element.94), channel_id=1, source_target_pairs={{0,8},{8,16},{16,24},{24,0},{32,40},{40,48},{48,56},{56,32},{64,72... | collective-permute-start | bytes 12296 | tf_op jit(solution)/shard_map/ppermute | solution.py:633
  209.1 4.0 %collective-permute-start.23 = (f32[8,128]{1,0:T(8,128)S(1)}, f32[8,128]{1,0:T(8,128)S(1)}, u32[]{:S(2)}, u32[]{:S(2)}) collective-permute-start(f32[8,128]{1,0:T(8,128)S(1)} %add_add_fusion.1), channel_id=1, source_target_pairs={{0,64},{8,72},{16,80},{24,88},{32,96},{40,104},{48,112},{56,120},{... | collective-permute-start | bytes 12296 | tf_op jit(solution)/shard_map/ppermute | solution.py:633
  210.2 3.7 %collective-permute-start.22 = (f32[8,128]{1,0:T(8,128)S(1)}, f32[8,128]{1,0:T(8,128)S(1)}, u32[]{:S(2)}, u32[]{:S(2)}) collective-permute-start(f32[8,128]{1,0:T(8,128)S(1)} %add_add_fusion.1), channel_id=1, source_target_pairs={{0,32},{8,40},{16,48},{24,56},{32,64},{40,72},{48,80},{56,88},{64,... | collective-permute-start | bytes 12296 | tf_op jit(solution)/shard_map/ppermute | solution.py:633
  (21 other events, 74.7 us)

commit v3 on v2

--- a/solution.py
+++ b/solution.py
@@ -17,6 +17,7 @@
 GROUPS = 8
 PENALTY = 2.0
 ABSENT = 15 * LANES
+PLAN = 13
 VMEM_BYTES = 12 * 1024 * 1024
 SMALL_VMEM_BYTES = 4 * 1024 * 1024
 F32 = jnp.float32
@@ -41,10 +42,12 @@
 def stacked_tables():
     along_x, along_y = gradient_table()
     table = np.concatenate([np.kron(np.eye(8), along_x), np.kron(np.eye(8), along_y)], axis=0)
-    table = jnp.asarray(table, F32)
-    high = table.astype(BF16)
-    low = (table - high.astype(F32)).astype(BF16)
-    return jnp.stack([high, low]), jnp.stack([high.T, low.T])
+    both = np.zeros((384, 256))
+    both[:256, :128] = table
+    both[256:] = table.T
+    both = jnp.asarray(both, F32)
+    high = both.astype(BF16)
+    return jnp.stack([high, (both - high.astype(F32)).astype(BF16)])
 
 
 def lane_take(values, index):
@@ -93,13 +96,13 @@
         put(LEVELS + pair, corner_table(even[:8], even[8:], odd[:8], odd[8:], rows))
 
 
-def gather_pick(table, first_tile, ints, counts, lists, per_list, tile, edges, corners, pick):
+def gather_pick(table, first_tile, ints, plan, far, tile, edges, corners, pick):
     rows, lanes = iotas()
     edges[...] = jnp.zeros(edges.shape, F32)
     corners[...] = jnp.zeros(corners.shape, F32)
 
     def step(turn, unused):
-        which = lists[tile * per_list + turn]
+        which = plan[tile * PLAN + (10 if far else 2) + turn]
         column = pl.multiple_of((which - first_tile) * LANES, LANES)
         values = [table[member, :, pl.ds(column, LANES)] for member in range(LEVELS + 8)]
         for side in range(4):
@@ -128,7 +131,7 @@
                 corners[corner, place] = sums[place]
         return unused
 
-    lax.fori_loop(0, counts[tile], step, 0)
+    lax.fori_loop(0, plan[tile * PLAN + (1 if far else 0)], step, 0)
     low_index = ints[16:24, :]
     high_index = ints[24:32, :]
     next_row = jnp.bitwise_and(rows, 4) + jnp.bitwise_and(rows + 1, 3)
@@ -228,34 +231,103 @@
     message[0, 36:40, :] = jnp.zeros((4, LANES), F32)
 
 
-def scan_groups(received, coupling, carried):
-    value = jnp.zeros((16, LANES), F32)
-    for group in range(GROUPS):
-        carried[group, 0:16, :] = value
-        value = coupling[group, 32:33, :] * value + received[group, 0:16, :]
-    value = jnp.zeros((16, LANES), F32)
-    for group in reversed(range(GROUPS)):
-        carried[group, 16:32, :] = value
-        value = (
-            received[group, 16:32, :]
-            + coupling[group, 33:34, :] * carried[group, 0:16, :]
-            + coupling[group, 34:35, :] * value
-        )
-
-
-def scan_first_kernel(received, carried):
-    scan_groups(received, received, carried)
-    for group in range(GROUPS):
-        below = received[group - 1, 35:36, :] if group else jnp.zeros((1, LANES), F32)
-        carried[group, 32:40, :] = jnp.broadcast_to(below, (8, LANES))
-
-
-def scan_kernel(received, coupling, carried, dots):
-    scan_groups(received, coupling, carried)
-    total = received[0, 32:40, :]
-    for group in range(1, GROUPS):
-        total = total + received[group, 32:40, :]
-    dots[...] = total
+def joined(first, last, *refs):
+    refs = list(refs)
+    flags, seg, got, inner = refs[:4]
+    del refs[:4]
+    if first:
+        aux = refs.pop(0)
+    else:
+        terms = refs.pop(0)
+    if last:
+        own = refs.pop(0)
+        if not first:
+            ends = refs.pop(0)
+        carried = refs.pop(0)
+    else:
+        seg_out, inner_out = refs.pop(0), refs.pop(0)
+    if first:
+        terms, aux_out = refs.pop(0), refs.pop(0)
+        if last:
+            ends = refs.pop(0)
+
+    def row(ref, tile, index):
+        return ref[tile, index : index + 1, :]
+
+    def finish(tile, below, above_up, above_down):
+        if last:
+            leaving = row(ends, tile, 1) * below + own[tile, 0:16, :]
+            carried[tile, 0:16, :] = below
+            carried[tile, 16:32, :] = above_down + row(ends, tile, 0) * leaving
+        else:
+            inner_out[tile, 0:16, :] = below
+            inner_out[tile, 16:32, :] = above_up
+            inner_out[tile, 32:48, :] = above_down
+
+    def prepare(tile, partner_below):
+        for index in range(3):
+            terms[tile, index : index + 1, :] = row(got, tile, 32 + index)
+            terms[tile, 3 + index : 4 + index, :] = row(seg, tile, 32 + index)
+        terms[tile, 6:7, :] = row(aux, tile, 0)
+        terms[tile, 7:8, :] = row(aux, tile, 3)
+        up_p, both_p, down_p, up, both, down = [row(terms, tile, index) for index in range(6)]
+        below, above, through, back, flow = [row(aux, tile, index) for index in range(5)]
+        if partner_below:
+            bottom = jnp.broadcast_to(flags[1], flow.shape)
+            flow = jnp.where(bottom == 1, row(got, tile, 35), flow)
+            below = below * up_p
+            joint = (up * up_p, both_p + down_p * both * up_p, down_p * down, row(seg, tile, 35))
+        else:
+            through = through + back * both_p * above
+            above = up_p * above
+            back = back * down_p
+            joint = (up_p * up, both + down * both_p * up, down * down_p, row(got, tile, 35))
+        for index, value in enumerate((below, above, through, back, flow)):
+            aux_out[tile, index : index + 1, :] = value
+        aux_out[tile, 5:8, :] = jnp.zeros((3, LANES), F32)
+        if last:
+            ends[tile, 0:1, :] = through
+            ends[tile, 1:2, :] = row(own, tile, 32)
+            ends[tile, 2:8, :] = jnp.zeros((6, LANES), F32)
+        else:
+            for index, value in enumerate(joint):
+                seg_out[tile, 32 + index : 33 + index, :] = value
+            seg_out[tile, 36:40, :] = jnp.zeros((4, LANES), F32)
+
+    @pl.when(flags[0] == 1)
+    def partner_below():
+        for tile in range(GROUPS):
+            if first:
+                prepare(tile, True)
+            came_up, came_down = got[tile, 0:16, :], got[tile, 16:32, :]
+            if not last:
+                upward, downward = seg[tile, 0:16, :], seg[tile, 16:32, :]
+                seg_out[tile, 0:16, :] = row(terms, tile, 3) * came_up + upward
+                seg_out[tile, 16:32, :] = came_down + row(terms, tile, 2) * (
+                    downward + row(terms, tile, 4) * came_up
+                )
+            below = row(terms, tile, 6) * came_up + inner[tile, 0:16, :]
+            finish(tile, below, inner[tile, 16:32, :], inner[tile, 32:48, :])
+
+    @pl.when(flags[0] != 1)
+    def partner_above():
+        for tile in range(GROUPS):
+            if first:
+                prepare(tile, False)
+            came_up, came_down = got[tile, 0:16, :], got[tile, 16:32, :]
+            if not last:
+                upward, downward = seg[tile, 0:16, :], seg[tile, 16:32, :]
+                seg_out[tile, 0:16, :] = row(terms, tile, 0) * upward + came_up
+                seg_out[tile, 16:32, :] = downward + row(terms, tile, 5) * (
+                    came_down + row(terms, tile, 1) * upward
+                )
+            above_up, above_down = inner[tile, 16:32, :], inner[tile, 32:48, :]
+            finish(
+                tile,
+                inner[tile, 0:16, :],
+                row(terms, tile, 0) * above_up + came_up,
+                above_down + row(terms, tile, 7) * (came_down + row(terms, tile, 1) * above_up),
+            )
 
 
 def solve_kernel(stage, last, *refs):
@@ -268,7 +340,8 @@
 
     count, inverse, vertical, residual_in, came = take(5)
     if stage:
-        smoothed_in, applied, state_in, dots = take(4)
+        smoothed_in, applied, state_in = take(3)
+        dot_parts = take(2)
     if stage == 2:
         solution_in, direction_in, image_in, flow_in, scalars_in = take(5)
     if stage:
@@ -279,12 +352,13 @@
         residual, state = residual_in, came
     smoothed, product = take(2)
     if not last:
-        tail, head, tables = take(3)
+        near, far, tables = take(3)
     (parts,) = take(1)
     tile = pl.program_id(0)
     rows, lanes = iotas()
 
     if stage:
+        dots = dot_parts[0][...] + dot_parts[1][...]
         norm = jnp.sum(dots[0:1, :], axis=1, keepdims=True)
         curvature = jnp.sum(dots[1:2, :], axis=1, keepdims=True)
         if stage == 2:
@@ -357,11 +431,6 @@
     if last:
         return
 
-    @pl.when(tile == 0)
-    def clear_tail():
-        tail[...] = jnp.zeros((25, 8, LANES), F32)
-        head[...] = jnp.zeros((25, 8, LANES), F32)
-
     start = count[0] - LANES
     start_tile = lax.shift_right_logical(start, 7)
     offset = jnp.bitwise_and(start, LANES - 1)
@@ -378,35 +447,47 @@
     def build():
         store_tables(lambda level: smoothed[level], rows, put)
 
-    @pl.when(in_tail)
-    def fill_tail():
-        index = jnp.bitwise_and(lanes + offset, LANES - 1)
-        before_wrap = (lanes < LANES - offset).astype(jnp.int32)
-        wanted = before_wrap == (tile == start_tile).astype(jnp.int32)
-        for position in range(24):
-            tail[position] = jnp.where(wanted, lane_take(tables[position], index), tail[position])
-
-    @pl.when(in_extra)
-    def fill_extra():
-        index = jnp.zeros_like(lanes) + extra_lane
-        packed = jnp.zeros((8, LANES), F32)
-        for position in range(24):
-            packed = jnp.where(lanes == position, lane_take(tables[position], index), packed)
-        tail[24] = packed
-
-    @pl.when(tile == 0)
-    def fill_head():
-        for position in range(24):
-            head[position] = tables[position]
-
-    @pl.when(tile == 1)
-    def fill_head_extra():
-        packed = jnp.zeros((8, LANES), F32)
-        for position in range(24):
-            packed = jnp.where(
-                lanes == position, lane_take(tables[position], jnp.zeros_like(lanes)), packed
-            )
-        head[24] = packed
+    def fill(tail, head):
+        @pl.when(tile == 0)
+        def clear_tail():
+            tail[...] = jnp.zeros((25, 8, LANES), F32)
+            head[...] = jnp.zeros((25, 8, LANES), F32)
+
+        @pl.when(in_tail)
+        def fill_tail():
+            index = jnp.bitwise_and(lanes + offset, LANES - 1)
+            before_wrap = (lanes < LANES - offset).astype(jnp.int32)
+            wanted = before_wrap == (tile == start_tile).astype(jnp.int32)
+            for position in range(24):
+                tail[position] = jnp.where(
+                    wanted, lane_take(tables[position], index), tail[position]
+                )
+
+        @pl.when(in_extra)
+        def fill_extra():
+            index = jnp.zeros_like(lanes) + extra_lane
+            packed = jnp.zeros((8, LANES), F32)
+            for position in range(24):
+                packed = jnp.where(lanes == position, lane_take(tables[position], index), packed)
+            tail[24] = packed
+
+        @pl.when(tile == 0)
+        def fill_head():
+            for position in range(24):
+                head[position] = tables[position]
+
+        @pl.when(tile == 1)
+        def fill_head_extra():
+            packed = jnp.zeros((8, LANES), F32)
+            for position in range(24):
+                packed = jnp.where(
+                    lanes == position, lane_take(tables[position], jnp.zeros_like(lanes)), packed
+                )
+            head[24] = packed
+
+    odd = jnp.bitwise_and(count[1], 1)
+    pl.when(odd == 0)(lambda: fill(near, far))
+    pl.when(odd == 1)(lambda: fill(far, near))
 
 
 def finish_kernel(norms, scalars_in, smoothed, direction_in, direction):
@@ -420,17 +501,16 @@
     return high, (values - high.astype(F32)).astype(BF16)
 
 
-def product3(table, values):
+def product3(tables, rows, columns, values):
     high, low = split(values)
-    result = jnp.dot(table[0], high, preferred_element_type=F32)
-    result = result + jnp.dot(table[0], low, preferred_element_type=F32)
-    return result + jnp.dot(table[1], high, preferred_element_type=F32)
+    result = jnp.dot(tables[0, rows, columns], high, preferred_element_type=F32)
+    result = result + jnp.dot(tables[0, rows, columns], low, preferred_element_type=F32)
+    return result + jnp.dot(tables[1, rows, columns], high, preferred_element_type=F32)
 
 
 def operate_kernel(
     helmholtz,
-    counts,
-    lists,
+    plan,
     field,
     ints,
     copies,
@@ -439,8 +519,7 @@
     vertical,
     below_row,
     state,
-    forward,
-    backward,
+    tables,
     applied,
     table,
     edges,
@@ -464,11 +543,11 @@
 
         lax.fori_loop(0, GROUPS, one, 0)
 
-    gather_pick(table, 0, ints, counts, lists, 8, tile, edges, corners, pick)
+    gather_pick(table, 0, ints, plan, False, tile, edges, corners, pick)
     mixed, along_y, along_x = metric[1], metric[2], metric[0]
     for half in range(2):
         values = jnp.concatenate([field[8 * half + level, :, here] for level in range(8)], axis=0)
-        gradients = product3(forward, values)
+        gradients = product3(tables, slice(0, 256), slice(0, 128), values)
         flux_x = []
         flux_y = []
         for level in range(8):
@@ -476,11 +555,11 @@
             part_y = gradients[128 + 16 * level : 144 + 16 * level]
             flux_x.append(along_x * part_x + mixed * part_y)
             flux_y.append(mixed * part_x + along_y * part_y)
-        stiff = product3(backward, jnp.concatenate(flux_x + flux_y, axis=0))
+        stiff = product3(tables, slice(256, 384), slice(0, 256), jnp.concatenate(flux_x + flux_y, axis=0))
         for level in range(8):
             applied[8 * half + level] = stiff[16 * level : 16 * level + 16]
     twice = PENALTY * copies[...]
-    flux = state[0, 0:16, :] + below_row[0, 32:33, :] * field[0, :, here]
+    flux = state[0, 0:16, :] + below_row[0, 4:5, :] * field[0, :, here]
     for level in range(LEVELS):
         value = field[level, :, here]
         higher = field[level + 1, :, here] if level < LEVELS - 1 else state[0, 16:32, :]
@@ -495,12 +574,12 @@
 
 
 def image_kernel(first, *refs):
-    counts, lists, applied, smoothed, ints, before, after, product, inverse, vertical = refs[:10]
+    count, plan, applied, smoothed, ints, near, far, product, inverse, vertical = refs[:10]
     refs = refs[10:]
     if not first:
         direction, previous = refs[:2]
         refs = refs[2:]
-    image, message, table, edges, corners, pick, parts, crosses = refs
+    image, message, dots, table, edges, corners, pick, parts, crosses = refs
     tile = pl.program_id(0)
     rows, lanes = iotas()
 
@@ -508,19 +587,25 @@
     def build():
         parts[...] = jnp.zeros((16, LANES), F32)
         crosses[...] = jnp.zeros((16, LANES), F32)
-        for position in range(24):
-            index = jnp.full((8, LANES), position, jnp.int32)
-            table[position, :, 0:LANES] = before[position]
-            table[position, :, LANES : 2 * LANES] = after[position]
-            table[position, :, 2 * LANES : 3 * LANES] = jnp.where(
-                lanes == 0, lane_take(before[24], index), lane_take(after[24], index)
-            )
+
+        def fill(before, after):
+            for position in range(24):
+                index = jnp.full((8, LANES), position, jnp.int32)
+                table[position, :, 0:LANES] = before[position]
+                table[position, :, LANES : 2 * LANES] = after[position]
+                table[position, :, 2 * LANES : 3 * LANES] = jnp.where(
+                    lanes == 0, lane_take(before[24], index), lane_take(after[24], index)
+                )
+
+        odd = jnp.bitwise_and(count[1], 1)
+        pl.when(odd == 0)(lambda: fill(far, near))
+        pl.when(odd == 1)(lambda: fill(near, far))
 
     pick[...] = jnp.zeros((LEVELS, NODES, LANES), F32)
 
-    @pl.when(counts[tile] > 0)
+    @pl.when(plan[tile * PLAN + 1] > 0)
     def reach():
-        gather_pick(table, 8, ints, counts, lists, 3, tile, edges, corners, pick)
+        gather_pick(table, 8, ints, plan, True, tile, edges, corners, pick)
 
     total = cross = None
     for level in range(LEVELS):
@@ -536,18 +621,15 @@
     if not first:
         crosses[...] += cross
     upward, downward = group_response(lambda level: image[level], inverse, vertical)
-    message[tile, 0:16, :] = upward
-    message[tile, 16:32, :] = downward
+    message[0, 0:16, :] = upward
+    message[0, 16:32, :] = downward
 
     @pl.when(tile == GROUPS - 1)
     def finish():
-        curvature = jnp.sum(parts[...], axis=0, keepdims=True)
-        mixed = jnp.sum(crosses[...], axis=0, keepdims=True)
-        for target in range(GROUPS):
-            message[target, 32:33, :] = product[0:1, :]
-            message[target, 33:34, :] = curvature
-            message[target, 34:35, :] = mixed
-            message[target, 35:40, :] = jnp.zeros((5, LANES), F32)
+        dots[0:1, :] = product[0:1, :]
+        dots[1:2, :] = jnp.sum(parts[...], axis=0, keepdims=True)
+        dots[2:3, :] = jnp.sum(crosses[...], axis=0, keepdims=True)
+        dots[3:8, :] = jnp.zeros((5, LANES), F32)
 
 
 def field_spec():
@@ -606,70 +688,95 @@
     return [pltpu.VMEM(shape, dtype) for shape, dtype in shapes]
 
 
-def neighbour_lists(source, first_tile, tile_count):
-    holder = (source // LANES).reshape(16, 8, LANES)
-    tiles = first_tile + jnp.arange(tile_count, dtype=jnp.int32)
-    used = jnp.any(holder[:, :, None, :] == tiles[None, None, :, None], axis=(0, 3))
-    slots = jnp.arange(tile_count, dtype=jnp.int32)
-    earlier = used[:, None, :] & (slots[None, None, :] < slots[None, :, None])
-    place = jnp.sum(earlier.astype(jnp.int32), axis=2)
-    chosen = used[:, :, None] & (place[:, :, None] == slots)
-    lists = jnp.sum(jnp.where(chosen, tiles[None, :, None], 0), axis=1)
-    return jnp.sum(used.astype(jnp.int32), axis=1), lists.astype(jnp.int32).reshape(-1)
-
-
-def sum_over_elem(value, peers):
-    side = math.isqrt(peers)
-    for inner in (True, False):
-        total = value
-        for shift in range(1, side):
-            pairs = []
-            for i in range(peers):
-                outer, within = i // side, i % side
-                if inner:
-                    pairs.append((i, outer * side + (within + shift) % side))
-                else:
-                    pairs.append((i, (outer + shift) % side * side + within))
-            total = total + lax.ppermute(value, "elem", pairs)
-        value = total
-    return value
-
-
-def neighbour_tables(edge_neighbour, edge_flip, corner_neighbour, count_before, position):
-    slot_count = edge_neighbour.shape[0]
-
-    def locate(element):
-        holder = element // slot_count
-        within = element % slot_count
+def prepare_kernel(place, edge_rows, flip_rows, corner_rows, ints, copies):
+    position, count_before = place[0], place[1]
+
+    def source_of(entry):
+        element = lax.shift_right_logical(entry, 2)
+        holder = lax.shift_right_logical(element, 10)
+        within = jnp.bitwise_and(element, 1023)
         earlier = within - (count_before - BORDER)
         earlier = jnp.where(earlier == 0, 10 * LANES, 8 * LANES + earlier - 1)
         later = jnp.where(within < LANES, 9 * LANES + within, 10 * LANES + 1)
-        return jnp.where(holder == position, within, jnp.where(holder < position, earlier, later))
-
-    edges = jnp.transpose(edge_neighbour)
-    flips = jnp.transpose(edge_flip)
-    corners = jnp.transpose(corner_neighbour, (1, 2, 0)).reshape(12, slot_count)
-    everything = jnp.concatenate([edges, corners], axis=0)
-    present = everything >= 0
-    target = jnp.where(present, everything, 0)
-    source = jnp.where(present, locate(target // 4), ABSENT)
-    side = target % 4
-    straight = 2 * side[:4] + jnp.where(flips == 1, 1, 0)
-    swapped = 2 * side[:4] + jnp.where(flips == 1, 0, 1)
-    none = jnp.zeros_like(straight[0])
-    low = [none, straight[0], swapped[0], none, straight[3], none, none, straight[1]]
-    high = [swapped[3], none, none, swapped[1], none, straight[2], swapped[2], none]
-    ints = jnp.concatenate([source, jnp.stack(low), jnp.stack(high), side], axis=0).astype(jnp.int32)
-    on = present.astype(F32)
-    shared = jnp.sum(on[4:].reshape(4, 3, slot_count), axis=1)
-    nothing = jnp.zeros_like(shared[0])
-    copies = jnp.stack(
-        [
-            shared[0], on[0], on[0], shared[1], on[3], nothing, nothing, on[1],
-            on[3], nothing, nothing, on[1], shared[3], on[2], on[2], shared[2],
-        ]
-    )
-    return source, ints, copies
+        source = jnp.where(holder == position, within, jnp.where(holder < position, earlier, later))
+        return jnp.where(entry >= 0, source, ABSENT)
+
+    edges, corners = edge_rows[...], corner_rows[...]
+    ints[0:4, :] = source_of(edges)
+    ints[4:16, :] = source_of(corners)
+    flipped = (flip_rows[...] == 1).astype(jnp.int32)
+    straight = 2 * jnp.bitwise_and(edges, 3) + flipped
+    swapped_row = 2 * jnp.bitwise_and(edges, 3) + 1 - flipped
+    none = jnp.zeros((1, LANES), jnp.int32)
+
+    def of(rows, side):
+        return rows[side : side + 1, :]
+
+    low = [none, of(straight, 0), of(swapped_row, 0), none, of(straight, 3), none, none, of(straight, 1)]
+    high = [of(swapped_row, 3), none, none, of(swapped_row, 1), none, of(straight, 2),
+            of(swapped_row, 2), none]
+    for row, value in enumerate(low + high):
+        ints[16 + row : 17 + row, :] = value
+    ints[32:36, :] = jnp.zeros((4, LANES), jnp.int32)
+    ints[36:48, :] = jnp.bitwise_and(corners, 3)
+    on = (edges >= 0).astype(F32)
+    there = (corners >= 0).astype(F32)
+    shared = [
+        of(there, 3 * corner) + of(there, 3 * corner + 1) + of(there, 3 * corner + 2)
+        for corner in range(4)
+    ]
+    zero = jnp.zeros((1, LANES), F32)
+    rows = [
+        shared[0], of(on, 0), of(on, 0), shared[1], of(on, 3), zero, zero, of(on, 1),
+        of(on, 3), zero, zero, of(on, 1), shared[3], of(on, 2), of(on, 2), shared[2],
+    ]
+    for row, value in enumerate(rows):
+        copies[row : row + 1, :] = value
+
+
+def gather_plan(ints):
+    holder = (ints[:16] // LANES).reshape(16, 8, LANES)
+    tiles = jnp.arange(11, dtype=jnp.int32)
+    used = jnp.any(holder[:, :, None, :] == tiles[None, None, :, None], axis=(0, 3))
+    far = tiles >= 8
+    same = far[:, None] == far[None, :]
+    earlier = used[:, None, :] & (same & (tiles[None, :] < tiles[:, None]))[None]
+    place = jnp.sum(earlier.astype(jnp.int32), axis=2) + jnp.where(far, 10, 2)[None]
+    columns = jnp.arange(PLAN, dtype=jnp.int32)
+    listed = (place[:, :, None] == columns) * tiles[None, :, None]
+    counted = columns[None, :] == jnp.where(far, 1, 0)[:, None]
+    values = jnp.where(used[:, :, None], listed + counted[None].astype(jnp.int32), 0)
+    return jnp.sum(values, axis=1).astype(jnp.int32).reshape(-1)
+
+
+def parts_along(value, peers, inner):
+    side = math.isqrt(peers)
+    parts = []
+    for shift in range(1, side):
+        pairs = []
+        for i in range(peers):
+            outer, within = i // side, i % side
+            if inner:
+                pairs.append((i, outer * side + (within ^ shift)))
+            else:
+                pairs.append((i, (outer ^ shift) * side + within))
+        parts.append(lax.ppermute(value, "elem", pairs))
+    return parts
+
+
+def swapped(value, distance):
+    return lax.ppermute(value, "lev", [(i, i ^ distance) for i in range(GROUPS)])
+
+
+def join(name, first, last, shapes, args):
+    return pl.pallas_call(
+        lambda *refs: joined(first, last, *refs),
+        in_specs=[scalars()] + [pl.BlockSpec(memory_space=pltpu.VMEM)] * (len(args) - 1),
+        out_shape=[struct(8, rows, LANES) for rows in shapes],
+        name=name,
+        cost_estimate=pl.CostEstimate(flops=1 << 16, bytes_accessed=1 << 18, transcendentals=0),
+        compiler_params=pltpu.CompilerParams(vmem_limit_bytes=SMALL_VMEM_BYTES),
+    )(*args)
 
 
 def body(
@@ -687,7 +794,9 @@
     peers = lax.axis_size("elem")
     position = lax.axis_index("elem")
     upward_elem = [(i, i + 1) for i in range(peers - 1)]
-    downward_elem = [(i + 1, i) for i in range(peers - 1)]
+    near_pairs = [(i, i ^ 1) for i in range(peers)]
+    far_pairs = [(i, i - 1 if i % 2 == 0 else i + 1) for i in range(1, peers - 1)]
+    count = jnp.concatenate([element_count, position.astype(jnp.int32)[None]])
 
     residual, message = call(
         begin_kernel,
@@ -699,30 +808,49 @@
         1 << 22,
         (element_count, right_side, block_inverse, vertical),
     )
-    coupling = lax.all_to_all(message, "lev", split_axis=0, concat_axis=0, tiled=True)
-    scan_cost = pl.CostEstimate(flops=1 << 16, bytes_accessed=1 << 18, transcendentals=0)
-    small = pltpu.CompilerParams(vmem_limit_bytes=SMALL_VMEM_BYTES)
-    carried = pl.pallas_call(
-        scan_first_kernel,
-        out_shape=struct(8, 40, LANES),
-        name="scan_first",
-        cost_estimate=scan_cost,
-        compiler_params=small,
-    )(coupling)
-    came = lax.all_to_all(carried, "lev", split_axis=0, concat_axis=0, tiled=True)
-    below_row = came
+    group = lax.axis_index("lev")
+    flags = [
+        jnp.stack([(group >> step) & 1, ((group & (2**step - 1)) == 0).astype(jnp.int32)])
+        for step in range(3)
+    ]
+    ones = jnp.ones((8, 1, LANES), F32)
+    nothing = jnp.zeros((8, 1, LANES), F32)
+    aux = jnp.concatenate([ones, ones, nothing, ones] + [nothing] * 4, axis=1)
+    empty = jnp.zeros((8, 48, LANES), F32)
+    terms = [None] * 3
+    seg, inner = message, empty
+    for step in range(2):
+        got = swapped(seg, 2**step)
+        seg, inner, terms[step], aux = join(
+            "join_first", True, False, [40, 48, 8, 8], (flags[step], seg, got, inner, aux)
+        )
+    got = swapped(seg, 4)
+    came, terms[2], below_row, ends = join(
+        "join_first_last", True, True, [32, 8, 8, 8], (flags[2], seg, got, inner, aux, message)
+    )
 
     count_before = lax.ppermute(element_count, "elem", upward_elem)[0]
-    source, ints, copies = neighbour_tables(
-        edge_neighbour, edge_flip, corner_neighbour, count_before, position
+    ints, copies = call(
+        prepare_kernel,
+        "prepare",
+        [scalars(), row_spec(4), row_spec(4), row_spec(12)],
+        [row_spec(48), row_spec(16)],
+        [jax.ShapeDtypeStruct((48, 1024), jnp.int32), struct(16, 1024)],
+        [],
+        1 << 18,
+        (
+            jnp.stack([position, count_before]).astype(jnp.int32),
+            jnp.transpose(edge_neighbour),
+            jnp.transpose(edge_flip),
+            jnp.transpose(corner_neighbour, (1, 2, 0)).reshape(12, 1024),
+        ),
     )
-    own_counts, own_lists = neighbour_lists(source, 0, 8)
-    far_counts, far_lists = neighbour_lists(source, 8, 3)
-    forward, backward = stacked_tables()
-
-    shared_specs = [scalars(), inverse_spec(), row_spec(16), field_spec(), tile_spec(40)]
+    plan = gather_plan(ints)
+    tables = stacked_tables()
+
+    shared_specs = [scalars(), inverse_spec(), row_spec(16), field_spec(), tile_spec(32)]
     halo = struct(25, 8, LANES)
-    smoothed, product, tail, head = call(
+    smoothed, product, near, far = call(
         lambda *refs: solve_kernel(0, False, *refs),
         "solve_first",
         shared_specs,
@@ -730,34 +858,34 @@
         [struct(*FIELD), struct(8, LANES), halo, halo],
         vmem([((24, 8, LANES), F32), ((16, LANES), F32)]),
         1 << 22,
-        (element_count, block_inverse, vertical, residual, came),
+        (count, block_inverse, vertical, residual, came),
     )
     state = came
     solution = direction = image = flow = scalar_rows = None
     for iteration in range(ITERATIONS):
         first = iteration == 0
         last = iteration == ITERATIONS - 1
-        before = lax.ppermute(tail, "elem", upward_elem)
-        after = lax.ppermute(head, "elem", downward_elem)
+        near = lax.ppermute(near, "elem", near_pairs)
+        far = lax.ppermute(far, "elem", far_pairs)
         applied = call(
             operate_kernel,
             "operate",
             [
-                scalars(), scalars(), scalars(), whole(*FIELD), row_spec(48), row_spec(16),
+                scalars(), scalars(), whole(*FIELD), row_spec(48), row_spec(16),
                 pl.BlockSpec((3, NODES, LANES), lambda t: (0, 0, t)), row_spec(16), row_spec(16),
-                tile_spec(40), tile_spec(state.shape[1]), whole(2, 256, 128), whole(2, 128, 256),
+                tile_spec(8), tile_spec(32), whole(2, 384, 256),
             ],
             field_spec(),
             struct(*FIELD),
             vmem([((24, 8, 1024), F32)] + PICK_SCRATCH),
             1 << 30,
             (
-                helmholtz, own_counts, own_lists, smoothed, ints, copies, metric, mass_weight,
-                vertical, below_row, state, forward, backward,
+                helmholtz, plan, smoothed, ints, copies, metric, mass_weight,
+                vertical, below_row, state, tables,
             ),
         )
         args = [
-            far_counts, far_lists, applied, smoothed, ints, before, after, product, block_inverse,
+            count, plan, applied, smoothed, ints, near, far, product, block_inverse,
             vertical,
         ]
         specs = [
@@ -767,34 +895,39 @@
         if not first:
             args += [direction, image]
             specs += [field_spec(), field_spec()]
-        applied, message = call(
+        applied, message, dots = call(
             lambda *refs, first=first: image_kernel(first, *refs),
             "image_first" if first else "image",
             specs,
-            [field_spec(), whole(8, 40, LANES)],
-            [struct(*FIELD), struct(8, 40, LANES)],
+            [field_spec(), tile_spec(32), whole(8, LANES)],
+            [struct(*FIELD), struct(8, 32, LANES), struct(8, LANES)],
             vmem(
                 [((24, 8, 3 * LANES), F32)] + PICK_SCRATCH + [((16, LANES), F32), ((16, LANES), F32)]
             ),
             1 << 22,
             args,
         )
-        received = lax.all_to_all(message, "lev", split_axis=0, concat_axis=0, tiled=True)
-        carried, dots = pl.pallas_call(
-            scan_kernel,
-            out_shape=[struct(8, 32, LANES), struct(8, LANES)],
-            name="scan",
-            cost_estimate=scan_cost,
-            compiler_params=small,
-        )(received, coupling)
-        dots = sum_over_elem(dots, peers)
-        carried, dots = lax.optimization_barrier((carried, dots))
-        came = lax.all_to_all(carried, "lev", split_axis=0, concat_axis=0, tiled=True)
-
-        args = [element_count, block_inverse, vertical, residual, came, smoothed, applied, state, dots]
-        specs = shared_specs[:4] + [
-            tile_spec(32), field_spec(), field_spec(), tile_spec(state.shape[1]), whole(8, LANES),
-        ]
+        seg, inner = message, empty
+        for step in range(2):
+            got = swapped(seg, 2**step)
+            others = parts_along(dots, peers, step == 0)
+            got, *others = lax.optimization_barrier((got, *others))
+            dots = (dots + others[0]) + (others[1] + others[2])
+            seg, inner = join(
+                "join", False, False, [32, 48], (flags[step], seg, got, inner, terms[step])
+            )
+        got = swapped(seg, 4)
+        other = swapped(dots, 4)
+        got, other = lax.optimization_barrier((got, other))
+        dots = dots + other
+        (came,) = join(
+            "join_last", False, True, [32], (flags[2], seg, got, inner, terms[2], message, ends)
+        )
+        dots = dots + swapped(dots, 2)
+        dots = [dots, swapped(dots, 1)]
+
+        args = [count, block_inverse, vertical, residual, came, smoothed, applied, state] + dots
+        specs = shared_specs + [field_spec(), field_spec(), tile_spec(32)] + [whole(8, LANES)] * 2
         if not first:
             args += [solution, direction, image, flow, scalar_rows]
             specs += [field_spec(), field_spec(), field_spec(), tile_spec(32), whole(8, LANES)]
@@ -824,7 +957,7 @@
             solution, residual, direction, scalar_rows, smoothed, product = results
         else:
             solution, residual, direction, scalar_rows, image, flow, state = results[:7]
-            smoothed, product, tail, head = results[7:]
+            smoothed, product, near, far = results[7:]
     norms = lax.all_to_all(product, ("elem", "lev"), split_axis=0, concat_axis=0, tiled=True)
     direction = call(
         finish_kernel,

time: 248 us -> 235 us (0.948); the launches traced: 248 us -> 231 us
  blocking collectives: 75.7 us -> 14.2 us
  Pallas kernels: 62.6 us -> 78.4 us
  waiting for transfers between devices: 28.7 us -> 41.5 us
  starting transfers between devices: 65.8 us -> 78.5 us
  local copies, waits for them, and re-layouts: 10.4 us -> 13.4 us
    all_to_all x6 -> x0, blocking collectives: 62.2 us -> none  [the longest x3 35.1 us: body(): lax.all_to_all(carried, 'lev', split_axis=0, concat_axis=0, tiled=True)]
    ppermute x24 -> x45, starting transfers between devices: 50.6 us -> 73.9 us  [the longest x21 39.2 us: swapped(): lax.ppermute(value, 'lev', [(i, i ^ distance) for i in range(GROUPS)])]
    ppermute x24 -> x45, waiting for transfers between devices: 21.4 us -> 41.5 us  [the longest x21 23.6 us: swapped(): lax.ppermute(value, 'lev', [(i, i ^ distance) for i in range(GROUPS)])]
    all_to_all x2 -> x0, starting transfers between devices: 10.7 us -> none  [the longest x1 6.4 us: body(): lax.all_to_all(message, 'lev', split_axis=0, concat_axis=0, tiled=True)]
    pallas_call x12 -> x13, Pallas kernels: 61.8 us -> 71.2 us  [call(): pl.pallas_call(kernel, grid=(GROUPS,), in_specs=in_specs, out_specs=out_s...]
    all_to_all x2 -> x0, waiting for transfers between devices: 7.34 us -> none  [the longest x1 5.39 us: body(): lax.all_to_all(carried, 'lev', split_axis=0, concat_axis=0, tiled=True)]
    pallas_call x4 -> x12, Pallas kernels: 0.8 us -> 7.17 us  [join(): pl.pallas_call(lambda *refs: joined(first, last, *refs), in_specs=[scalar...]
    unnamed x37 -> x63, local copies, waits for them, and re-layouts: 8.04 us -> 11.9 us
  transfers between devices with their start and end apart: 27 -> 46, of which waited for: 15 -> 22; matrix products, arithmetic and copies ran while one was open for 2% -> 2% of each run, Pallas kernels for 13% -> 18%
where the time goes in v3:
time: 235 us; the launch traced here: 231 us
  starting transfers between devices  78.5 us (33%)
  Pallas kernels  78.4 us (33%)
  waiting for transfers between devices  41.5 us (18%)
  blocking collectives  14.2 us (6%)
  local copies, waits for them, and re-layouts  13.4 us (6%)
  other arithmetic  3.24 us (1%)
    pallas_call x13, Pallas kernels, call(): pl.pallas_call(kernel, grid=(GROUPS,), in_specs=in_specs, out_specs=out_s...  71.2 us
    ppermute x21, starting transfers between devices, swapped(): lax.ppermute(value, 'lev', [(i, i ^ distance) for i in range(GROUPS)])  39.2 us
    ppermute x18, starting transfers between devices, parts_along(): parts.append(lax.ppermute(value, 'elem', pairs))  31.7 us
    ppermute x21, waiting for transfers between devices, swapped(): lax.ppermute(value, 'lev', [(i, i ^ distance) for i in range(GROUPS)])  23.6 us
    ppermute x18, waiting for transfers between devices, parts_along(): parts.append(lax.ppermute(value, 'elem', pairs))  17.8 us
    all_to_all x1, blocking collectives, body(): lax.all_to_all(product, ('elem', 'lev'), split_axis=0, concat_axis=0, til...  14.2 us
    unnamed x63, local copies, waits for them, and re-layouts  11.9 us
    pallas_call x12, Pallas kernels, join(): pl.pallas_call(lambda *refs: joined(first, last, *refs), in_specs=[scalar...  7.17 us
  transfers between devices with their start and end apart: 46, of which 22 were waited for; matrix products, arithmetic and copies ran while one was open for 2% of the time, Pallas kernels for 18%

profile of v3, /device:TPU:1, one launch (start us, length us, event | category | flops | bytes accessed | tf_op | source)
XLA Modules:
  0.0 231.0 jit_solution(5513511742936147461)
XLA Ops:
  0.6 4.6 %collective-permute-start = (s32[1]{0:T(128)}, s32[1]{0:T(128)}, u32[]{:S(2)}, u32[]{:S(2)}) collective-permute-start(s32[1]{0:T(128)} %param.20), channel_id=1, source_target_pairs={{0,8},{8,16},{16,24},{24,32},{32,40},{40,48},{48,56},{56,64},{64,7... | collective-permute-start | bytes 20 | tf_op jit(solution)/shard_map/ppermute | solution.py:832
  18.6 3.2 %collective-permute-done.2.refs_2_ = f32[8,40,128]{2,1,0:T(8,128)S(1)} collective-permute-done((f32[8,40,128]{2,1,0:T(8,128)S(1)}, f32[8,40,128]{2,1,0:T(8,128)S(1)}, u32[]{:S(2)}, u32[]{:S(2)}) %collective-permute-start.2) | collective-permute-done | bytes 163872 | tf_op jit(solution)/shard_map/ppermute | solution.py:768
  22.5 3.4 %collective-permute-start.3 = (f32[8,40,128]{2,1,0:T(8,128)S(1)}, f32[8,40,128]{2,1,0:T(8,128)S(1)}, u32[]{:S(2)}, u32[]{:S(2)}) collective-permute-start(f32[8,40,128]{2,1,0:T(8,128)S(1)} %get-tuple-element.108.refs_1_), channel_id=1, source_target_pairs={{0,4},{1,5},{2,6},{3,7},{4,0},{5,1},{6,2},{7,3},{8,12},{9,13},{10,... | collective-permute-start | bytes 491528 | tf_op jit(solution)/shard_map/ppermute | solution.py:768
  25.9 3.7 %collective-permute-done.3.refs_2_ = f32[8,40,128]{2,1,0:T(8,128)S(1)} collective-permute-done((f32[8,40,128]{2,1,0:T(8,128)S(1)}, f32[8,40,128]{2,1,0:T(8,128)S(1)}, u32[]{:S(2)}, u32[]{:S(2)}) %collective-permute-start.3) | collective-permute-done | bytes 163872 | tf_op jit(solution)/shard_map/ppermute | solution.py:768
  30.8 3.3 %solve_first.1 = (f32[16,16,1024]{2,1,0:T(8,128)S(1)}, f32[8,128]{1,0:T(8,128)S(1)}, f32[25,8,128]{2,1,0:T(8,128)}, f32[25,8,128]{2,1,0:T(8,128)}) custom-call(s32[2]{0:T(128)S(1)} %pad_add_fusion.refs_0_, f32[2,8,8,1024]{3,2,1,0:T(8,128)S(1)} %copy-done.1, f32[16,1024]{1,0:T(8,128)S(1)} %copy-done.3, f32[16,16,1024]{2,1,0:T(8,128)S(1)} %get-tuple-element.102.refs_3_, ...), custom_call_target="tpu_custom_call" | custom-call | flops 4194304 | bytes 6291456 | tf_op jit(solution)/shard_map/solve_first/pallas_call | solution.py:664
  43.2 12.4 %operate.3.refs_2_ = f32[16,16,1024]{2,1,0:T(8,128)S(1)} custom-call(f32[16]{0:T(128)S(1)} %copy-done.24, s32[104]{0:T(128)S(1)} %copy-done.12, f32[16,16,1024]{2,1,0:T(8,128)S(1)} %get-tuple-element.112.field.refs_3_.refs_5_, s32[48,1024]{1,0:T(8,128)S(1)} %get-tuple-element.103.ints.refs_4_, f32[16,1024]{1,0:T(8,128)S(1)} %copy-done.19, ...), custom_call_target="tpu_custom_call" | custom-call | flops 1073741824 | bytes 6291456 | tf_op jit(solution)/shard_map/operate/pallas_call | solution.py:664
  60.4 6.5 %collective-permute-start.9 = (f32[8,128]{1,0:T(8,128)S(1)}, f32[8,128]{1,0:T(8,128)S(1)}, u32[]{:S(2)}, u32[]{:S(2)}) collective-permute-start(f32[8,128]{1,0:T(8,128)S(1)} %get-tuple-element.119), channel_id=1, source_target_pairs={{0,24},{8,16},{16,8},{24,0},{32,56},{40,48},{48,40},{56,32},{64,88... | collective-permute-start | bytes 12296 | tf_op jit(solution)/shard_map/ppermute | solution.py:763
  80.6 3.4 %collective-permute-start.14 = (f32[8,32,128]{2,1,0:T(8,128)S(1)}, f32[8,32,128]{2,1,0:T(8,128)S(1)}, u32[]{:S(2)}, u32[]{:S(2)}) collective-permute-start(f32[8,32,128]{2,1,0:T(8,128)S(1)} %get-tuple-element.129.refs_1_), channel_id=1, source_target_pairs={{0,4},{1,5},{2,6},{3,7},{4,0},{5,1},{6,2},{7,3},{8,12},{9,13},{10,... | collective-permute-start | bytes 393224 | tf_op jit(solution)/shard_map/ppermute | solution.py:768
  84.1 3.9 %collective-permute-done.15 = f32[8,128]{1,0:T(8,128)S(1)} collective-permute-done((f32[8,128]{1,0:T(8,128)S(1)}, f32[8,128]{1,0:T(8,128)S(1)}, u32[]{:S(2)}, u32[]{:S(2)}) %collective-permute-start.15) | collective-permute-done | bytes 4128 | tf_op jit(solution)/shard_map/ppermute | solution.py:768
  90.4 5.8 %collective-permute-start.17 = (f32[8,128]{1,0:T(8,128)S(1)}, f32[8,128]{1,0:T(8,128)S(1)}, u32[]{:S(2)}, u32[]{:S(2)}) collective-permute-start(f32[8,128]{1,0:T(8,128)S(1)} %add.104.refs_8_), channel_id=1, source_target_pairs={{0,1},{1,0},{2,3},{3,2},{4,5},{5,4},{6,7},{7,6},{8,9},{9,8},{10,11... | collective-permute-start | bytes 12296 | tf_op jit(solution)/shard_map/ppermute | solution.py:768
  97.5 4.8 %solve.2 = (f32[16,16,1024]{2,1,0:T(8,128)S(1)}, f32[16,16,1024]{2,1,0:T(8,128)S(1)}, f32[16,16,1024]{2,1,0:T(8,128)S(1)}, f32[8,128]{1,0:T(8,128)S(1)}, f32[16,...) custom-call(s32[2]{0:T(128)S(1)} %pad_add_fusion.refs_0_, ...), custom_call_target="tpu_custom_call" | custom-call | flops 4194304 | bytes 6291456 | tf_op jit(solution)/shard_map/solve/pallas_call | solution.py:664
  103.1 12.5 %operate.4.refs_2_ = f32[16,16,1024]{2,1,0:T(8,128)S(1)} custom-call(f32[16]{0:T(128)S(1)} %copy-done.24, s32[104]{0:T(128)S(1)} %copy-done.12, f32[16,16,1024]{2,1,0:T(8,128)S(1)} %get-tuple-element.140.field.refs_3_.refs_5_, s32[48,1024]{1,0:T(8,128)S(1)} %get-tuple-element.103.ints.refs_4_, f32[16,1024]{1,0:T(8,128)S(1)} %copy-done.20, ...), custom_call_target="tpu_custom_call" | custom-call | flops 1073741824 | bytes 6291456 | tf_op jit(solution)/shard_map/operate/pallas_call | solution.py:664
  115.6 3.4 %image.2 = (f32[16,16,1024]{2,1,0:T(8,128)S(1)}, f32[8,32,128]{2,1,0:T(8,128)S(1)}, f32[8,128]{1,0:T(8,128)S(1)}) custom-call(s32[2]{0:T(128)S(1)} %pad_add_fusion.refs_0_, s32[104]{0:T(128)S(1)} %copy-done.12, f32[16,16,1024]{2,1,0:T(8,128)S(1)} %operate.4.refs_2_, f32[16,16,1024]{2,1,0:T(8,128)S(1)} %get-tuple-element.140.field.refs_3_.refs_5_, ...), custom_call_target="tpu_custom_call" | custom-call | flops 4194304 | bytes 6291456 | tf_op jit(solution)/shard_map/image/pallas_call | solution.py:664
  119.1 5.0 %collective-permute-start.23 = (f32[8,128]{1,0:T(8,128)S(1)}, f32[8,128]{1,0:T(8,128)S(1)}, u32[]{:S(2)}, u32[]{:S(2)}) collective-permute-start(f32[8,128]{1,0:T(8,128)S(1)} %get-tuple-element.148), channel_id=1, source_target_pairs={{0,24},{8,16},{16,8},{24,0},{32,56},{40,48},{48,40},{56,32},{64,88... | collective-permute-start | bytes 12296 | tf_op jit(solution)/shard_map/ppermute | solution.py:763
  144.5 5.6 %collective-permute-start.31 = (f32[8,128]{1,0:T(8,128)S(1)}, f32[8,128]{1,0:T(8,128)S(1)}, u32[]{:S(2)}, u32[]{:S(2)}) collective-permute-start(f32[8,128]{1,0:T(8,128)S(1)} %add.112.refs_8_), channel_id=1, source_target_pairs={{0,1},{1,0},{2,3},{3,2},{4,5},{5,4},{6,7},{7,6},{8,9},{9,8},{10,11... | collective-permute-start | bytes 12296 | tf_op jit(solution)/shard_map/ppermute | solution.py:768
  151.0 5.5 %solve.3 = (f32[16,16,1024]{2,1,0:T(8,128)S(1)}, f32[16,16,1024]{2,1,0:T(8,128)S(1)}, f32[16,16,1024]{2,1,0:T(8,128)S(1)}, f32[8,128]{1,0:T(8,128)S(1)}, f32[16,...) custom-call(s32[2]{0:T(128)S(1)} %pad_add_fusion.refs_0_, ...), custom_call_target="tpu_custom_call" | custom-call | flops 4194304 | bytes 6291456 | tf_op jit(solution)/shard_map/solve/pallas_call | solution.py:664
  157.3 12.4 %operate.5.refs_2_ = f32[16,16,1024]{2,1,0:T(8,128)S(1)} custom-call(f32[16]{0:T(128)S(1)} %copy-done.24, s32[104]{0:T(128)S(1)} %copy-done.12, f32[16,16,1024]{2,1,0:T(8,128)S(1)} %get-tuple-element.168.field.refs_3_.refs_5_, s32[48,1024]{1,0:T(8,128)S(1)} %get-tuple-element.103.ints.refs_4_, f32[16,1024]{1,0:T(8,128)S(1)} %copy-done.20, ...), custom_call_target="tpu_custom_call" | custom-call | flops 1073741824 | bytes 6291456 | tf_op jit(solution)/shard_map/operate/pallas_call | solution.py:664
  169.7 3.4 %image.3 = (f32[16,16,1024]{2,1,0:T(8,128)S(1)}, f32[8,32,128]{2,1,0:T(8,128)S(1)}, f32[8,128]{1,0:T(8,128)S(1)}) custom-call(s32[2]{0:T(128)S(1)} %pad_add_fusion.refs_0_, s32[104]{0:T(128)S(1)} %copy-done.12, f32[16,16,1024]{2,1,0:T(8,128)S(1)} %operate.5.refs_2_, f32[16,16,1024]{2,1,0:T(8,128)S(1)} %get-tuple-element.168.field.refs_3_.refs_5_, ...), custom_call_target="tpu_custom_call" | custom-call | flops 4194304 | bytes 6291456 | tf_op jit(solution)/shard_map/image/pallas_call | solution.py:664
  173.6 5.0 %collective-permute-start.37 = (f32[8,128]{1,0:T(8,128)S(1)}, f32[8,128]{1,0:T(8,128)S(1)}, u32[]{:S(2)}, u32[]{:S(2)}) collective-permute-start(f32[8,128]{1,0:T(8,128)S(1)} %get-tuple-element.176), channel_id=1, source_target_pairs={{0,24},{8,16},{16,8},{24,0},{32,56},{40,48},{48,40},{56,32},{64,88... | collective-permute-start | bytes 12296 | tf_op jit(solution)/shard_map/ppermute | solution.py:763
  195.1 3.4 %collective-permute-done.43 = f32[8,128]{1,0:T(8,128)S(1)} collective-permute-done((f32[8,128]{1,0:T(8,128)S(1)}, f32[8,128]{1,0:T(8,128)S(1)}, u32[]{:S(2)}, u32[]{:S(2)}) %collective-permute-start.43) | collective-permute-done | bytes 4128 | tf_op jit(solution)/shard_map/ppermute | solution.py:768
  201.3 5.8 %collective-permute-start.45 = (f32[8,128]{1,0:T(8,128)S(1)}, f32[8,128]{1,0:T(8,128)S(1)}, u32[]{:S(2)}, u32[]{:S(2)}) collective-permute-start(f32[8,128]{1,0:T(8,128)S(1)} %add.120.refs_8_), channel_id=1, source_target_pairs={{0,1},{1,0},{2,3},{3,2},{4,5},{5,4},{6,7},{7,6},{8,9},{9,8},{10,11... | collective-permute-start | bytes 12296 | tf_op jit(solution)/shard_map/ppermute | solution.py:768
  207.9 5.4 %solve_last.1 = (f32[16,16,1024]{2,1,0:T(8,128)}, f32[16,16,1024]{2,1,0:T(8,128)}, f32[16,16,1024]{2,1,0:T(8,128)S(1)}, f32[8,128]{1,0:T(8,128)S(1)}, f32[16,16,...) custom-call(s32[2]{0:T(128)S(1)} %pad_add_fusion.refs_0_, f32[2,8,8,1024]{3,2,1,0:T(8,128)S(1)} %copy-done.1, ...), custom_call_target="tpu_custom_call" | custom-call | flops 4194304 | bytes 6291456 | tf_op jit(solution)/shard_map/solve_last/pallas_call | solution.py:664
  213.3 14.2 %all_to_all.11 = f32[128,1,128]{2,1,0:T(1,128)S(1)} all-to-all(f32[128,1,128]{2,1,0:T(1,128)S(1)} %bitcast.17), channel_id=1, replica_groups=mesh['elem'=16,'lev'=8] {'elem','lev'}, dimensions={0} | all-to-all | bytes 131072 | tf_op jit(solution)/shard_map/all_to_all | solution.py:961
  227.5 3.6 %finish.1 = f32[16,16,1024]{2,1,0:T(8,128)} custom-call(f32[128,128]{1,0:T(8,128)S(1)} %bitcast.16, f32[8,128]{1,0:T(8,128)S(1)} %get-tuple-element.198.scalars_in, f32[16,16,1024]{2,1,0:T(8,128)S(1)} %get-tuple-element.199.smoothed, f32[16,16,1024]{2,1,0:T(8,128)S(1)} %get-tuple-element.200.direction_in), custom_call_target="tpu_custom_call" | custom-call | flops 1048576 | bytes 6291456 | tf_op jit(solution)/shard_map/finish/pallas_call | solution.py:664
  (189 shorter events, 89.2 us)
Async XLA Ops:
  0.6 11.3 %collective-permute-start = (s32[1]{0:T(128)}, s32[1]{0:T(128)}, u32[]{:S(2)}, u32[]{:S(2)}) collective-permute-start(s32[1]{0:T(128)} %param.20), channel_id=1, source_target_pairs={{0,8},{8,16},{16,24},{24,32},{32,40},{40,48},{48,56},{56,64},{64,7... | collective-permute-start | bytes 20 | tf_op jit(solution)/shard_map/ppermute | solution.py:832
  15.7 6.1 %collective-permute-start.2 = (f32[8,40,128]{2,1,0:T(8,128)S(1)}, f32[8,40,128]{2,1,0:T(8,128)S(1)}, u32[]{:S(2)}, u32[]{:S(2)}) collective-permute-start(f32[8,40,128]{2,1,0:T(8,128)S(1)} %get-tuple-element.105.refs_1_), channel_id=1, source_target_pairs={{0,2},{1,3},{2,0},{3,1},{4,6},{5,7},{6,4},{7,5},{8,10},{9,11},{10,... | collective-permute-start | bytes 491528 | tf_op jit(solution)/shard_map/ppermute | solution.py:768
  22.5 7.1 %collective-permute-start.3 = (f32[8,40,128]{2,1,0:T(8,128)S(1)}, f32[8,40,128]{2,1,0:T(8,128)S(1)}, u32[]{:S(2)}, u32[]{:S(2)}) collective-permute-start(f32[8,40,128]{2,1,0:T(8,128)S(1)} %get-tuple-element.108.refs_1_), channel_id=1, source_target_pairs={{0,4},{1,5},{2,6},{3,7},{4,0},{5,1},{6,2},{7,3},{8,12},{9,13},{10,... | collective-permute-start | bytes 491528 | tf_op jit(solution)/shard_map/ppermute | solution.py:768
  34.8 20.9 %collective-permute-start.4 = (f32[25,8,128]{2,1,0:T(8,128)}, f32[25,8,128]{2,1,0:T(8,128)S(1)}, u32[]{:S(2)}, u32[]{:S(2)}) collective-permute-start(f32[25,8,128]{2,1,0:T(8,128)} %get-tuple-element.115), channel_id=1, source_target_pairs={{0,8},{8,0},{16,24},{24,16},{32,40},{40,32},{48,56},{56,48},{64,72... | collective-permute-start | bytes 307208 | tf_op jit(solution)/shard_map/ppermute | solution.py:868
  35.5 20.1 %collective-permute-start.5 = (f32[25,8,128]{2,1,0:T(8,128)}, f32[25,8,128]{2,1,0:T(8,128)S(1)}, u32[]{:S(2)}, u32[]{:S(2)}) collective-permute-start(f32[25,8,128]{2,1,0:T(8,128)} %get-tuple-element.116), channel_id=1, source_target_pairs={{8,16},{16,8},{24,32},{32,24},{40,48},{48,40},{56,64},{64,56},{72,... | collective-permute-start | bytes 307208 | tf_op jit(solution)/shard_map/ppermute | solution.py:869
  58.6 12.2 %collective-permute-start.6 = (f32[8,32,128]{2,1,0:T(8,128)S(1)}, f32[8,32,128]{2,1,0:T(8,128)S(1)}, u32[]{:S(2)}, u32[]{:S(2)}) collective-permute-start(f32[8,32,128]{2,1,0:T(8,128)S(1)} %get-tuple-element.118.refs_1_.refs_5_), channel_id=1, source_target_pairs={{0,1},{1,0},{2,3},{3,2},{4,5},{5,4},{6,7},{7,6},{8,9},{9,8},{10,11... | collective-permute-start | bytes 393224 | tf_op jit(solution)/shard_map/ppermute | solution.py:768
  60.4 7.4 %collective-permute-start.9 = (f32[8,128]{1,0:T(8,128)S(1)}, f32[8,128]{1,0:T(8,128)S(1)}, u32[]{:S(2)}, u32[]{:S(2)}) collective-permute-start(f32[8,128]{1,0:T(8,128)S(1)} %get-tuple-element.119), channel_id=1, source_target_pairs={{0,24},{8,16},{16,8},{24,0},{32,56},{40,48},{48,40},{56,32},{64,88... | collective-permute-start | bytes 12296 | tf_op jit(solution)/shard_map/ppermute | solution.py:763
  71.4 8.6 %collective-permute-start.10 = (f32[8,32,128]{2,1,0:T(8,128)S(1)}, f32[8,32,128]{2,1,0:T(8,128)S(1)}, u32[]{:S(2)}, u32[]{:S(2)}) collective-permute-start(f32[8,32,128]{2,1,0:T(8,128)S(1)} %get-tuple-element.122.refs_1_), channel_id=1, source_target_pairs={{0,2},{1,3},{2,0},{3,1},{4,6},{5,7},{6,4},{7,5},{8,10},{9,11},{10,... | collective-permute-start | bytes 393224 | tf_op jit(solution)/shard_map/ppermute | solution.py:768
  80.6 7.4 %collective-permute-start.14 = (f32[8,32,128]{2,1,0:T(8,128)S(1)}, f32[8,32,128]{2,1,0:T(8,128)S(1)}, u32[]{:S(2)}, u32[]{:S(2)}) collective-permute-start(f32[8,32,128]{2,1,0:T(8,128)S(1)} %get-tuple-element.129.refs_1_), channel_id=1, source_target_pairs={{0,4},{1,5},{2,6},{3,7},{4,0},{5,1},{6,2},{7,3},{8,12},{9,13},{10,... | collective-permute-start | bytes 393224 | tf_op jit(solution)/shard_map/ppermute | solution.py:768
  90.4 7.0 %collective-permute-start.17 = (f32[8,128]{1,0:T(8,128)S(1)}, f32[8,128]{1,0:T(8,128)S(1)}, u32[]{:S(2)}, u32[]{:S(2)}) collective-permute-start(f32[8,128]{1,0:T(8,128)S(1)} %add.104.refs_8_), channel_id=1, source_target_pairs={{0,1},{1,0},{2,3},{3,2},{4,5},{5,4},{6,7},{7,6},{8,9},{9,8},{10,11... | collective-permute-start | bytes 12296 | tf_op jit(solution)/shard_map/ppermute | solution.py:768
  102.3 13.3 %collective-permute-start.18 = (f32[25,8,128]{2,1,0:T(8,128)S(1)}, f32[25,8,128]{2,1,0:T(8,128)S(1)}, u32[]{:S(2)}, u32[]{:S(2)}) collective-permute-start(f32[25,8,128]{2,1,0:T(8,128)S(1)} %get-tuple-element.142), channel_id=1, source_target_pairs={{0,8},{8,0},{16,24},{24,16},{32,40},{40,32},{48,56},{56,48},{64,72... | collective-permute-start | bytes 307208 | tf_op jit(solution)/shard_map/ppermute | solution.py:868
  102.4 13.2 %collective-permute-start.19 = (f32[25,8,128]{2,1,0:T(8,128)S(1)}, f32[25,8,128]{2,1,0:T(8,128)S(1)}, u32[]{:S(2)}, u32[]{:S(2)}) collective-permute-start(f32[25,8,128]{2,1,0:T(8,128)S(1)} %get-tuple-element.143), channel_id=1, source_target_pairs={{8,16},{16,8},{24,32},{32,24},{40,48},{48,40},{56,64},{64,56},{72,... | collective-permute-start | bytes 307208 | tf_op jit(solution)/shard_map/ppermute | solution.py:869
  119.0 9.1 %collective-permute-start.20 = (f32[8,32,128]{2,1,0:T(8,128)S(1)}, f32[8,32,128]{2,1,0:T(8,128)S(1)}, u32[]{:S(2)}, u32[]{:S(2)}) collective-permute-start(f32[8,32,128]{2,1,0:T(8,128)S(1)} %get-tuple-element.147.refs_1_.refs_5_), channel_id=1, source_target_pairs={{0,1},{1,0},{2,3},{3,2},{4,5},{5,4},{6,7},{7,6},{8,9},{9,8},{10,11... | collective-permute-start | bytes 393224 | tf_op jit(solution)/shard_map/ppermute | solution.py:768
  119.1 6.0 %collective-permute-start.23 = (f32[8,128]{1,0:T(8,128)S(1)}, f32[8,128]{1,0:T(8,128)S(1)}, u32[]{:S(2)}, u32[]{:S(2)}) collective-permute-start(f32[8,128]{1,0:T(8,128)S(1)} %get-tuple-element.148), channel_id=1, source_target_pairs={{0,24},{8,16},{16,8},{24,0},{32,56},{40,48},{48,40},{56,32},{64,88... | collective-permute-start | bytes 12296 | tf_op jit(solution)/shard_map/ppermute | solution.py:763
  128.7 7.0 %collective-permute-start.24 = (f32[8,32,128]{2,1,0:T(8,128)S(1)}, f32[8,32,128]{2,1,0:T(8,128)S(1)}, u32[]{:S(2)}, u32[]{:S(2)}) collective-permute-start(f32[8,32,128]{2,1,0:T(8,128)S(1)} %get-tuple-element.150.refs_1_), channel_id=1, source_target_pairs={{0,2},{1,3},{2,0},{3,1},{4,6},{5,7},{6,4},{7,5},{8,10},{9,11},{10,... | collective-permute-start | bytes 393224 | tf_op jit(solution)/shard_map/ppermute | solution.py:768
  136.3 5.4 %collective-permute-start.28 = (f32[8,32,128]{2,1,0:T(8,128)S(1)}, f32[8,32,128]{2,1,0:T(8,128)S(1)}, u32[]{:S(2)}, u32[]{:S(2)}) collective-permute-start(f32[8,32,128]{2,1,0:T(8,128)S(1)} %get-tuple-element.156.refs_1_), channel_id=1, source_target_pairs={{0,4},{1,5},{2,6},{3,7},{4,0},{5,1},{6,2},{7,3},{8,12},{9,13},{10,... | collective-permute-start | bytes 393224 | tf_op jit(solution)/shard_map/ppermute | solution.py:768
  144.5 6.5 %collective-permute-start.31 = (f32[8,128]{1,0:T(8,128)S(1)}, f32[8,128]{1,0:T(8,128)S(1)}, u32[]{:S(2)}, u32[]{:S(2)}) collective-permute-start(f32[8,128]{1,0:T(8,128)S(1)} %add.112.refs_8_), channel_id=1, source_target_pairs={{0,1},{1,0},{2,3},{3,2},{4,5},{5,4},{6,7},{7,6},{8,9},{9,8},{10,11... | collective-permute-start | bytes 12296 | tf_op jit(solution)/shard_map/ppermute | solution.py:768
  156.5 13.2 %collective-permute-start.32 = (f32[25,8,128]{2,1,0:T(8,128)S(1)}, f32[25,8,128]{2,1,0:T(8,128)S(1)}, u32[]{:S(2)}, u32[]{:S(2)}) collective-permute-start(f32[25,8,128]{2,1,0:T(8,128)S(1)} %get-tuple-element.170), channel_id=1, source_target_pairs={{0,8},{8,0},{16,24},{24,16},{32,40},{40,32},{48,56},{56,48},{64,72... | collective-permute-start | bytes 307208 | tf_op jit(solution)/shard_map/ppermute | solution.py:868
  156.6 13.1 %collective-permute-start.33 = (f32[25,8,128]{2,1,0:T(8,128)S(1)}, f32[25,8,128]{2,1,0:T(8,128)S(1)}, u32[]{:S(2)}, u32[]{:S(2)}) collective-permute-start(f32[25,8,128]{2,1,0:T(8,128)S(1)} %get-tuple-element.171), channel_id=1, source_target_pairs={{8,16},{16,8},{24,32},{32,24},{40,48},{48,40},{56,64},{64,56},{72,... | collective-permute-start | bytes 307208 | tf_op jit(solution)/shard_map/ppermute | solution.py:869
  173.2 9.4 %collective-permute-start.34 = (f32[8,32,128]{2,1,0:T(8,128)S(1)}, f32[8,32,128]{2,1,0:T(8,128)S(1)}, u32[]{:S(2)}, u32[]{:S(2)}) collective-permute-start(f32[8,32,128]{2,1,0:T(8,128)S(1)} %get-tuple-element.175.refs_1_.refs_5_), channel_id=1, source_target_pairs={{0,1},{1,0},{2,3},{3,2},{4,5},{5,4},{6,7},{7,6},{8,9},{9,8},{10,11... | collective-permute-start | bytes 393224 | tf_op jit(solution)/shard_map/ppermute | solution.py:768
  173.6 6.0 %collective-permute-start.37 = (f32[8,128]{1,0:T(8,128)S(1)}, f32[8,128]{1,0:T(8,128)S(1)}, u32[]{:S(2)}, u32[]{:S(2)}) collective-permute-start(f32[8,128]{1,0:T(8,128)S(1)} %get-tuple-element.176), channel_id=1, source_target_pairs={{0,24},{8,16},{16,8},{24,0},{32,56},{40,48},{48,40},{56,32},{64,88... | collective-permute-start | bytes 12296 | tf_op jit(solution)/shard_map/ppermute | solution.py:763
  183.2 8.3 %collective-permute-start.38 = (f32[8,32,128]{2,1,0:T(8,128)S(1)}, f32[8,32,128]{2,1,0:T(8,128)S(1)}, u32[]{:S(2)}, u32[]{:S(2)}) collective-permute-start(f32[8,32,128]{2,1,0:T(8,128)S(1)} %get-tuple-element.178.refs_1_), channel_id=1, source_target_pairs={{0,2},{1,3},{2,0},{3,1},{4,6},{5,7},{6,4},{7,5},{8,10},{9,11},{10,... | collective-permute-start | bytes 393224 | tf_op jit(solution)/shard_map/ppermute | solution.py:768
  192.1 6.5 %collective-permute-start.42 = (f32[8,32,128]{2,1,0:T(8,128)S(1)}, f32[8,32,128]{2,1,0:T(8,128)S(1)}, u32[]{:S(2)}, u32[]{:S(2)}) collective-permute-start(f32[8,32,128]{2,1,0:T(8,128)S(1)} %get-tuple-element.184.refs_1_), channel_id=1, source_target_pairs={{0,4},{1,5},{2,6},{3,7},{4,0},{5,1},{6,2},{7,3},{8,12},{9,13},{10,... | collective-permute-start | bytes 393224 | tf_op jit(solution)/shard_map/ppermute | solution.py:768
  201.3 6.6 %collective-permute-start.45 = (f32[8,128]{1,0:T(8,128)S(1)}, f32[8,128]{1,0:T(8,128)S(1)}, u32[]{:S(2)}, u32[]{:S(2)}) collective-permute-start(f32[8,128]{1,0:T(8,128)S(1)} %add.120.refs_8_), channel_id=1, source_target_pairs={{0,1},{1,0},{2,3},{3,2},{4,5},{5,4},{6,7},{7,6},{8,9},{9,8},{10,11... | collective-permute-start | bytes 12296 | tf_op jit(solution)/shard_map/ppermute | solution.py:768
  (53 other events, 180.8 us)

commit v4 on v3

--- a/solution.py
+++ b/solution.py
@@ -102,17 +102,21 @@
     corners[...] = jnp.zeros(corners.shape, F32)
 
     def step(turn, unused):
-        which = plan[tile * PLAN + (10 if far else 2) + turn]
+        entry = plan[tile * PLAN + (10 if far else 2) + turn]
+        which = jnp.bitwise_and(entry, 15)
         column = pl.multiple_of((which - first_tile) * LANES, LANES)
         values = [table[member, :, pl.ds(column, LANES)] for member in range(LEVELS + 8)]
-        for side in range(4):
-            source = jnp.broadcast_to(ints[side : side + 1, :], (8, LANES))
-            lane = jnp.bitwise_and(source, LANES - 1)
-            hit = lax.shift_right_logical(source, 7) == which
-            for place in range(LEVELS):
-                edges[side, place] = jnp.where(
-                    hit, lane_take(values[place], lane), edges[side, place]
-                )
+        @pl.when(entry >= 16)
+        def sides():
+            for side in range(4):
+                source = jnp.broadcast_to(ints[side : side + 1, :], (8, LANES))
+                lane = jnp.bitwise_and(source, LANES - 1)
+                hit = lax.shift_right_logical(source, 7) == which
+                for place in range(LEVELS):
+                    edges[side, place] = jnp.where(
+                        hit, lane_take(values[place], lane), edges[side, place]
+                    )
+
         for corner in range(4):
             sums = [corners[corner, place] for place in range(8)]
             for other in range(3):
@@ -737,13 +741,15 @@
 def gather_plan(ints):
     holder = (ints[:16] // LANES).reshape(16, 8, LANES)
     tiles = jnp.arange(11, dtype=jnp.int32)
-    used = jnp.any(holder[:, :, None, :] == tiles[None, None, :, None], axis=(0, 3))
+    by_item = jnp.any(holder[:, :, None, :] == tiles[None, None, :, None], axis=3)
+    used = jnp.any(by_item, axis=0)
+    entry = tiles[None] + 16 * jnp.any(by_item[:4], axis=0).astype(jnp.int32)
     far = tiles >= 8
     same = far[:, None] == far[None, :]
     earlier = used[:, None, :] & (same & (tiles[None, :] < tiles[:, None]))[None]
     place = jnp.sum(earlier.astype(jnp.int32), axis=2) + jnp.where(far, 10, 2)[None]
     columns = jnp.arange(PLAN, dtype=jnp.int32)
-    listed = (place[:, :, None] == columns) * tiles[None, :, None]
+    listed = (place[:, :, None] == columns) * entry[:, :, None]
     counted = columns[None, :] == jnp.where(far, 1, 0)[:, None]
     values = jnp.where(used[:, :, None], listed + counted[None].astype(jnp.int32), 0)
     return jnp.sum(values, axis=1).astype(jnp.int32).reshape(-1)

time: 235 us -> 238 us (1.013); the launches traced: 231 us -> 237 us
  starting transfers between devices: 78.5 us -> 82.8 us
  waiting for transfers between devices: 41.5 us -> 37.5 us
  other arithmetic: 3.24 us -> 6.19 us
    ppermute x18, starting transfers between devices: 31.7 us -> 36.3 us  [parts_along(): parts.append(lax.ppermute(value, 'elem', pairs))]
    ppermute x18, waiting for transfers between devices: 17.8 us -> 13.9 us  [parts_along(): parts.append(lax.ppermute(value, 'elem', pairs))]
    reduce_or x1 -> x2, other arithmetic: 0.3 us -> 3.34 us  [the longest x1 3.32 us: gather_plan(): used = jnp.any(by_item, axis=0)]
    unnamed x63 -> x66, local copies, waits for them, and re-layouts: 11.9 us -> 11.5 us
  transfers between devices with their start and end apart: 46 -> 46, of which waited for: 22 -> 25; matrix products, arithmetic and copies ran while one was open for 2% -> 4% of each run, Pallas kernels for 18% -> 18%
where the time goes in v4:
time: 238 us; the launch traced here: 237 us
  starting transfers between devices  82.8 us (35%)
  Pallas kernels  79.9 us (34%)
  waiting for transfers between devices  37.5 us (16%)
  blocking collectives  15.3 us (6%)
  local copies, waits for them, and re-layouts  13.6 us (6%)
  other arithmetic  6.19 us (3%)
    pallas_call x13, Pallas kernels, call(): pl.pallas_call(kernel, grid=(GROUPS,), in_specs=in_specs, out_specs=out_s...  72.7 us
    ppermute x21, starting transfers between devices, swapped(): lax.ppermute(value, 'lev', [(i, i ^ distance) for i in range(GROUPS)])  38.8 us
    ppermute x18, starting transfers between devices, parts_along(): parts.append(lax.ppermute(value, 'elem', pairs))  36.3 us
    ppermute x21, waiting for transfers between devices, swapped(): lax.ppermute(value, 'lev', [(i, i ^ distance) for i in range(GROUPS)])  23.6 us
    all_to_all x1, blocking collectives, body(): lax.all_to_all(product, ('elem', 'lev'), split_axis=0, concat_axis=0, til...  15.3 us
    ppermute x18, waiting for transfers between devices, parts_along(): parts.append(lax.ppermute(value, 'elem', pairs))  13.9 us
    unnamed x66, local copies, waits for them, and re-layouts  11.5 us
    pallas_call x12, Pallas kernels, join(): pl.pallas_call(lambda *refs: joined(first, last, *refs), in_specs=[scalar...  7.17 us
  transfers between devices with their start and end apart: 46, of which 25 were waited for; matrix products, arithmetic and copies ran while one was open for 4% of the time, Pallas kernels for 18%

profile of v4, /device:TPU:1, one launch (start us, length us, event | category | flops | bytes accessed | tf_op | source)
XLA Modules:
  0.0 237.1 jit_solution(12434561264835939141)
XLA Ops:
  0.6 4.5 %collective-permute-start = (s32[1]{0:T(128)}, s32[1]{0:T(128)}, u32[]{:S(2)}, u32[]{:S(2)}) collective-permute-start(s32[1]{0:T(128)} %param.20), channel_id=1, source_target_pairs={{0,8},{8,16},{16,24},{24,32},{32,40},{40,48},{48,56},{56,64},{64,7... | collective-permute-start | bytes 20 | tf_op jit(solution)/shard_map/ppermute | solution.py:838
  14.1 3.3 %fusion.1 = (pred[8,11]{0,1:T(8,128)(4,1)S(1)}, pred[16,8,11]{1,2,0:T(8,128)(4,1)S(1)}) fusion(s32[16,8,128]{2,1,0:T(8,128)S(1)} %bitcast.20), kind=kLoop, calls=%fused_computation.2 | loop fusion | flops 539176 | bytes 67032 | tf_op jit(solution)/shard_map/reduce_or | solution.py:745
  21.7 3.4 %collective-permute-done.2.refs_2_ = f32[8,40,128]{2,1,0:T(8,128)S(1)} collective-permute-done((f32[8,40,128]{2,1,0:T(8,128)S(1)}, f32[8,40,128]{2,1,0:T(8,128)S(1)}, u32[]{:S(2)}, u32[]{:S(2)}) %collective-permute-start.2) | collective-permute-done | bytes 163872 | tf_op jit(solution)/shard_map/ppermute | solution.py:774
  25.7 3.4 %collective-permute-start.3 = (f32[8,40,128]{2,1,0:T(8,128)S(1)}, f32[8,40,128]{2,1,0:T(8,128)S(1)}, u32[]{:S(2)}, u32[]{:S(2)}) collective-permute-start(f32[8,40,128]{2,1,0:T(8,128)S(1)} %get-tuple-element.108.refs_1_), channel_id=1, source_target_pairs={{0,4},{1,5},{2,6},{3,7},{4,0},{5,1},{6,2},{7,3},{8,12},{9,13},{10,... | collective-permute-start | bytes 491528 | tf_op jit(solution)/shard_map/ppermute | solution.py:774
  29.2 3.7 %collective-permute-done.3.refs_2_ = f32[8,40,128]{2,1,0:T(8,128)S(1)} collective-permute-done((f32[8,40,128]{2,1,0:T(8,128)S(1)}, f32[8,40,128]{2,1,0:T(8,128)S(1)}, u32[]{:S(2)}, u32[]{:S(2)}) %collective-permute-start.3) | collective-permute-done | bytes 163872 | tf_op jit(solution)/shard_map/ppermute | solution.py:774
  34.1 3.3 %solve_first.1 = (f32[16,16,1024]{2,1,0:T(8,128)S(1)}, f32[8,128]{1,0:T(8,128)S(1)}, f32[25,8,128]{2,1,0:T(8,128)}, f32[25,8,128]{2,1,0:T(8,128)}) custom-call(s32[2]{0:T(128)S(1)} %pad_add_fusion.refs_0_, f32[2,8,8,1024]{3,2,1,0:T(8,128)S(1)} %copy-done.1, f32[16,1024]{1,0:T(8,128)S(1)} %copy-done.3, f32[16,16,1024]{2,1,0:T(8,128)S(1)} %get-tuple-element.102.refs_3_, ...), custom_call_target="tpu_custom_call" | custom-call | flops 4194304 | bytes 6291456 | tf_op jit(solution)/shard_map/solve_first/pallas_call | solution.py:668
  46.5 12.8 %operate.3.refs_2_ = f32[16,16,1024]{2,1,0:T(8,128)S(1)} custom-call(f32[16]{0:T(128)S(1)} %copy-done.24, s32[104]{0:T(128)S(1)} %copy-done.12, f32[16,16,1024]{2,1,0:T(8,128)S(1)} %get-tuple-element.112.field.refs_3_.refs_5_, s32[48,1024]{1,0:T(8,128)S(1)} %get-tuple-element.103.ints.refs_4_, f32[16,1024]{1,0:T(8,128)S(1)} %copy-done.19, ...), custom_call_target="tpu_custom_call" | custom-call | flops 1073741824 | bytes 6291456 | tf_op jit(solution)/shard_map/operate/pallas_call | solution.py:668
  64.2 8.1 %collective-permute-start.9 = (f32[8,128]{1,0:T(8,128)S(1)}, f32[8,128]{1,0:T(8,128)S(1)}, u32[]{:S(2)}, u32[]{:S(2)}) collective-permute-start(f32[8,128]{1,0:T(8,128)S(1)} %get-tuple-element.119), channel_id=1, source_target_pairs={{0,24},{8,16},{16,8},{24,0},{32,56},{40,48},{48,40},{56,32},{64,88... | collective-permute-start | bytes 12296 | tf_op jit(solution)/shard_map/ppermute | solution.py:769
  83.1 3.4 %collective-permute-start.14 = (f32[8,32,128]{2,1,0:T(8,128)S(1)}, f32[8,32,128]{2,1,0:T(8,128)S(1)}, u32[]{:S(2)}, u32[]{:S(2)}) collective-permute-start(f32[8,32,128]{2,1,0:T(8,128)S(1)} %get-tuple-element.129.refs_1_), channel_id=1, source_target_pairs={{0,4},{1,5},{2,6},{3,7},{4,0},{5,1},{6,2},{7,3},{8,12},{9,13},{10,... | collective-permute-start | bytes 393224 | tf_op jit(solution)/shard_map/ppermute | solution.py:774
  86.6 3.9 %collective-permute-done.15 = f32[8,128]{1,0:T(8,128)S(1)} collective-permute-done((f32[8,128]{1,0:T(8,128)S(1)}, f32[8,128]{1,0:T(8,128)S(1)}, u32[]{:S(2)}, u32[]{:S(2)}) %collective-permute-start.15) | collective-permute-done | bytes 4128 | tf_op jit(solution)/shard_map/ppermute | solution.py:774
  92.9 5.5 %collective-permute-start.17 = (f32[8,128]{1,0:T(8,128)S(1)}, f32[8,128]{1,0:T(8,128)S(1)}, u32[]{:S(2)}, u32[]{:S(2)}) collective-permute-start(f32[8,128]{1,0:T(8,128)S(1)} %add.118.refs_8_), channel_id=1, source_target_pairs={{0,1},{1,0},{2,3},{3,2},{4,5},{5,4},{6,7},{7,6},{8,9},{9,8},{10,11... | collective-permute-start | bytes 12296 | tf_op jit(solution)/shard_map/ppermute | solution.py:774
  99.8 4.8 %solve.2 = (f32[16,16,1024]{2,1,0:T(8,128)S(1)}, f32[16,16,1024]{2,1,0:T(8,128)S(1)}, f32[16,16,1024]{2,1,0:T(8,128)S(1)}, f32[8,128]{1,0:T(8,128)S(1)}, f32[16,...) custom-call(s32[2]{0:T(128)S(1)} %pad_add_fusion.refs_0_, ...), custom_call_target="tpu_custom_call" | custom-call | flops 4194304 | bytes 6291456 | tf_op jit(solution)/shard_map/solve/pallas_call | solution.py:668
  105.5 12.9 %operate.4.refs_2_ = f32[16,16,1024]{2,1,0:T(8,128)S(1)} custom-call(f32[16]{0:T(128)S(1)} %copy-done.24, s32[104]{0:T(128)S(1)} %copy-done.12, f32[16,16,1024]{2,1,0:T(8,128)S(1)} %get-tuple-element.140.field.refs_3_.refs_5_, s32[48,1024]{1,0:T(8,128)S(1)} %get-tuple-element.103.ints.refs_4_, f32[16,1024]{1,0:T(8,128)S(1)} %copy-done.20, ...), custom_call_target="tpu_custom_call" | custom-call | flops 1073741824 | bytes 6291456 | tf_op jit(solution)/shard_map/operate/pallas_call | solution.py:668
  118.5 3.5 %image.2 = (f32[16,16,1024]{2,1,0:T(8,128)S(1)}, f32[8,32,128]{2,1,0:T(8,128)S(1)}, f32[8,128]{1,0:T(8,128)S(1)}) custom-call(s32[2]{0:T(128)S(1)} %pad_add_fusion.refs_0_, s32[104]{0:T(128)S(1)} %copy-done.12, f32[16,16,1024]{2,1,0:T(8,128)S(1)} %operate.4.refs_2_, f32[16,16,1024]{2,1,0:T(8,128)S(1)} %get-tuple-element.140.field.refs_3_.refs_5_, ...), custom_call_target="tpu_custom_call" | custom-call | flops 4194304 | bytes 6291456 | tf_op jit(solution)/shard_map/image/pallas_call | solution.py:668
  122.2 8.4 %collective-permute-start.23 = (f32[8,128]{1,0:T(8,128)S(1)}, f32[8,128]{1,0:T(8,128)S(1)}, u32[]{:S(2)}, u32[]{:S(2)}) collective-permute-start(f32[8,128]{1,0:T(8,128)S(1)} %get-tuple-element.148), channel_id=1, source_target_pairs={{0,24},{8,16},{16,8},{24,0},{32,56},{40,48},{48,40},{56,32},{64,88... | collective-permute-start | bytes 12296 | tf_op jit(solution)/shard_map/ppermute | solution.py:769
  148.6 5.2 %collective-permute-start.31 = (f32[8,128]{1,0:T(8,128)S(1)}, f32[8,128]{1,0:T(8,128)S(1)}, u32[]{:S(2)}, u32[]{:S(2)}) collective-permute-start(f32[8,128]{1,0:T(8,128)S(1)} %add.126.refs_8_), channel_id=1, source_target_pairs={{0,1},{1,0},{2,3},{3,2},{4,5},{5,4},{6,7},{7,6},{8,9},{9,8},{10,11... | collective-permute-start | bytes 12296 | tf_op jit(solution)/shard_map/ppermute | solution.py:774
  154.7 5.5 %solve.3 = (f32[16,16,1024]{2,1,0:T(8,128)S(1)}, f32[16,16,1024]{2,1,0:T(8,128)S(1)}, f32[16,16,1024]{2,1,0:T(8,128)S(1)}, f32[8,128]{1,0:T(8,128)S(1)}, f32[16,...) custom-call(s32[2]{0:T(128)S(1)} %pad_add_fusion.refs_0_, ...), custom_call_target="tpu_custom_call" | custom-call | flops 4194304 | bytes 6291456 | tf_op jit(solution)/shard_map/solve/pallas_call | solution.py:668
  161.0 12.9 %operate.5.refs_2_ = f32[16,16,1024]{2,1,0:T(8,128)S(1)} custom-call(f32[16]{0:T(128)S(1)} %copy-done.24, s32[104]{0:T(128)S(1)} %copy-done.12, f32[16,16,1024]{2,1,0:T(8,128)S(1)} %get-tuple-element.168.field.refs_3_.refs_5_, s32[48,1024]{1,0:T(8,128)S(1)} %get-tuple-element.103.ints.refs_4_, f32[16,1024]{1,0:T(8,128)S(1)} %copy-done.20, ...), custom_call_target="tpu_custom_call" | custom-call | flops 1073741824 | bytes 6291456 | tf_op jit(solution)/shard_map/operate/pallas_call | solution.py:668
  173.9 3.5 %image.3 = (f32[16,16,1024]{2,1,0:T(8,128)S(1)}, f32[8,32,128]{2,1,0:T(8,128)S(1)}, f32[8,128]{1,0:T(8,128)S(1)}) custom-call(s32[2]{0:T(128)S(1)} %pad_add_fusion.refs_0_, s32[104]{0:T(128)S(1)} %copy-done.12, f32[16,16,1024]{2,1,0:T(8,128)S(1)} %operate.5.refs_2_, f32[16,16,1024]{2,1,0:T(8,128)S(1)} %get-tuple-element.168.field.refs_3_.refs_5_, ...), custom_call_target="tpu_custom_call" | custom-call | flops 4194304 | bytes 6291456 | tf_op jit(solution)/shard_map/image/pallas_call | solution.py:668
  178.1 8.2 %collective-permute-start.37 = (f32[8,128]{1,0:T(8,128)S(1)}, f32[8,128]{1,0:T(8,128)S(1)}, u32[]{:S(2)}, u32[]{:S(2)}) collective-permute-start(f32[8,128]{1,0:T(8,128)S(1)} %get-tuple-element.176), channel_id=1, source_target_pairs={{0,24},{8,16},{16,8},{24,0},{32,56},{40,48},{48,40},{56,32},{64,88... | collective-permute-start | bytes 12296 | tf_op jit(solution)/shard_map/ppermute | solution.py:769
  206.6 5.5 %collective-permute-start.45 = (f32[8,128]{1,0:T(8,128)S(1)}, f32[8,128]{1,0:T(8,128)S(1)}, u32[]{:S(2)}, u32[]{:S(2)}) collective-permute-start(f32[8,128]{1,0:T(8,128)S(1)} %add.134.refs_8_), channel_id=1, source_target_pairs={{0,1},{1,0},{2,3},{3,2},{4,5},{5,4},{6,7},{7,6},{8,9},{9,8},{10,11... | collective-permute-start | bytes 12296 | tf_op jit(solution)/shard_map/ppermute | solution.py:774
  212.8 5.4 %solve_last.1 = (f32[16,16,1024]{2,1,0:T(8,128)}, f32[16,16,1024]{2,1,0:T(8,128)}, f32[16,16,1024]{2,1,0:T(8,128)S(1)}, f32[8,128]{1,0:T(8,128)S(1)}, f32[16,16,...) custom-call(s32[2]{0:T(128)S(1)} %pad_add_fusion.refs_0_, f32[2,8,8,1024]{3,2,1,0:T(8,128)S(1)} %copy-done.1, ...), custom_call_target="tpu_custom_call" | custom-call | flops 4194304 | bytes 6291456 | tf_op jit(solution)/shard_map/solve_last/pallas_call | solution.py:668
  218.2 15.3 %all_to_all.11 = f32[128,1,128]{2,1,0:T(1,128)S(1)} all-to-all(f32[128,1,128]{2,1,0:T(1,128)S(1)} %bitcast.17), channel_id=1, replica_groups=mesh['elem'=16,'lev'=8] {'elem','lev'}, dimensions={0} | all-to-all | bytes 131072 | tf_op jit(solution)/shard_map/all_to_all | solution.py:967
  233.6 3.6 %finish.1 = f32[16,16,1024]{2,1,0:T(8,128)} custom-call(f32[128,128]{1,0:T(8,128)S(1)} %bitcast.16, f32[8,128]{1,0:T(8,128)S(1)} %get-tuple-element.198.scalars_in, f32[16,16,1024]{2,1,0:T(8,128)S(1)} %get-tuple-element.199.smoothed, f32[16,16,1024]{2,1,0:T(8,128)S(1)} %get-tuple-element.200.direction_in), custom_call_target="tpu_custom_call" | custom-call | flops 1048576 | bytes 6291456 | tf_op jit(solution)/shard_map/finish/pallas_call | solution.py:668
  (195 shorter events, 85.4 us)
Async XLA Ops:
  0.6 11.2 %collective-permute-start = (s32[1]{0:T(128)}, s32[1]{0:T(128)}, u32[]{:S(2)}, u32[]{:S(2)}) collective-permute-start(s32[1]{0:T(128)} %param.20), channel_id=1, source_target_pairs={{0,8},{8,16},{16,24},{24,32},{32,40},{40,48},{48,56},{56,64},{64,7... | collective-permute-start | bytes 20 | tf_op jit(solution)/shard_map/ppermute | solution.py:838
  9.7 7.9 %collective-permute-start.1 = (f32[8,40,128]{2,1,0:T(8,128)S(1)}, f32[8,40,128]{2,1,0:T(8,128)S(1)}, u32[]{:S(2)}, u32[]{:S(2)}) collective-permute-start(f32[8,40,128]{2,1,0:T(8,128)S(1)} %get-tuple-element.104.refs_1_.refs_5_), channel_id=1, source_target_pairs={{0,1},{1,0},{2,3},{3,2},{4,5},{5,4},{6,7},{7,6},{8,9},{9,8},{10,11... | collective-permute-start | bytes 491528 | tf_op jit(solution)/shard_map/ppermute | solution.py:774
  18.9 6.1 %collective-permute-start.2 = (f32[8,40,128]{2,1,0:T(8,128)S(1)}, f32[8,40,128]{2,1,0:T(8,128)S(1)}, u32[]{:S(2)}, u32[]{:S(2)}) collective-permute-start(f32[8,40,128]{2,1,0:T(8,128)S(1)} %get-tuple-element.105.refs_1_), channel_id=1, source_target_pairs={{0,2},{1,3},{2,0},{3,1},{4,6},{5,7},{6,4},{7,5},{8,10},{9,11},{10,... | collective-permute-start | bytes 491528 | tf_op jit(solution)/shard_map/ppermute | solution.py:774
  25.7 7.1 %collective-permute-start.3 = (f32[8,40,128]{2,1,0:T(8,128)S(1)}, f32[8,40,128]{2,1,0:T(8,128)S(1)}, u32[]{:S(2)}, u32[]{:S(2)}) collective-permute-start(f32[8,40,128]{2,1,0:T(8,128)S(1)} %get-tuple-element.108.refs_1_), channel_id=1, source_target_pairs={{0,4},{1,5},{2,6},{3,7},{4,0},{5,1},{6,2},{7,3},{8,12},{9,13},{10,... | collective-permute-start | bytes 491528 | tf_op jit(solution)/shard_map/ppermute | solution.py:774
  38.1 21.3 %collective-permute-start.4 = (f32[25,8,128]{2,1,0:T(8,128)}, f32[25,8,128]{2,1,0:T(8,128)S(1)}, u32[]{:S(2)}, u32[]{:S(2)}) collective-permute-start(f32[25,8,128]{2,1,0:T(8,128)} %get-tuple-element.115), channel_id=1, source_target_pairs={{0,8},{8,0},{16,24},{24,16},{32,40},{40,32},{48,56},{56,48},{64,72... | collective-permute-start | bytes 307208 | tf_op jit(solution)/shard_map/ppermute | solution.py:874
  38.9 20.5 %collective-permute-start.5 = (f32[25,8,128]{2,1,0:T(8,128)}, f32[25,8,128]{2,1,0:T(8,128)S(1)}, u32[]{:S(2)}, u32[]{:S(2)}) collective-permute-start(f32[25,8,128]{2,1,0:T(8,128)} %get-tuple-element.116), channel_id=1, source_target_pairs={{8,16},{16,8},{24,32},{32,24},{40,48},{48,40},{56,64},{64,56},{72,... | collective-permute-start | bytes 307208 | tf_op jit(solution)/shard_map/ppermute | solution.py:875
  62.4 13.8 %collective-permute-start.6 = (f32[8,32,128]{2,1,0:T(8,128)S(1)}, f32[8,32,128]{2,1,0:T(8,128)S(1)}, u32[]{:S(2)}, u32[]{:S(2)}) collective-permute-start(f32[8,32,128]{2,1,0:T(8,128)S(1)} %get-tuple-element.118.refs_1_.refs_5_), channel_id=1, source_target_pairs={{0,1},{1,0},{2,3},{3,2},{4,5},{5,4},{6,7},{7,6},{8,9},{9,8},{10,11... | collective-permute-start | bytes 393224 | tf_op jit(solution)/shard_map/ppermute | solution.py:774
  64.2 9.1 %collective-permute-start.9 = (f32[8,128]{1,0:T(8,128)S(1)}, f32[8,128]{1,0:T(8,128)S(1)}, u32[]{:S(2)}, u32[]{:S(2)}) collective-permute-start(f32[8,128]{1,0:T(8,128)S(1)} %get-tuple-element.119), channel_id=1, source_target_pairs={{0,24},{8,16},{16,8},{24,0},{32,56},{40,48},{48,40},{56,32},{64,88... | collective-permute-start | bytes 12296 | tf_op jit(solution)/shard_map/ppermute | solution.py:769
  76.8 5.7 %collective-permute-start.10 = (f32[8,32,128]{2,1,0:T(8,128)S(1)}, f32[8,32,128]{2,1,0:T(8,128)S(1)}, u32[]{:S(2)}, u32[]{:S(2)}) collective-permute-start(f32[8,32,128]{2,1,0:T(8,128)S(1)} %get-tuple-element.122.refs_1_), channel_id=1, source_target_pairs={{0,2},{1,3},{2,0},{3,1},{4,6},{5,7},{6,4},{7,5},{8,10},{9,11},{10,... | collective-permute-start | bytes 393224 | tf_op jit(solution)/shard_map/ppermute | solution.py:774
  83.1 7.3 %collective-permute-start.14 = (f32[8,32,128]{2,1,0:T(8,128)S(1)}, f32[8,32,128]{2,1,0:T(8,128)S(1)}, u32[]{:S(2)}, u32[]{:S(2)}) collective-permute-start(f32[8,32,128]{2,1,0:T(8,128)S(1)} %get-tuple-element.129.refs_1_), channel_id=1, source_target_pairs={{0,4},{1,5},{2,6},{3,7},{4,0},{5,1},{6,2},{7,3},{8,12},{9,13},{10,... | collective-permute-start | bytes 393224 | tf_op jit(solution)/shard_map/ppermute | solution.py:774
  92.9 6.8 %collective-permute-start.17 = (f32[8,128]{1,0:T(8,128)S(1)}, f32[8,128]{1,0:T(8,128)S(1)}, u32[]{:S(2)}, u32[]{:S(2)}) collective-permute-start(f32[8,128]{1,0:T(8,128)S(1)} %add.118.refs_8_), channel_id=1, source_target_pairs={{0,1},{1,0},{2,3},{3,2},{4,5},{5,4},{6,7},{7,6},{8,9},{9,8},{10,11... | collective-permute-start | bytes 12296 | tf_op jit(solution)/shard_map/ppermute | solution.py:774
  104.6 13.9 %collective-permute-start.18 = (f32[25,8,128]{2,1,0:T(8,128)S(1)}, f32[25,8,128]{2,1,0:T(8,128)S(1)}, u32[]{:S(2)}, u32[]{:S(2)}) collective-permute-start(f32[25,8,128]{2,1,0:T(8,128)S(1)} %get-tuple-element.142), channel_id=1, source_target_pairs={{0,8},{8,0},{16,24},{24,16},{32,40},{40,32},{48,56},{56,48},{64,72... | collective-permute-start | bytes 307208 | tf_op jit(solution)/shard_map/ppermute | solution.py:874
  104.8 13.6 %collective-permute-start.19 = (f32[25,8,128]{2,1,0:T(8,128)S(1)}, f32[25,8,128]{2,1,0:T(8,128)S(1)}, u32[]{:S(2)}, u32[]{:S(2)}) collective-permute-start(f32[25,8,128]{2,1,0:T(8,128)S(1)} %get-tuple-element.143), channel_id=1, source_target_pairs={{8,16},{16,8},{24,32},{32,24},{40,48},{48,40},{56,64},{64,56},{72,... | collective-permute-start | bytes 307208 | tf_op jit(solution)/shard_map/ppermute | solution.py:875
  122.0 12.6 %collective-permute-start.20 = (f32[8,32,128]{2,1,0:T(8,128)S(1)}, f32[8,32,128]{2,1,0:T(8,128)S(1)}, u32[]{:S(2)}, u32[]{:S(2)}) collective-permute-start(f32[8,32,128]{2,1,0:T(8,128)S(1)} %get-tuple-element.147.refs_1_.refs_5_), channel_id=1, source_target_pairs={{0,1},{1,0},{2,3},{3,2},{4,5},{5,4},{6,7},{7,6},{8,9},{9,8},{10,11... | collective-permute-start | bytes 393224 | tf_op jit(solution)/shard_map/ppermute | solution.py:774
  122.2 9.4 %collective-permute-start.23 = (f32[8,128]{1,0:T(8,128)S(1)}, f32[8,128]{1,0:T(8,128)S(1)}, u32[]{:S(2)}, u32[]{:S(2)}) collective-permute-start(f32[8,128]{1,0:T(8,128)S(1)} %get-tuple-element.148), channel_id=1, source_target_pairs={{0,24},{8,16},{16,8},{24,0},{32,56},{40,48},{48,40},{56,32},{64,88... | collective-permute-start | bytes 12296 | tf_op jit(solution)/shard_map/ppermute | solution.py:769
  140.3 5.4 %collective-permute-start.28 = (f32[8,32,128]{2,1,0:T(8,128)S(1)}, f32[8,32,128]{2,1,0:T(8,128)S(1)}, u32[]{:S(2)}, u32[]{:S(2)}) collective-permute-start(f32[8,32,128]{2,1,0:T(8,128)S(1)} %get-tuple-element.156.refs_1_), channel_id=1, source_target_pairs={{0,4},{1,5},{2,6},{3,7},{4,0},{5,1},{6,2},{7,3},{8,12},{9,13},{10,... | collective-permute-start | bytes 393224 | tf_op jit(solution)/shard_map/ppermute | solution.py:774
  148.6 6.1 %collective-permute-start.31 = (f32[8,128]{1,0:T(8,128)S(1)}, f32[8,128]{1,0:T(8,128)S(1)}, u32[]{:S(2)}, u32[]{:S(2)}) collective-permute-start(f32[8,128]{1,0:T(8,128)S(1)} %add.126.refs_8_), channel_id=1, source_target_pairs={{0,1},{1,0},{2,3},{3,2},{4,5},{5,4},{6,7},{7,6},{8,9},{9,8},{10,11... | collective-permute-start | bytes 12296 | tf_op jit(solution)/shard_map/ppermute | solution.py:774
  160.2 13.7 %collective-permute-start.32 = (f32[25,8,128]{2,1,0:T(8,128)S(1)}, f32[25,8,128]{2,1,0:T(8,128)S(1)}, u32[]{:S(2)}, u32[]{:S(2)}) collective-permute-start(f32[25,8,128]{2,1,0:T(8,128)S(1)} %get-tuple-element.170), channel_id=1, source_target_pairs={{0,8},{8,0},{16,24},{24,16},{32,40},{40,32},{48,56},{56,48},{64,72... | collective-permute-start | bytes 307208 | tf_op jit(solution)/shard_map/ppermute | solution.py:874
  160.4 13.6 %collective-permute-start.33 = (f32[25,8,128]{2,1,0:T(8,128)S(1)}, f32[25,8,128]{2,1,0:T(8,128)S(1)}, u32[]{:S(2)}, u32[]{:S(2)}) collective-permute-start(f32[25,8,128]{2,1,0:T(8,128)S(1)} %get-tuple-element.171), channel_id=1, source_target_pairs={{8,16},{16,8},{24,32},{32,24},{40,48},{48,40},{56,64},{64,56},{72,... | collective-permute-start | bytes 307208 | tf_op jit(solution)/shard_map/ppermute | solution.py:875
  177.4 12.9 %collective-permute-start.34 = (f32[8,32,128]{2,1,0:T(8,128)S(1)}, f32[8,32,128]{2,1,0:T(8,128)S(1)}, u32[]{:S(2)}, u32[]{:S(2)}) collective-permute-start(f32[8,32,128]{2,1,0:T(8,128)S(1)} %get-tuple-element.175.refs_1_.refs_5_), channel_id=1, source_target_pairs={{0,1},{1,0},{2,3},{3,2},{4,5},{5,4},{6,7},{7,6},{8,9},{9,8},{10,11... | collective-permute-start | bytes 393224 | tf_op jit(solution)/shard_map/ppermute | solution.py:774
  178.1 9.2 %collective-permute-start.37 = (f32[8,128]{1,0:T(8,128)S(1)}, f32[8,128]{1,0:T(8,128)S(1)}, u32[]{:S(2)}, u32[]{:S(2)}) collective-permute-start(f32[8,128]{1,0:T(8,128)S(1)} %get-tuple-element.176), channel_id=1, source_target_pairs={{0,24},{8,16},{16,8},{24,0},{32,56},{40,48},{48,40},{56,32},{64,88... | collective-permute-start | bytes 12296 | tf_op jit(solution)/shard_map/ppermute | solution.py:769
  190.9 6.0 %collective-permute-start.38 = (f32[8,32,128]{2,1,0:T(8,128)S(1)}, f32[8,32,128]{2,1,0:T(8,128)S(1)}, u32[]{:S(2)}, u32[]{:S(2)}) collective-permute-start(f32[8,32,128]{2,1,0:T(8,128)S(1)} %get-tuple-element.178.refs_1_), channel_id=1, source_target_pairs={{0,2},{1,3},{2,0},{3,1},{4,6},{5,7},{6,4},{7,5},{8,10},{9,11},{10,... | collective-permute-start | bytes 393224 | tf_op jit(solution)/shard_map/ppermute | solution.py:774
  197.5 6.3 %collective-permute-start.42 = (f32[8,32,128]{2,1,0:T(8,128)S(1)}, f32[8,32,128]{2,1,0:T(8,128)S(1)}, u32[]{:S(2)}, u32[]{:S(2)}) collective-permute-start(f32[8,32,128]{2,1,0:T(8,128)S(1)} %get-tuple-element.184.refs_1_), channel_id=1, source_target_pairs={{0,4},{1,5},{2,6},{3,7},{4,0},{5,1},{6,2},{7,3},{8,12},{9,13},{10,... | collective-permute-start | bytes 393224 | tf_op jit(solution)/shard_map/ppermute | solution.py:774
  206.6 6.3 %collective-permute-start.45 = (f32[8,128]{1,0:T(8,128)S(1)}, f32[8,128]{1,0:T(8,128)S(1)}, u32[]{:S(2)}, u32[]{:S(2)}) collective-permute-start(f32[8,128]{1,0:T(8,128)S(1)} %add.134.refs_8_), channel_id=1, source_target_pairs={{0,1},{1,0},{2,3},{3,2},{4,5},{5,4},{6,7},{7,6},{8,9},{9,8},{10,11... | collective-permute-start | bytes 12296 | tf_op jit(solution)/shard_map/ppermute | solution.py:774
  (54 other events, 199.4 us)

commit v5 on v3

--- a/solution.py
+++ b/solution.py
@@ -134,16 +134,14 @@
     lax.fori_loop(0, plan[tile * PLAN + (1 if far else 0)], step, 0)
     low_index = ints[16:24, :]
     high_index = ints[24:32, :]
-    next_row = jnp.bitwise_and(rows, 4) + jnp.bitwise_and(rows + 1, 3)
-    next_pair = jnp.bitwise_and(rows, 4) + jnp.bitwise_and(rows + 2, 3)
-    other_half = jnp.bitwise_xor(rows, 4)
     for pair in range(LEVELS // 2):
         sums = []
         for corner in range(4):
             total = corners[corner, pair]
-            total = total + row_take(total, next_row)
-            total = total + row_take(total, next_pair)
-            sums.append((total, row_take(total, other_half)))
+            near, far_by = (7, 6) if corner in (0, 3) else (1, 2)
+            total = total + pltpu.roll(total, near, 0)
+            total = total + pltpu.roll(total, far_by, 0)
+            sums.append((total, pltpu.roll(total, 4, 0)))
         for half in range(2):
             level = 2 * pair + half
             low = jnp.where(

time: 235 us -> 233 us (level); the launches traced: 231 us -> 233 us
  starting transfers between devices: 78.5 us -> 92.6 us
  Pallas kernels: 78.4 us -> 70.6 us
  waiting for transfers between devices: 41.5 us -> 37 us
    ppermute x18, starting transfers between devices: 31.7 us -> 45.1 us  [parts_along(): parts.append(lax.ppermute(value, 'elem', pairs))]
    pallas_call x13, Pallas kernels: 71.2 us -> 63.4 us  [call(): pl.pallas_call(kernel, grid=(GROUPS,), in_specs=in_specs, out_specs=out_s...]
    ppermute x18, waiting for transfers between devices: 17.8 us -> 13.1 us  [parts_along(): parts.append(lax.ppermute(value, 'elem', pairs))]
  transfers between devices with their start and end apart: 46 -> 46, of which waited for: 22 -> 24; matrix products, arithmetic and copies ran while one was open for 2% -> 2% of each run, Pallas kernels for 18% -> 14%
where the time goes in v5:
time: 233 us
  starting transfers between devices  92.6 us (40%)
  Pallas kernels  70.6 us (30%)
  waiting for transfers between devices  37 us (16%)
  blocking collectives  14 us (6%)
  local copies, waits for them, and re-layouts  13.4 us (6%)
  other arithmetic  3.24 us (1%)
    pallas_call x13, Pallas kernels, call(): pl.pallas_call(kernel, grid=(GROUPS,), in_specs=in_specs, out_specs=out_s...  63.4 us
    ppermute x18, starting transfers between devices, parts_along(): parts.append(lax.ppermute(value, 'elem', pairs))  45.1 us
    ppermute x21, starting transfers between devices, swapped(): lax.ppermute(value, 'lev', [(i, i ^ distance) for i in range(GROUPS)])  40 us
    ppermute x21, waiting for transfers between devices, swapped(): lax.ppermute(value, 'lev', [(i, i ^ distance) for i in range(GROUPS)])  23.9 us
    all_to_all x1, blocking collectives, body(): lax.all_to_all(product, ('elem', 'lev'), split_axis=0, concat_axis=0, til...  14 us
    ppermute x18, waiting for transfers between devices, parts_along(): parts.append(lax.ppermute(value, 'elem', pairs))  13.1 us
    unnamed x63, local copies, waits for them, and re-layouts  11.9 us
    pallas_call x12, Pallas kernels, join(): pl.pallas_call(lambda *refs: joined(first, last, *refs), in_specs=[scalar...  7.17 us
  transfers between devices with their start and end apart: 46, of which 24 were waited for; matrix products, arithmetic and copies ran while one was open for 2% of the time, Pallas kernels for 14%

profile of v5, /device:TPU:1, one launch (start us, length us, event | category | flops | bytes accessed | tf_op | source)
XLA Modules:
  0.0 232.7 jit_solution(10896786236130600780)
XLA Ops:
  0.6 4.6 %collective-permute-start = (s32[1]{0:T(128)}, s32[1]{0:T(128)}, u32[]{:S(2)}, u32[]{:S(2)}) collective-permute-start(s32[1]{0:T(128)} %param.20), channel_id=1, source_target_pairs={{0,8},{8,16},{16,24},{24,32},{32,40},{40,48},{48,56},{56,64},{64,7... | collective-permute-start | bytes 20 | tf_op jit(solution)/shard_map/ppermute | solution.py:830
  18.6 3.2 %collective-permute-done.2.refs_2_ = f32[8,40,128]{2,1,0:T(8,128)S(1)} collective-permute-done((f32[8,40,128]{2,1,0:T(8,128)S(1)}, f32[8,40,128]{2,1,0:T(8,128)S(1)}, u32[]{:S(2)}, u32[]{:S(2)}) %collective-permute-start.2) | collective-permute-done | bytes 163872 | tf_op jit(solution)/shard_map/ppermute | solution.py:766
  22.5 3.4 %collective-permute-start.3 = (f32[8,40,128]{2,1,0:T(8,128)S(1)}, f32[8,40,128]{2,1,0:T(8,128)S(1)}, u32[]{:S(2)}, u32[]{:S(2)}) collective-permute-start(f32[8,40,128]{2,1,0:T(8,128)S(1)} %get-tuple-element.108.refs_1_), channel_id=1, source_target_pairs={{0,4},{1,5},{2,6},{3,7},{4,0},{5,1},{6,2},{7,3},{8,12},{9,13},{10,... | collective-permute-start | bytes 491528 | tf_op jit(solution)/shard_map/ppermute | solution.py:766
  25.9 3.7 %collective-permute-done.3.refs_2_ = f32[8,40,128]{2,1,0:T(8,128)S(1)} collective-permute-done((f32[8,40,128]{2,1,0:T(8,128)S(1)}, f32[8,40,128]{2,1,0:T(8,128)S(1)}, u32[]{:S(2)}, u32[]{:S(2)}) %collective-permute-start.3) | collective-permute-done | bytes 163872 | tf_op jit(solution)/shard_map/ppermute | solution.py:766
  30.8 3.3 %solve_first.1 = (f32[16,16,1024]{2,1,0:T(8,128)S(1)}, f32[8,128]{1,0:T(8,128)S(1)}, f32[25,8,128]{2,1,0:T(8,128)}, f32[25,8,128]{2,1,0:T(8,128)}) custom-call(s32[2]{0:T(128)S(1)} %pad_add_fusion.refs_0_, f32[2,8,8,1024]{3,2,1,0:T(8,128)S(1)} %copy-done.1, f32[16,1024]{1,0:T(8,128)S(1)} %copy-done.3, f32[16,16,1024]{2,1,0:T(8,128)S(1)} %get-tuple-element.102.refs_3_, ...), custom_call_target="tpu_custom_call" | custom-call | flops 4194304 | bytes 6291456 | tf_op jit(solution)/shard_map/solve_first/pallas_call | solution.py:662
  43.2 9.8 %operate.3.refs_2_ = f32[16,16,1024]{2,1,0:T(8,128)S(1)} custom-call(f32[16]{0:T(128)S(1)} %copy-done.24, s32[104]{0:T(128)S(1)} %copy-done.12, f32[16,16,1024]{2,1,0:T(8,128)S(1)} %get-tuple-element.112.field.refs_3_.refs_5_, s32[48,1024]{1,0:T(8,128)S(1)} %get-tuple-element.103.ints.refs_4_, f32[16,1024]{1,0:T(8,128)S(1)} %copy-done.19, ...), custom_call_target="tpu_custom_call" | custom-call | flops 1073741824 | bytes 6291456 | tf_op jit(solution)/shard_map/operate/pallas_call | solution.py:662
  57.8 10.5 %collective-permute-start.9 = (f32[8,128]{1,0:T(8,128)S(1)}, f32[8,128]{1,0:T(8,128)S(1)}, u32[]{:S(2)}, u32[]{:S(2)}) collective-permute-start(f32[8,128]{1,0:T(8,128)S(1)} %get-tuple-element.119), channel_id=1, source_target_pairs={{0,24},{8,16},{16,8},{24,0},{32,56},{40,48},{48,40},{56,32},{64,88... | collective-permute-start | bytes 12296 | tf_op jit(solution)/shard_map/ppermute | solution.py:761
  80.0 3.4 %collective-permute-start.14 = (f32[8,32,128]{2,1,0:T(8,128)S(1)}, f32[8,32,128]{2,1,0:T(8,128)S(1)}, u32[]{:S(2)}, u32[]{:S(2)}) collective-permute-start(f32[8,32,128]{2,1,0:T(8,128)S(1)} %get-tuple-element.129.refs_1_), channel_id=1, source_target_pairs={{0,4},{1,5},{2,6},{3,7},{4,0},{5,1},{6,2},{7,3},{8,12},{9,13},{10,... | collective-permute-start | bytes 393224 | tf_op jit(solution)/shard_map/ppermute | solution.py:766
  83.5 3.9 %collective-permute-done.15 = f32[8,128]{1,0:T(8,128)S(1)} collective-permute-done((f32[8,128]{1,0:T(8,128)S(1)}, f32[8,128]{1,0:T(8,128)S(1)}, u32[]{:S(2)}, u32[]{:S(2)}) %collective-permute-start.15) | collective-permute-done | bytes 4128 | tf_op jit(solution)/shard_map/ppermute | solution.py:766
  90.0 6.2 %collective-permute-start.17 = (f32[8,128]{1,0:T(8,128)S(1)}, f32[8,128]{1,0:T(8,128)S(1)}, u32[]{:S(2)}, u32[]{:S(2)}) collective-permute-start(f32[8,128]{1,0:T(8,128)S(1)} %add.104.refs_8_), channel_id=1, source_target_pairs={{0,1},{1,0},{2,3},{3,2},{4,5},{5,4},{6,7},{7,6},{8,9},{9,8},{10,11... | collective-permute-start | bytes 12296 | tf_op jit(solution)/shard_map/ppermute | solution.py:766
  97.5 4.8 %solve.2 = (f32[16,16,1024]{2,1,0:T(8,128)S(1)}, f32[16,16,1024]{2,1,0:T(8,128)S(1)}, f32[16,16,1024]{2,1,0:T(8,128)S(1)}, f32[8,128]{1,0:T(8,128)S(1)}, f32[16,...) custom-call(s32[2]{0:T(128)S(1)} %pad_add_fusion.refs_0_, ...), custom_call_target="tpu_custom_call" | custom-call | flops 4194304 | bytes 6291456 | tf_op jit(solution)/shard_map/solve/pallas_call | solution.py:662
  103.1 9.9 %operate.4.refs_2_ = f32[16,16,1024]{2,1,0:T(8,128)S(1)} custom-call(f32[16]{0:T(128)S(1)} %copy-done.24, s32[104]{0:T(128)S(1)} %copy-done.12, f32[16,16,1024]{2,1,0:T(8,128)S(1)} %get-tuple-element.140.field.refs_3_.refs_5_, s32[48,1024]{1,0:T(8,128)S(1)} %get-tuple-element.103.ints.refs_4_, f32[16,1024]{1,0:T(8,128)S(1)} %copy-done.20, ...), custom_call_target="tpu_custom_call" | custom-call | flops 1073741824 | bytes 6291456 | tf_op jit(solution)/shard_map/operate/pallas_call | solution.py:662
  113.0 3.4 %image.2 = (f32[16,16,1024]{2,1,0:T(8,128)S(1)}, f32[8,32,128]{2,1,0:T(8,128)S(1)}, f32[8,128]{1,0:T(8,128)S(1)}) custom-call(s32[2]{0:T(128)S(1)} %pad_add_fusion.refs_0_, s32[104]{0:T(128)S(1)} %copy-done.12, f32[16,16,1024]{2,1,0:T(8,128)S(1)} %operate.4.refs_2_, f32[16,16,1024]{2,1,0:T(8,128)S(1)} %get-tuple-element.140.field.refs_3_.refs_5_, ...), custom_call_target="tpu_custom_call" | custom-call | flops 4194304 | bytes 6291456 | tf_op jit(solution)/shard_map/image/pallas_call | solution.py:662
  116.5 9.5 %collective-permute-start.23 = (f32[8,128]{1,0:T(8,128)S(1)}, f32[8,128]{1,0:T(8,128)S(1)}, u32[]{:S(2)}, u32[]{:S(2)}) collective-permute-start(f32[8,128]{1,0:T(8,128)S(1)} %get-tuple-element.148), channel_id=1, source_target_pairs={{0,24},{8,16},{16,8},{24,0},{32,56},{40,48},{48,40},{56,32},{64,88... | collective-permute-start | bytes 12296 | tf_op jit(solution)/shard_map/ppermute | solution.py:761
  144.9 5.7 %collective-permute-start.31 = (f32[8,128]{1,0:T(8,128)S(1)}, f32[8,128]{1,0:T(8,128)S(1)}, u32[]{:S(2)}, u32[]{:S(2)}) collective-permute-start(f32[8,128]{1,0:T(8,128)S(1)} %add.112.refs_8_), channel_id=1, source_target_pairs={{0,1},{1,0},{2,3},{3,2},{4,5},{5,4},{6,7},{7,6},{8,9},{9,8},{10,11... | collective-permute-start | bytes 12296 | tf_op jit(solution)/shard_map/ppermute | solution.py:766
  151.4 5.5 %solve.3 = (f32[16,16,1024]{2,1,0:T(8,128)S(1)}, f32[16,16,1024]{2,1,0:T(8,128)S(1)}, f32[16,16,1024]{2,1,0:T(8,128)S(1)}, f32[8,128]{1,0:T(8,128)S(1)}, f32[16,...) custom-call(s32[2]{0:T(128)S(1)} %pad_add_fusion.refs_0_, ...), custom_call_target="tpu_custom_call" | custom-call | flops 4194304 | bytes 6291456 | tf_op jit(solution)/shard_map/solve/pallas_call | solution.py:662
  157.7 9.8 %operate.5.refs_2_ = f32[16,16,1024]{2,1,0:T(8,128)S(1)} custom-call(f32[16]{0:T(128)S(1)} %copy-done.24, s32[104]{0:T(128)S(1)} %copy-done.12, f32[16,16,1024]{2,1,0:T(8,128)S(1)} %get-tuple-element.168.field.refs_3_.refs_5_, s32[48,1024]{1,0:T(8,128)S(1)} %get-tuple-element.103.ints.refs_4_, f32[16,1024]{1,0:T(8,128)S(1)} %copy-done.20, ...), custom_call_target="tpu_custom_call" | custom-call | flops 1073741824 | bytes 6291456 | tf_op jit(solution)/shard_map/operate/pallas_call | solution.py:662
  167.5 3.4 %image.3 = (f32[16,16,1024]{2,1,0:T(8,128)S(1)}, f32[8,32,128]{2,1,0:T(8,128)S(1)}, f32[8,128]{1,0:T(8,128)S(1)}) custom-call(s32[2]{0:T(128)S(1)} %pad_add_fusion.refs_0_, s32[104]{0:T(128)S(1)} %copy-done.12, f32[16,16,1024]{2,1,0:T(8,128)S(1)} %operate.5.refs_2_, f32[16,16,1024]{2,1,0:T(8,128)S(1)} %get-tuple-element.168.field.refs_3_.refs_5_, ...), custom_call_target="tpu_custom_call" | custom-call | flops 4194304 | bytes 6291456 | tf_op jit(solution)/shard_map/image/pallas_call | solution.py:662
  171.4 10.5 %collective-permute-start.37 = (f32[8,128]{1,0:T(8,128)S(1)}, f32[8,128]{1,0:T(8,128)S(1)}, u32[]{:S(2)}, u32[]{:S(2)}) collective-permute-start(f32[8,128]{1,0:T(8,128)S(1)} %get-tuple-element.176), channel_id=1, source_target_pairs={{0,24},{8,16},{16,8},{24,0},{32,56},{40,48},{48,40},{56,32},{64,88... | collective-permute-start | bytes 12296 | tf_op jit(solution)/shard_map/ppermute | solution.py:761
  196.6 3.5 %collective-permute-done.43 = f32[8,128]{1,0:T(8,128)S(1)} collective-permute-done((f32[8,128]{1,0:T(8,128)S(1)}, f32[8,128]{1,0:T(8,128)S(1)}, u32[]{:S(2)}, u32[]{:S(2)}) %collective-permute-start.43) | collective-permute-done | bytes 4128 | tf_op jit(solution)/shard_map/ppermute | solution.py:766
  202.8 6.1 %collective-permute-start.45 = (f32[8,128]{1,0:T(8,128)S(1)}, f32[8,128]{1,0:T(8,128)S(1)}, u32[]{:S(2)}, u32[]{:S(2)}) collective-permute-start(f32[8,128]{1,0:T(8,128)S(1)} %add.120.refs_8_), channel_id=1, source_target_pairs={{0,1},{1,0},{2,3},{3,2},{4,5},{5,4},{6,7},{7,6},{8,9},{9,8},{10,11... | collective-permute-start | bytes 12296 | tf_op jit(solution)/shard_map/ppermute | solution.py:766
  209.7 5.4 %solve_last.1 = (f32[16,16,1024]{2,1,0:T(8,128)}, f32[16,16,1024]{2,1,0:T(8,128)}, f32[16,16,1024]{2,1,0:T(8,128)S(1)}, f32[8,128]{1,0:T(8,128)S(1)}, f32[16,16,...) custom-call(s32[2]{0:T(128)S(1)} %pad_add_fusion.refs_0_, f32[2,8,8,1024]{3,2,1,0:T(8,128)S(1)} %copy-done.1, ...), custom_call_target="tpu_custom_call" | custom-call | flops 4194304 | bytes 6291456 | tf_op jit(solution)/shard_map/solve_last/pallas_call | solution.py:662
  215.1 14.0 %all_to_all.11 = f32[128,1,128]{2,1,0:T(1,128)S(1)} all-to-all(f32[128,1,128]{2,1,0:T(1,128)S(1)} %bitcast.17), channel_id=1, replica_groups=mesh['elem'=16,'lev'=8] {'elem','lev'}, dimensions={0} | all-to-all | bytes 131072 | tf_op jit(solution)/shard_map/all_to_all | solution.py:959
  229.1 3.6 %finish.1 = f32[16,16,1024]{2,1,0:T(8,128)} custom-call(f32[128,128]{1,0:T(8,128)S(1)} %bitcast.16, f32[8,128]{1,0:T(8,128)S(1)} %get-tuple-element.198.scalars_in, f32[16,16,1024]{2,1,0:T(8,128)S(1)} %get-tuple-element.199.smoothed, f32[16,16,1024]{2,1,0:T(8,128)S(1)} %get-tuple-element.200.direction_in), custom_call_target="tpu_custom_call" | custom-call | flops 1048576 | bytes 6291456 | tf_op jit(solution)/shard_map/finish/pallas_call | solution.py:662
  (189 shorter events, 84.0 us)
Async XLA Ops:
  0.6 11.3 %collective-permute-start = (s32[1]{0:T(128)}, s32[1]{0:T(128)}, u32[]{:S(2)}, u32[]{:S(2)}) collective-permute-start(s32[1]{0:T(128)} %param.20), channel_id=1, source_target_pairs={{0,8},{8,16},{16,24},{24,32},{32,40},{40,48},{48,56},{56,64},{64,7... | collective-permute-start | bytes 20 | tf_op jit(solution)/shard_map/ppermute | solution.py:830
  9.7 4.6 %collective-permute-start.1 = (f32[8,40,128]{2,1,0:T(8,128)S(1)}, f32[8,40,128]{2,1,0:T(8,128)S(1)}, u32[]{:S(2)}, u32[]{:S(2)}) collective-permute-start(f32[8,40,128]{2,1,0:T(8,128)S(1)} %get-tuple-element.104.refs_1_.refs_5_), channel_id=1, source_target_pairs={{0,1},{1,0},{2,3},{3,2},{4,5},{5,4},{6,7},{7,6},{8,9},{9,8},{10,11... | collective-permute-start | bytes 491528 | tf_op jit(solution)/shard_map/ppermute | solution.py:766
  15.7 6.1 %collective-permute-start.2 = (f32[8,40,128]{2,1,0:T(8,128)S(1)}, f32[8,40,128]{2,1,0:T(8,128)S(1)}, u32[]{:S(2)}, u32[]{:S(2)}) collective-permute-start(f32[8,40,128]{2,1,0:T(8,128)S(1)} %get-tuple-element.105.refs_1_), channel_id=1, source_target_pairs={{0,2},{1,3},{2,0},{3,1},{4,6},{5,7},{6,4},{7,5},{8,10},{9,11},{10,... | collective-permute-start | bytes 491528 | tf_op jit(solution)/shard_map/ppermute | solution.py:766
  22.5 7.1 %collective-permute-start.3 = (f32[8,40,128]{2,1,0:T(8,128)S(1)}, f32[8,40,128]{2,1,0:T(8,128)S(1)}, u32[]{:S(2)}, u32[]{:S(2)}) collective-permute-start(f32[8,40,128]{2,1,0:T(8,128)S(1)} %get-tuple-element.108.refs_1_), channel_id=1, source_target_pairs={{0,4},{1,5},{2,6},{3,7},{4,0},{5,1},{6,2},{7,3},{8,12},{9,13},{10,... | collective-permute-start | bytes 491528 | tf_op jit(solution)/shard_map/ppermute | solution.py:766
  34.8 18.3 %collective-permute-start.4 = (f32[25,8,128]{2,1,0:T(8,128)}, f32[25,8,128]{2,1,0:T(8,128)S(1)}, u32[]{:S(2)}, u32[]{:S(2)}) collective-permute-start(f32[25,8,128]{2,1,0:T(8,128)} %get-tuple-element.115), channel_id=1, source_target_pairs={{0,8},{8,0},{16,24},{24,16},{32,40},{40,32},{48,56},{56,48},{64,72... | collective-permute-start | bytes 307208 | tf_op jit(solution)/shard_map/ppermute | solution.py:866
  35.5 17.5 %collective-permute-start.5 = (f32[25,8,128]{2,1,0:T(8,128)}, f32[25,8,128]{2,1,0:T(8,128)S(1)}, u32[]{:S(2)}, u32[]{:S(2)}) collective-permute-start(f32[25,8,128]{2,1,0:T(8,128)} %get-tuple-element.116), channel_id=1, source_target_pairs={{8,16},{16,8},{24,32},{32,24},{40,48},{48,40},{56,64},{64,56},{72,... | collective-permute-start | bytes 307208 | tf_op jit(solution)/shard_map/ppermute | solution.py:867
  56.0 16.5 %collective-permute-start.6 = (f32[8,32,128]{2,1,0:T(8,128)S(1)}, f32[8,32,128]{2,1,0:T(8,128)S(1)}, u32[]{:S(2)}, u32[]{:S(2)}) collective-permute-start(f32[8,32,128]{2,1,0:T(8,128)S(1)} %get-tuple-element.118.refs_1_.refs_5_), channel_id=1, source_target_pairs={{0,1},{1,0},{2,3},{3,2},{4,5},{5,4},{6,7},{7,6},{8,9},{9,8},{10,11... | collective-permute-start | bytes 393224 | tf_op jit(solution)/shard_map/ppermute | solution.py:766
  57.8 12.0 %collective-permute-start.9 = (f32[8,128]{1,0:T(8,128)S(1)}, f32[8,128]{1,0:T(8,128)S(1)}, u32[]{:S(2)}, u32[]{:S(2)}) collective-permute-start(f32[8,128]{1,0:T(8,128)S(1)} %get-tuple-element.119), channel_id=1, source_target_pairs={{0,24},{8,16},{16,8},{24,0},{32,56},{40,48},{48,40},{56,32},{64,88... | collective-permute-start | bytes 12296 | tf_op jit(solution)/shard_map/ppermute | solution.py:761
  73.1 6.3 %collective-permute-start.10 = (f32[8,32,128]{2,1,0:T(8,128)S(1)}, f32[8,32,128]{2,1,0:T(8,128)S(1)}, u32[]{:S(2)}, u32[]{:S(2)}) collective-permute-start(f32[8,32,128]{2,1,0:T(8,128)S(1)} %get-tuple-element.122.refs_1_), channel_id=1, source_target_pairs={{0,2},{1,3},{2,0},{3,1},{4,6},{5,7},{6,4},{7,5},{8,10},{9,11},{10,... | collective-permute-start | bytes 393224 | tf_op jit(solution)/shard_map/ppermute | solution.py:766
  80.0 7.3 %collective-permute-start.14 = (f32[8,32,128]{2,1,0:T(8,128)S(1)}, f32[8,32,128]{2,1,0:T(8,128)S(1)}, u32[]{:S(2)}, u32[]{:S(2)}) collective-permute-start(f32[8,32,128]{2,1,0:T(8,128)S(1)} %get-tuple-element.129.refs_1_), channel_id=1, source_target_pairs={{0,4},{1,5},{2,6},{3,7},{4,0},{5,1},{6,2},{7,3},{8,12},{9,13},{10,... | collective-permute-start | bytes 393224 | tf_op jit(solution)/shard_map/ppermute | solution.py:766
  90.0 7.4 %collective-permute-start.17 = (f32[8,128]{1,0:T(8,128)S(1)}, f32[8,128]{1,0:T(8,128)S(1)}, u32[]{:S(2)}, u32[]{:S(2)}) collective-permute-start(f32[8,128]{1,0:T(8,128)S(1)} %add.104.refs_8_), channel_id=1, source_target_pairs={{0,1},{1,0},{2,3},{3,2},{4,5},{5,4},{6,7},{7,6},{8,9},{9,8},{10,11... | collective-permute-start | bytes 12296 | tf_op jit(solution)/shard_map/ppermute | solution.py:766
  102.3 10.7 %collective-permute-start.18 = (f32[25,8,128]{2,1,0:T(8,128)S(1)}, f32[25,8,128]{2,1,0:T(8,128)S(1)}, u32[]{:S(2)}, u32[]{:S(2)}) collective-permute-start(f32[25,8,128]{2,1,0:T(8,128)S(1)} %get-tuple-element.142), channel_id=1, source_target_pairs={{0,8},{8,0},{16,24},{24,16},{32,40},{40,32},{48,56},{56,48},{64,72... | collective-permute-start | bytes 307208 | tf_op jit(solution)/shard_map/ppermute | solution.py:866
  102.4 10.6 %collective-permute-start.19 = (f32[25,8,128]{2,1,0:T(8,128)S(1)}, f32[25,8,128]{2,1,0:T(8,128)S(1)}, u32[]{:S(2)}, u32[]{:S(2)}) collective-permute-start(f32[25,8,128]{2,1,0:T(8,128)S(1)} %get-tuple-element.143), channel_id=1, source_target_pairs={{8,16},{16,8},{24,32},{32,24},{40,48},{48,40},{56,64},{64,56},{72,... | collective-permute-start | bytes 307208 | tf_op jit(solution)/shard_map/ppermute | solution.py:867
  116.4 14.5 %collective-permute-start.20 = (f32[8,32,128]{2,1,0:T(8,128)S(1)}, f32[8,32,128]{2,1,0:T(8,128)S(1)}, u32[]{:S(2)}, u32[]{:S(2)}) collective-permute-start(f32[8,32,128]{2,1,0:T(8,128)S(1)} %get-tuple-element.147.refs_1_.refs_5_), channel_id=1, source_target_pairs={{0,1},{1,0},{2,3},{3,2},{4,5},{5,4},{6,7},{7,6},{8,9},{9,8},{10,11... | collective-permute-start | bytes 393224 | tf_op jit(solution)/shard_map/ppermute | solution.py:766
  116.5 11.6 %collective-permute-start.23 = (f32[8,128]{1,0:T(8,128)S(1)}, f32[8,128]{1,0:T(8,128)S(1)}, u32[]{:S(2)}, u32[]{:S(2)}) collective-permute-start(f32[8,128]{1,0:T(8,128)S(1)} %get-tuple-element.148), channel_id=1, source_target_pairs={{0,24},{8,16},{16,8},{24,0},{32,56},{40,48},{48,40},{56,32},{64,88... | collective-permute-start | bytes 12296 | tf_op jit(solution)/shard_map/ppermute | solution.py:761
  136.6 5.5 %collective-permute-start.28 = (f32[8,32,128]{2,1,0:T(8,128)S(1)}, f32[8,32,128]{2,1,0:T(8,128)S(1)}, u32[]{:S(2)}, u32[]{:S(2)}) collective-permute-start(f32[8,32,128]{2,1,0:T(8,128)S(1)} %get-tuple-element.156.refs_1_), channel_id=1, source_target_pairs={{0,4},{1,5},{2,6},{3,7},{4,0},{5,1},{6,2},{7,3},{8,12},{9,13},{10,... | collective-permute-start | bytes 393224 | tf_op jit(solution)/shard_map/ppermute | solution.py:766
  144.9 6.5 %collective-permute-start.31 = (f32[8,128]{1,0:T(8,128)S(1)}, f32[8,128]{1,0:T(8,128)S(1)}, u32[]{:S(2)}, u32[]{:S(2)}) collective-permute-start(f32[8,128]{1,0:T(8,128)S(1)} %add.112.refs_8_), channel_id=1, source_target_pairs={{0,1},{1,0},{2,3},{3,2},{4,5},{5,4},{6,7},{7,6},{8,9},{9,8},{10,11... | collective-permute-start | bytes 12296 | tf_op jit(solution)/shard_map/ppermute | solution.py:766
  156.9 10.6 %collective-permute-start.32 = (f32[25,8,128]{2,1,0:T(8,128)S(1)}, f32[25,8,128]{2,1,0:T(8,128)S(1)}, u32[]{:S(2)}, u32[]{:S(2)}) collective-permute-start(f32[25,8,128]{2,1,0:T(8,128)S(1)} %get-tuple-element.170), channel_id=1, source_target_pairs={{0,8},{8,0},{16,24},{24,16},{32,40},{40,32},{48,56},{56,48},{64,72... | collective-permute-start | bytes 307208 | tf_op jit(solution)/shard_map/ppermute | solution.py:866
  157.0 10.5 %collective-permute-start.33 = (f32[25,8,128]{2,1,0:T(8,128)S(1)}, f32[25,8,128]{2,1,0:T(8,128)S(1)}, u32[]{:S(2)}, u32[]{:S(2)}) collective-permute-start(f32[25,8,128]{2,1,0:T(8,128)S(1)} %get-tuple-element.171), channel_id=1, source_target_pairs={{8,16},{16,8},{24,32},{32,24},{40,48},{48,40},{56,64},{64,56},{72,... | collective-permute-start | bytes 307208 | tf_op jit(solution)/shard_map/ppermute | solution.py:867
  170.9 14.9 %collective-permute-start.34 = (f32[8,32,128]{2,1,0:T(8,128)S(1)}, f32[8,32,128]{2,1,0:T(8,128)S(1)}, u32[]{:S(2)}, u32[]{:S(2)}) collective-permute-start(f32[8,32,128]{2,1,0:T(8,128)S(1)} %get-tuple-element.175.refs_1_.refs_5_), channel_id=1, source_target_pairs={{0,1},{1,0},{2,3},{3,2},{4,5},{5,4},{6,7},{7,6},{8,9},{9,8},{10,11... | collective-permute-start | bytes 393224 | tf_op jit(solution)/shard_map/ppermute | solution.py:766
  171.4 11.6 %collective-permute-start.37 = (f32[8,128]{1,0:T(8,128)S(1)}, f32[8,128]{1,0:T(8,128)S(1)}, u32[]{:S(2)}, u32[]{:S(2)}) collective-permute-start(f32[8,128]{1,0:T(8,128)S(1)} %get-tuple-element.176), channel_id=1, source_target_pairs={{0,24},{8,16},{16,8},{24,0},{32,56},{40,48},{48,40},{56,32},{64,88... | collective-permute-start | bytes 12296 | tf_op jit(solution)/shard_map/ppermute | solution.py:761
  186.5 6.5 %collective-permute-start.38 = (f32[8,32,128]{2,1,0:T(8,128)S(1)}, f32[8,32,128]{2,1,0:T(8,128)S(1)}, u32[]{:S(2)}, u32[]{:S(2)}) collective-permute-start(f32[8,32,128]{2,1,0:T(8,128)S(1)} %get-tuple-element.178.refs_1_), channel_id=1, source_target_pairs={{0,2},{1,3},{2,0},{3,1},{4,6},{5,7},{6,4},{7,5},{8,10},{9,11},{10,... | collective-permute-start | bytes 393224 | tf_op jit(solution)/shard_map/ppermute | solution.py:766
  193.5 6.5 %collective-permute-start.42 = (f32[8,32,128]{2,1,0:T(8,128)S(1)}, f32[8,32,128]{2,1,0:T(8,128)S(1)}, u32[]{:S(2)}, u32[]{:S(2)}) collective-permute-start(f32[8,32,128]{2,1,0:T(8,128)S(1)} %get-tuple-element.184.refs_1_), channel_id=1, source_target_pairs={{0,4},{1,5},{2,6},{3,7},{4,0},{5,1},{6,2},{7,3},{8,12},{9,13},{10,... | collective-permute-start | bytes 393224 | tf_op jit(solution)/shard_map/ppermute | solution.py:766
  202.8 6.9 %collective-permute-start.45 = (f32[8,128]{1,0:T(8,128)S(1)}, f32[8,128]{1,0:T(8,128)S(1)}, u32[]{:S(2)}, u32[]{:S(2)}) collective-permute-start(f32[8,128]{1,0:T(8,128)S(1)} %add.120.refs_8_), channel_id=1, source_target_pairs={{0,1},{1,0},{2,3},{3,2},{4,5},{5,4},{6,7},{7,6},{8,9},{9,8},{10,11... | collective-permute-start | bytes 12296 | tf_op jit(solution)/shard_map/ppermute | solution.py:766
  (53 other events, 176.3 us)
